TPU v7x, 32 devices: a whole 2x2x4 slice. The times are simulated.
32 devices in a mesh: section: 4 (over y, x), dp: 8 (over z, core).
Axes of the slice: x: 2, y: 2, z: 4, core: 2. Of those that a mesh axis runs over, the one named last changes fastest.
Arguments:
- inputs: bfloat16 [2, 640, 4096], P(None, 'dp'), may hold values from -36 to 36
- target: bfloat16 [2, 640, 4096], P(None, 'dp'), may hold values from -8 to 8
- blocks: bfloat16 [4, 64, 8, 4096], P('section', 'dp'), may hold values from -0.25 to 0.25
- columns: int32 [4, 64, 8], P('section', 'dp'), may hold values from 0 to 63, as said below
- counts: int32 [4, 64], P('section', 'dp'), may hold values from 4 to 8, as said below
Outputs:
- block_grads: bfloat16 [4, 64, 8, 4096], P('section', 'dp')
Inputs may be any that keep to these rules, and one draw needn't show every extreme that they name: Each block row lists 8 different block columns; only its first counts entries are kept blocks, the rest are padding. `counts`: every layer has a block row with exactly 8 kept blocks.
All inputs are finite; a program needn't handle non-finite values.
Results may differ from a plain program's by a relative error of at most 0.015.
Values may be sent and summed in bfloat16 or wider, within the bound.
No kernel may reach another device: no remote copies, remote signals or barrier semaphores. Data moves between devices by JAX's collectives and lax.ppermute only.
A program may use at most 128 MiB of HBM per device.

v0:
```python
import functools

import jax
import jax.numpy as jnp
from jax import lax
from jax.experimental import pallas as pl
from jax.experimental.pallas import tpu as pltpu
from jax.sharding import PartitionSpec as P

BLK = 64
LANES = 128
EPSILON = 1e-05
VMEM_LIMIT = 54 * 1024 * 1024
STEP_ROWS = 8

TAIL = 16

IN_VMEM = pl.BlockSpec(memory_space=pltpu.VMEM)
IN_SMEM = pl.BlockSpec(memory_space=pltpu.SMEM)
IN_HBM = pl.BlockSpec(memory_space=pl.ANY)


def about(microseconds):
    return pl.CostEstimate(
        flops=int(microseconds * 1.1e9), bytes_accessed=1 << 20, transcendentals=0
    )


def step_units(units, rows):
    size = max(1, STEP_ROWS // rows)
    while units % size:
        size -= 1
    return size


def low_half(rows):
    return lax.broadcasted_iota(jnp.int32, (rows, LANES), 1) < BLK


def tile(pair):
    return pl.ds(pl.multiple_of(pair * LANES, LANES), LANES)


def over_pairs(feats, visit, carry):
    return lax.fori_loop(0, feats // LANES, visit, carry, unroll=4)


def inv_rms_of(ref):
    tokens, feats = ref.shape

    def visit(pair, total):
        values = ref[:, tile(pair)].astype(jnp.float32)
        return total + values * values

    total = over_pairs(feats, visit, jnp.zeros((tokens, LANES), jnp.float32))
    return lax.rsqrt(jnp.sum(total, axis=-1, keepdims=True) / feats + EPSILON)


def start_loads(pieces, held, arrived, roles):
    units = held.shape[1]
    for role in roles:
        for unit in range(units):
            pltpu.make_async_copy(
                pieces[2 * unit + role], held.at[role, unit], arrived.at[role, unit]
            ).start()


def start_loads_in_order(side, pieces, held, arrived, layers):
    for value in range(2):
        pl.when(side == value)(
            functools.partial(
                start_loads, pieces, held, arrived, [abs(layer - value) for layer in layers]
            )
        )


def wait_load(pieces, held, arrived, role, unit):
    pltpu.make_async_copy(pieces[0], held.at[role, unit], arrived.at[role, unit]).wait()


def forward_layer(role, wait, cols, bases, current, held, parts, sums, rows, slots):
    tokens, feats = current.shape
    units = held.shape[1]
    per_step = step_units(units, rows)
    low = low_half(tokens)
    inv_rms = inv_rms_of(current)

    def normalise(pair, carry):
        lanes = tile(pair)
        unit_rows = current[:, lanes].astype(jnp.float32) * inv_rms
        parts[2 * pair] = jnp.where(low, unit_rows, 0.0).astype(jnp.bfloat16)
        parts[2 * pair + 1] = jnp.where(low, 0.0, unit_rows).astype(jnp.bfloat16)
        sums[2 * pair] = jnp.zeros((tokens, LANES), jnp.float32)
        sums[2 * pair + 1] = jnp.zeros((tokens, LANES), jnp.float32)
        return carry

    over_pairs(feats, normalise, 0)

    def run_step(step, carry):
        for inner in range(per_step):
            wait(role, step * per_step + inner)
        items = [(inner, row) for inner in range(per_step) for row in range(0, rows, 2)]

        def product_of(index):
            inner, row = items[index]
            unit = step * per_step + inner
            place = bases[unit] + row
            left = jnp.concatenate([parts[place], parts[place + 1]], axis=0)
            right = held[role, unit, row * BLK : (row + 2) * BLK]
            return jnp.dot(left, right, preferred_element_type=jnp.float32)

        upcoming = product_of(0)
        for index, (inner, row) in enumerate(items):
            product = upcoming
            if index + 1 < len(items):
                upcoming = product_of(index + 1)
            for which in range(2):
                line = role * units + step * per_step + inner
                flat = (row + which) * slots
                for begin in range(0, slots, 4):
                    at = [cols[line, flat + slot] for slot in range(begin, min(begin + 4, slots))]
                    added = []
                    for offset in range(len(at)):
                        slot = begin + offset
                        lanes = slice((slot // 2) * LANES, (slot // 2 + 1) * LANES)
                        piece = product[which * tokens : (which + 1) * tokens, lanes]
                        piece = jnp.where(low, piece, 0.0) if slot % 2 == 0 else jnp.where(low, 0.0, piece)
                        added.append(sums[at[offset]] + piece)
                    for offset in range(len(at)):
                        sums[at[offset]] = added[offset]
        return carry

    lax.fori_loop(0, units // per_step, run_step, 0)

    def finish(pair, carry):
        lanes = tile(pair)
        first, second = sums[2 * pair], sums[2 * pair + 1]
        branch = jnp.where(low, first, second) + pltpu.roll(jnp.where(low, second, first), BLK, 1)
        current[:, lanes] = (current[:, lanes].astype(jnp.float32) + branch).astype(jnp.bfloat16)
        return carry

    over_pairs(feats, finish, 0)


def spread(source, lows, highs):
    tokens, feats = source.shape
    low = low_half(tokens)

    def visit(pair, carry):
        both = source[:, tile(pair)].astype(jnp.float32)
        moved = pltpu.roll(both, BLK, 1)
        lows[2 * pair] = jnp.where(low, both, 0.0).astype(jnp.bfloat16)
        highs[2 * pair] = jnp.where(low, 0.0, moved).astype(jnp.bfloat16)
        lows[2 * pair + 1] = jnp.where(low, moved, 0.0).astype(jnp.bfloat16)
        highs[2 * pair + 1] = jnp.where(low, 0.0, both).astype(jnp.bfloat16)
        return carry

    over_pairs(feats, visit, 0)


def pick_columns(lows, highs, cols, line, flat, slots):
    return jnp.concatenate(
        [
            lows[cols[line, flat + 2 * half]] + highs[cols[line, flat + 2 * half + 1]]
            for half in range(slots // 2)
        ],
        axis=1,
    )


def input_grad_layer(role, wait, cols, bases, hidden, cotangent, out, held, lows, highs, back, rows, slots):
    tokens, feats = cotangent.shape
    units = held.shape[1]
    per_step = step_units(units, rows)
    low = low_half(tokens)

    def run_step(step, carry):
        for inner in range(per_step):
            wait(role, step * per_step + inner)
        items = [(inner, row) for inner in range(per_step) for row in range(0, rows, 2)]

        def picked_at(index):
            inner, row = items[index]
            line = role * units + step * per_step + inner
            return jnp.concatenate(
                [
                    pick_columns(lows, highs, cols, line, (row + which) * slots, slots)
                    for which in range(2)
                ],
                axis=0,
            )

        upcoming = picked_at(0)
        for index, (inner, row) in enumerate(items):
            unit = step * per_step + inner
            picked = upcoming
            if index + 1 < len(items):
                upcoming = picked_at(index + 1)
            result = lax.dot_general(
                picked,
                held[role, unit, row * BLK : (row + 2) * BLK],
                (((1,), (1,)), ((), ())),
                preferred_element_type=jnp.float32,
            )
            place = (bases[unit] + row) // 2
            back[place] = jnp.where(low, result[:tokens], result[tokens:])
        return carry

    lax.fori_loop(0, units // per_step, run_step, 0)
    inv_rms = inv_rms_of(hidden)

    def correlate(pair, total):
        unit_rows = hidden[:, tile(pair)].astype(jnp.float32) * inv_rms
        return total + back[pair] * unit_rows

    total = over_pairs(feats, correlate, jnp.zeros((tokens, LANES), jnp.float32))
    mean = jnp.sum(total, axis=-1, keepdims=True) / feats

    def finish(pair, carry):
        lanes = tile(pair)
        unit_rows = hidden[:, lanes].astype(jnp.float32) * inv_rms
        centred = back[pair] - unit_rows * mean
        out[:, lanes] = (cotangent[:, lanes].astype(jnp.float32) + inv_rms * centred).astype(jnp.bfloat16)
        return carry

    over_pairs(feats, finish, 0)


def block_grad_layer(layer, role, cols, flipped, lows, highs, out, chosen, units, rows, slots):
    items = [(which, row) for which in range(len(chosen)) for row in range(rows)]

    def operands(index):
        which, row = items[index]
        picked = pick_columns(lows, highs, cols, role * units + chosen[which], row * slots, slots)
        return flipped[layer, which * rows + row], picked

    upcoming = operands(0)
    for index, (which, row) in enumerate(items):
        left, right = upcoming
        if index + 1 < len(items):
            upcoming = operands(index + 1)
        result = jnp.dot(left, right, preferred_element_type=jnp.float32)
        out[which][row * BLK : (row + 1) * BLK] = result.astype(jnp.bfloat16)


def choose(flag, first, second, target):
    @pl.when(flag == 1)
    def _():
        target[...] = first[...]

    @pl.when(flag != 1)
    def _():
        target[...] = second[...]


def forward_kernel(rows, slots, count, scale, cols, bases, flags, *rest):
    turning = scale is not None
    start, moved = rest[:2]
    rest = rest[2:]
    if turning:
        goal, rest = rest[0], rest[1:]
    straight, rest = rest[:count], rest[count:]
    if turning:
        stash, loss_grad, final, held, parts, sums, arrived, lows, highs, back = rest
    else:
        final, held, parts, sums, arrived = rest
    start_loads_in_order(flags[0], straight, held, arrived, (0, 1))
    choose(flags[1], start, moved, final)
    wait = functools.partial(wait_load, straight, held, arrived)

    def run_forward(layer, carry):
        if turning:
            stash[layer] = final[...]
        role = jnp.abs(layer - flags[0])
        forward_layer(role, wait, cols, bases, final, held, parts, sums, rows, slots)
        return carry

    lax.fori_loop(0, 2, run_forward, 0)
    if not turning:
        return
    tokens, feats = final.shape

    def residue(pair, carry):
        lanes = tile(pair)
        gap = final[:, lanes].astype(jnp.float32) - goal[:, lanes].astype(jnp.float32)
        loss_grad[:, lanes] = (gap * scale).astype(jnp.bfloat16)
        return carry

    over_pairs(feats, residue, 0)
    final[...] = loss_grad[...]
    def run_back(turn, carry):
        layer = 1 - turn
        role = jnp.abs(layer - flags[0])
        hidden = stash.at[layer]
        spread(final, lows, highs)
        input_grad_layer(
            role, nothing, cols, bases, hidden, final, final, held, lows, highs, back, rows, slots
        )
        return carry

    lax.fori_loop(0, 2, run_back, 0)


def nothing(*_):
    return None


def state_of(tokens, feats):
    return jax.ShapeDtypeStruct((tokens, feats), jnp.bfloat16)


def unit_scratch(pieces):
    units = len(pieces) // 2
    return [pltpu.VMEM((2, units) + pieces[0].shape, jnp.bfloat16), pltpu.SemaphoreType.DMA((2, units))]


def forward_pass(start, moved, goal, scale, straight, meta, rows, slots):
    tokens, feats = start.shape
    blocks = feats // BLK
    stack = jax.ShapeDtypeStruct((2, tokens, feats), jnp.bfloat16)
    held, arrived = unit_scratch(straight)
    scratch = [
        held,
        pltpu.VMEM((blocks, tokens, LANES), jnp.bfloat16),
        pltpu.VMEM((blocks, tokens, LANES), jnp.float32),
        arrived,
    ]
    outs = [state_of(tokens, feats)]
    ins = [start, moved]
    pieces = list(straight)
    if goal is not None:
        ins.append(goal)
        outs = [stack, state_of(tokens, feats)] + outs
        scratch += [
            pltpu.VMEM((blocks, tokens, LANES), jnp.bfloat16),
            pltpu.VMEM((blocks, tokens, LANES), jnp.bfloat16),
            pltpu.VMEM((blocks // 2, tokens, LANES), jnp.float32),
        ]
    return pl.pallas_call(
        functools.partial(forward_kernel, rows, slots, len(straight), None if goal is None else scale),
        in_specs=[IN_SMEM] * 3 + [IN_VMEM] * len(ins) + [IN_HBM] * len(pieces),
        out_specs=[IN_VMEM] * len(outs),
        out_shape=outs,
        scratch_shapes=scratch,
        compiler_params=pltpu.CompilerParams(vmem_limit_bytes=VMEM_LIMIT),
        cost_estimate=about(8 if goal is None else 14),
        name="forward_layers" if goal is None else "turning_layers",
    )(*meta, *ins, *pieces)


def backward_kernel(rows, slots, count, depth, cols, bases, flags, stash, loss_grad, moved, *rest):
    across, rest = rest[:count], rest[count:]
    outs, crossed, lows, highs, back, landed = rest
    if depth == 1:
        first, second = outs.at[1], outs.at[0]
    else:
        first = second = outs
    start_loads_in_order(flags[0], across, crossed, landed, (1,) if depth == 1 else (1, 0))
    choose(flags[2], loss_grad, moved, first)
    wait = functools.partial(wait_load, across, crossed, landed)

    def run_back(layer):
        spread(first, lows, highs)
        role = jnp.abs(layer - flags[0])
        input_grad_layer(
            role, wait, cols, bases, stash.at[layer], first, second, crossed, lows, highs, back, rows, slots
        )

    run_back(1)
    if depth == 2:
        run_back(0)


def backward_pass(stash, loss_grad, moved, across, meta, rows, slots, depth):
    _, tokens, feats = stash.shape
    blocks = feats // BLK
    crossed, landed = unit_scratch(across)
    if depth == 1:
        out = jax.ShapeDtypeStruct((2, tokens, feats), jnp.bfloat16)
    else:
        out = state_of(tokens, feats)
    return pl.pallas_call(
        functools.partial(backward_kernel, rows, slots, len(across), depth),
        in_specs=[IN_SMEM] * 3 + [IN_VMEM] * 3 + [IN_HBM] * len(across),
        out_specs=IN_VMEM,
        out_shape=out,
        scratch_shapes=[
            crossed,
            pltpu.VMEM((blocks, tokens, LANES), jnp.bfloat16),
            pltpu.VMEM((blocks, tokens, LANES), jnp.bfloat16),
            pltpu.VMEM((blocks // 2, tokens, LANES), jnp.float32),
            landed,
        ],
        compiler_params=pltpu.CompilerParams(vmem_limit_bytes=VMEM_LIMIT),
        cost_estimate=about(4 * depth),
        name="backward_layers",
    )(*meta, stash, loss_grad, moved, *across)


def join_tokens(sources, joined, arrived):
    copies = []
    begin = 0
    for index, source in enumerate(sources):
        span = pl.ds(begin, source.shape[1])
        copies.append(pltpu.make_async_copy(source, joined.at[:, span], arrived.at[index]))
        begin += source.shape[1]
    for copy in copies:
        copy.start()
    for copy in copies:
        copy.wait()


def flip_kernel(rows, chosen, bases, *refs):
    *sources, flipped, joined, arrived = refs
    join_tokens(sources, joined, arrived)

    def run(layer, carry):
        hidden = joined.at[layer]
        inv_rms = inv_rms_of(hidden)
        for unit in range(chosen):

            def visit(step, carry):
                lanes = tile(bases[unit] // 2 + step)
                turned = (hidden[:, lanes].astype(jnp.float32) * inv_rms).T.astype(jnp.bfloat16)
                flipped[layer, unit * rows + 2 * step] = turned[:BLK]
                flipped[layer, unit * rows + 2 * step + 1] = turned[BLK:]
                return carry

            lax.fori_loop(0, rows // 2, visit, 0, unroll=True)
        return carry

    lax.fori_loop(0, 2, run, 0)


def flip_pass(stashes, bases, rows, chosen):
    tokens = sum(stash.shape[1] for stash in stashes)
    feats = stashes[0].shape[2]
    return pl.pallas_call(
        functools.partial(flip_kernel, rows, chosen),
        in_specs=[IN_SMEM] + [IN_HBM] * len(stashes),
        out_specs=IN_VMEM,
        out_shape=jax.ShapeDtypeStruct((2, chosen * rows, BLK, tokens), jnp.bfloat16),
        scratch_shapes=[
            pltpu.VMEM((2, tokens, feats), jnp.bfloat16),
            pltpu.SemaphoreType.DMA((len(stashes),)),
        ],
        compiler_params=pltpu.CompilerParams(vmem_limit_bytes=VMEM_LIMIT),
        cost_estimate=about(4),
        name="flip_rows",
    )(bases, *stashes)


def block_grad_kernel(rows, slots, chosen, units, parts, cols, flags, turned, *rest):
    sources, rest = rest[:parts], rest[parts:]
    outs = rest[: 2 * len(chosen)]
    joined, flipped, lows, highs, arrived, fetched = rest[2 * len(chosen) :]
    fetches = [
        pltpu.make_async_copy(
            turned.at[:, pl.ds(unit * rows, rows)],
            flipped.at[:, pl.ds(which * rows, rows)],
            fetched.at[which],
        )
        for which, unit in enumerate(chosen)
    ]
    for fetch in fetches:
        fetch.start()
    join_tokens(sources, joined, arrived)
    for fetch in fetches:
        fetch.wait()
    for role in (1, 0):
        layer = jnp.abs(role - flags[0])
        spread(joined.at[layer], lows, highs)
        block_grad_layer(
            layer, role, cols, flipped, lows, highs, outs[role::2], chosen, units, rows, slots
        )


def block_grad_pass(turned, cotangents, meta, rows, slots, chosen):
    tokens = turned.shape[3]
    feats = cotangents[0].shape[2]
    blocks = feats // BLK
    cols, bases, flags = meta
    out = jax.ShapeDtypeStruct((rows * BLK, slots * BLK), jnp.bfloat16)
    return pl.pallas_call(
        functools.partial(
            block_grad_kernel, rows, slots, tuple(chosen), bases.shape[0], len(cotangents)
        ),
        in_specs=[IN_SMEM] * 2 + [IN_HBM] * (1 + len(cotangents)),
        out_specs=[IN_VMEM] * (2 * len(chosen)),
        out_shape=[out] * (2 * len(chosen)),
        scratch_shapes=[
            pltpu.VMEM((2, tokens, feats), jnp.bfloat16),
            pltpu.VMEM((2, len(chosen) * rows, BLK, tokens), jnp.bfloat16),
            pltpu.VMEM((blocks, tokens, LANES), jnp.bfloat16),
            pltpu.VMEM((blocks, tokens, LANES), jnp.bfloat16),
            pltpu.SemaphoreType.DMA((len(cotangents),)),
            pltpu.SemaphoreType.DMA((len(chosen),)),
        ],
        compiler_params=pltpu.CompilerParams(vmem_limit_bytes=VMEM_LIMIT),
        cost_estimate=about(4 + len(chosen)),
        name="block_grads",
    )(cols, flags, turned, *cotangents)


def list_kernel(rows, pieces_count, *refs):
    pieces, (listed, tails, arrived) = refs[:pieces_count], refs[pieces_count:]
    copies = [
        pltpu.make_async_copy(piece.at[pl.ds(rows * BLK, TAIL)], tails.at[i], arrived.at[i])
        for i, piece in enumerate(pieces)
    ]
    for copy in copies:
        copy.start()
    for i, copy in enumerate(copies):
        copy.wait()
        line = tails[i].astype(jnp.float32)[:1, : listed.shape[1]]
        listed[i : i + 1] = line.astype(jnp.int32)


def list_pass(pieces, rows, slots):
    count = len(pieces)
    lanes = -(-rows * slots // LANES) * LANES
    return pl.pallas_call(
        functools.partial(list_kernel, rows, count),
        in_specs=[IN_HBM] * count,
        out_specs=IN_VMEM,
        out_shape=jax.ShapeDtypeStruct((count, lanes), jnp.int32),
        scratch_shapes=[
            pltpu.VMEM((count, TAIL, slots * BLK), jnp.bfloat16),
            pltpu.SemaphoreType.DMA((count,)),
        ],
        compiler_params=pltpu.CompilerParams(vmem_limit_bytes=VMEM_LIMIT),
        cost_estimate=about(2),
        name="list_columns",
    )(*pieces)


def to_rows(blocks):
    rows, slots, _ = blocks.shape
    split = blocks.reshape(rows, slots, BLK, BLK)
    return split.transpose(0, 2, 1, 3).reshape(rows * BLK, slots * BLK)


def from_rows(matrix, slots):
    rows = matrix.shape[0] // BLK
    split = matrix.reshape(rows, BLK, slots, BLK)
    return split.transpose(0, 2, 1, 3).reshape(rows, slots, BLK * BLK)


def token_cuts(tokens):
    if tokens % 16 or tokens < 32:
        return [(0, tokens)]
    first = -(-tokens // 32) * 16
    return [(0, first), (first, tokens)]


def folded(count):
    return list(range(0, 1)) + list(range(1, count, 2)) + list(range(2, count, 2))[::-1]


def body(inputs, target, blocks, columns, counts):
    stage, stages = lax.axis_index("stage"), lax.axis_size("stage")
    side, sides = lax.axis_index("side"), lax.axis_size("side")
    dp_id, dp_count = lax.axis_index("dp"), lax.axis_size("dp")
    mb_count, tok_local, feats = inputs.shape
    rows, slots = columns.shape[1:]
    loss_scale = (mb_count * tok_local * dp_count) ** (-0.5)
    places = dp_count // 2
    place = dp_id // 2
    core = dp_id % 2
    share = mb_count * tok_local // sides

    around = folded(places)
    ranks = [around.index(spot) for spot in range(places)]
    rank = jnp.array(ranks, jnp.int32)[place]
    hops = [
        (2 * around[i] + half, 2 * around[(i + 1) % places] + half)
        for i in range(places)
        for half in range(2)
    ]

    def ring(array):
        return lax.ppermute(array, "dp", hops)

    def sibling(array):
        return lax.ppermute(array, "dp", [(i, i ^ 1) for i in range(dp_count)])

    def partner(array):
        return lax.ppermute(array, "side", [(i, sides - 1 - i) for i in range(sides)])

    live = jnp.arange(slots, dtype=jnp.int32)[None, :] < counts[0][:, None]
    kept = jnp.where(live[:, :, None], blocks[0], jnp.zeros_like(blocks[0]))
    listed = columns[0].reshape(1, rows * slots).astype(jnp.bfloat16)
    tail = jnp.pad(listed, ((0, TAIL - 1), (0, slots * BLK - rows * slots)))
    own = jnp.concatenate([to_rows(kept), tail], axis=0)

    owns, others, far_owns, far_others = [own], [], [], []
    for slot in range(places):
        moving = {"other": partner(owns[slot]), "far_own": sibling(owns[slot])}
        if slot + 1 < places:
            moving["own"] = ring(owns[slot])
        if slot:
            moving["far_other"] = sibling(others[slot - 1])
        moving = lax.optimization_barrier(moving)
        others.append(moving["other"])
        far_owns.append(moving["far_own"])
        if slot + 1 < places:
            owns.append(moving["own"])
        if slot:
            far_others.append(moving["far_other"])
    far_others.append(sibling(others[-1]))
    own_units, other_units = owns + far_owns, others + far_others
    pieces = [piece for pair in zip(own_units, other_units) for piece in pair]
    cols = list_pass(own_units + other_units, rows, slots)
    turns = jnp.array(around, jnp.int32)[(rank - jnp.arange(places)) % places]
    bases = jnp.concatenate([turns * 2 + core, turns * 2 + 1 - core]).astype(jnp.int32) * rows
    flags = jnp.stack([side, stage == 0, stage == stages - 1]).astype(jnp.int32)
    meta = (cols, bases, flags)

    def my_rows(array):
        flat = array.reshape(mb_count * tok_local, feats)
        return lax.dynamic_slice_in_dim(flat, side * share, share, 0)

    def hop(array, distance):
        route = [(i, i + distance) for i in range(stages) if 0 <= i + distance < stages]
        return lax.ppermute(array, "stage", route)

    cuts = token_cuts(share)
    ways = range(len(cuts))
    whole_start, whole_goal = my_rows(inputs), my_rows(target)
    start = [whole_start[begin:end] for begin, end in cuts]
    goal = [whole_goal[begin:end] for begin, end in cuts]
    moved = list(start)
    for step in range(stages - 1):
        final = [
            forward_pass(start[i], moved[i], None, None, pieces, meta, rows, slots)[0]
            for i in ways
        ]
        moved = [hop(final[i], 1) for i in ways]
    turned = [
        forward_pass(start[i], moved[i], goal[i], loss_scale, pieces, meta, rows, slots)
        for i in ways
    ]
    stashes, loss_grads, result = [list(column) for column in zip(*turned)]
    moved = loss_grads
    for step in range(stages - 1):
        if step:
            result = [
                backward_pass(stashes[i], loss_grads[i], moved[i], pieces, meta, rows, slots, 2)
                for i in ways
            ]
        moved = [hop(result[i], -1) for i in ways]
    flipped = flip_pass(stashes + [sibling(stash) for stash in stashes], bases, rows, places)
    cotangents = [
        backward_pass(stashes[i], loss_grads[i], moved[i], pieces, meta, rows, slots, 1) for i in ways
    ]

    order = list(range(1, places)) + [0]

    cotangents = cotangents + [sibling(part) for part in cotangents]
    kept, outgoing = block_grad_pass(flipped, cotangents, meta, rows, slots, order[:1])
    cotangents, tied = lax.optimization_barrier((cotangents, outgoing))
    late = block_grad_pass(flipped, cotangents, meta, rows, slots, order[1:])
    coming, late = lax.optimization_barrier((partner(tied), late))
    travelling = add_rounded(kept, coming)
    for index in range(places - 1):
        kept, outgoing = late[2 * index], late[2 * index + 1]
        passed, coming = lax.optimization_barrier((ring(travelling), partner(outgoing)))
        total = kept.astype(jnp.float32) + coming.astype(jnp.float32) + passed.astype(jnp.float32)
        travelling = total.astype(jnp.bfloat16)
    result = from_rows(travelling, slots)
    return jnp.where(live[:, :, None], result, jnp.zeros_like(result))[None]


def add_rounded(left, right):
    return (left.astype(jnp.float32) + right.astype(jnp.float32)).astype(jnp.bfloat16)


def solution(mesh):
    sections, width = mesh.devices.shape
    split = jax.sharding.Mesh(mesh.devices.reshape(sections // 2, 2, width), ("stage", "side", "dp"))
    section = ("stage", "side")
    return jax.shard_map(
        body,
        mesh=split,
        in_specs=(
            P(None, "dp", None),
            P(None, "dp", None),
            P(section, "dp", None, None),
            P(section, "dp", None),
            P(section, "dp"),
        ),
        out_specs=P(section, "dp", None, None),
        check_vma=False,
    )
```

profile of v0, /device:TPU:0, one launch (start us, length us, event | category | flops | bytes accessed | tf_op | source)
XLA Modules:
  0.0 234.5 jit_solution(4756594689548237348)
XLA Ops:
  0.9 2.1 squeeze.6
  6.8 2.6 %collective-permute-start.1 = (bf16[528,512]{1,0:T(8,128)(2,1)S(1)}, bf16[528,512]{1,0:T(8,128)(2,1)S(1)}, u32[]{:S(2)}, u32[]{:S(2)}) collective-permute-start(bf16[528,512]{1,0:T(8,128)(2,1)S(1)} %fusion.2.refs_0_.rest_2_.rest_3_.rest_0_), channel_id=1, source_target_pairs={{0,8},{8,0},{1,9},{9,1},{2,10},{10,2},{3,11},{11,3},{4,12},{12,4},... | collective-permute-start | bytes 1622024 | tf_op jit(solution)/shard_map/ppermute | solution.py:588
  9.3 1.6 collective-permute-start.2
  12.2 10.0 %collective-permute-done.1.refs_8_.rest_3_.rest_4_.rest_1_ = bf16[528,512]{1,0:T(8,128)(2,1)S(1)} collective-permute-done((bf16[528,512]{1,0:T(8,128)(2,1)S(1)}, bf16[528,512]{1,0:T(8,128)(2,1)S(1)}, u32[]{:S(2)}, u32[]{:S(2)}) %collective-permute-start.1) | collective-permute-done | bytes 540704 | tf_op jit(solution)/shard_map/ppermute | solution.py:588
  22.2 2.4 %collective-permute-done.2.refs_1_.rest_4_.rest_5_.rest_2_ = bf16[528,512]{1,0:T(8,128)(2,1)S(1)} collective-permute-done((bf16[528,512]{1,0:T(8,128)(2,1)S(1)}, bf16[528,512]{1,0:T(8,128)(2,1)S(1)}, u32[]{:S(2)}, u32[]{:S(2)}) %collective-permute-start.2) | collective-permute-done | bytes 540704 | tf_op jit(solution)/shard_map/ppermute | solution.py:582
  28.0 11.4 %collective-permute-done.5.refs_9_.rest_5_.rest_6_.rest_3_ = bf16[528,512]{1,0:T(8,128)(2,1)} collective-permute-done((bf16[528,512]{1,0:T(8,128)(2,1)S(1)}, bf16[528,512]{1,0:T(8,128)(2,1)}, u32[]{:S(2)}, u32[]{:S(2)}) %collective-permute-start.5) | collective-permute-done | bytes 540704 | tf_op jit(solution)/shard_map/ppermute | solution.py:588
  40.5 1.5 collective-permute-start.9
  42.7 1.7 constant_dynamic-slice_fusion.2.rest_2_
  45.0 10.5 %collective-permute-done.9.refs_10_.rest_7_.rest_8_.rest_5_ = bf16[528,512]{1,0:T(8,128)(2,1)} collective-permute-done((bf16[528,512]{1,0:T(8,128)(2,1)}, bf16[528,512]{1,0:T(8,128)(2,1)}, u32[]{:S(2)}, u32[]{:S(2)}) %collective-permute-start.9) | collective-permute-done | bytes 540704 | tf_op jit(solution)/shard_map/ppermute | solution.py:588
  55.5 2.2 collective-permute-done.10.refs_3_.rest_8_.rest_9_.rest_6_
  60.6 12.0 %collective-permute-done.13.refs_11_.rest_9_.rest_10_.rest_7_ = bf16[528,512]{1,0:T(8,128)(2,1)S(1)} collective-permute-done((bf16[528,512]{1,0:T(8,128)(2,1)}, bf16[528,512]{1,0:T(8,128)(2,1)S(1)}, u32[]{:S(2)}, u32[]{:S(2)}) %collective-permute-start.13) | collective-permute-done | bytes 540704 | tf_op jit(solution)/shard_map/ppermute | solution.py:588
  73.2 1.8 constant_dynamic-slice_fusion.rest_2_
  75.9 1.6 list_columns.1.cols
  77.5 11.2 %forward_layers.2 = bf16[48,4096]{1,0:T(8,128)(2,1)} custom-call(s32[16,128]{1,0:T(8,128)} %list_columns.1.cols, s32[8]{0:T(128)} %add_multiply_fusion.bases, s32[3]{0:T(128)} %pad_add_fusion.flags, bf16[48,4096]{1,0:T(8,128)(2,1)} %constant_dynamic-slice_fusion.1.rest_0_.rest_1_, bf16[48,4096]{1,0:T(8,128)(2,1)} %constant_dynamic-slice_fusion.1.rest_0_.rest_1_, ...), custom_call_target="tpu_custom_call" | custom-call | flops 8800000000 | bytes 1048576 | tf_op jit(solution)/shard_map/forward_layers/pallas_call | solution.py:339
  88.7 3.5 %collective-permute-start.15 = (bf16[48,4096]{1,0:T(8,128)(2,1)}, bf16[48,4096]{1,0:T(8,128)(2,1)S(1)}, u32[]{:S(2)}, u32[]{:S(2)}) collective-permute-start(bf16[48,4096]{1,0:T(8,128)(2,1)} %forward_layers.2), channel_id=1, source_target_pairs={{0,16},{1,17},{2,18},{3,19},{4,20},{5,21},{6,22},{7,23},{8,24},{9,... | collective-permute-start | bytes 1179656 | tf_op jit(solution)/shard_map/ppermute | solution.py:625
  92.2 9.9 %forward_layers.3 = bf16[32,4096]{1,0:T(8,128)(2,1)} custom-call(s32[16,128]{1,0:T(8,128)} %list_columns.1.cols, s32[8]{0:T(128)} %add_multiply_fusion.bases, s32[3]{0:T(128)} %pad_add_fusion.flags, bf16[32,4096]{1,0:T(8,128)(2,1)} %constant_dynamic-slice_fusion.3.rest_0_.rest_1_, bf16[32,4096]{1,0:T(8,128)(2,1)} %constant_dynamic-slice_fusion.3.rest_0_.rest_1_, ...), custom_call_target="tpu_custom_call" | custom-call | flops 8800000000 | bytes 1048576 | tf_op jit(solution)/shard_map/forward_layers/pallas_call | solution.py:339
  104.2 20.1 %turning_layers.2 = (bf16[2,48,4096]{2,1,0:T(8,128)(2,1)}, bf16[48,4096]{1,0:T(8,128)(2,1)}, bf16[48,4096]{1,0:T(8,128)(2,1)}) custom-call(s32[16,128]{1,0:T(8,128)} %list_columns.1.cols, s32[8]{0:T(128)} %add_multiply_fusion.bases, s32[3]{0:T(128)} %pad_add_fusion.flags, bf16[48,4096]{1,0:T(8,128)(2,1)} %constant_dynamic-slice_fusion.1.rest_0_.rest_1_, ...), custom_call_target="tpu_custom_call" | custom-call | flops 15399999488 | bytes 1048576 | tf_op jit(solution)/shard_map/turning_layers/pallas_call | solution.py:339
  124.3 1.4 collective-permute-start.16
  126.5 17.9 %turning_layers.3 = (bf16[2,32,4096]{2,1,0:T(8,128)(2,1)}, bf16[32,4096]{1,0:T(8,128)(2,1)}, bf16[32,4096]{1,0:T(8,128)(2,1)}) custom-call(s32[16,128]{1,0:T(8,128)} %list_columns.1.cols, s32[8]{0:T(128)} %add_multiply_fusion.bases, s32[3]{0:T(128)} %pad_add_fusion.flags, bf16[32,4096]{1,0:T(8,128)(2,1)} %constant_dynamic-slice_fusion.3.rest_0_.rest_1_, ...), custom_call_target="tpu_custom_call" | custom-call | flops 15399999488 | bytes 1048576 | tf_op jit(solution)/shard_map/turning_layers/pallas_call | solution.py:339
  147.0 6.8 %backward_layers.2.rest_0_ = bf16[2,48,4096]{2,1,0:T(8,128)(2,1)} custom-call(s32[16,128]{1,0:T(8,128)} %list_columns.1.cols, s32[8]{0:T(128)} %add_multiply_fusion.bases, s32[3]{0:T(128)} %pad_add_fusion.flags, bf16[2,48,4096]{2,1,0:T(8,128)(2,1)} %get-tuple-element.65.stash.refs_0_, bf16[48,4096]{1,0:T(8,128)(2,1)} %get-tuple-element.66.loss_grad, ...), custom_call_target="tpu_custom_call" | custom-call | flops 4400000000 | bytes 1048576 | tf_op jit(solution)/shard_map/backward_layers/pallas_call | solution.py:382
  155.5 6.3 %backward_layers.3.rest_1_ = bf16[2,32,4096]{2,1,0:T(8,128)(2,1)} custom-call(s32[16,128]{1,0:T(8,128)} %list_columns.1.cols, s32[8]{0:T(128)} %add_multiply_fusion.bases, s32[3]{0:T(128)} %pad_add_fusion.flags, bf16[2,32,4096]{2,1,0:T(8,128)(2,1)} %get-tuple-element.68.stash.refs_1_, bf16[32,4096]{1,0:T(8,128)(2,1)} %get-tuple-element.69.loss_grad, ...), custom_call_target="tpu_custom_call" | custom-call | flops 4400000000 | bytes 1048576 | tf_op jit(solution)/shard_map/backward_layers/pallas_call | solution.py:382
  163.5 5.4 %flip_rows.1.turned = bf16[2,32,64,160]{3,2,1,0:T(8,128)(2,1)} custom-call(s32[8]{0:T(128)} %add_multiply_fusion.bases, bf16[2,48,4096]{2,1,0:T(8,128)(2,1)} %get-tuple-element.65.stash.refs_0_, bf16[2,32,4096]{2,1,0:T(8,128)(2,1)} %get-tuple-element.68.stash.refs_1_, bf16[2,48,4096]{2,1,0:T(8,128)(2,1)} %copy-done.16, bf16[2,32,4096]{2,1,0:T(8,128)(2,1)} %copy-done.18), custom_call_target="tpu_custom_call" | custom-call | flops 4400000000 | bytes 1048576 | tf_op jit(solution)/shard_map/flip_rows/pallas_call | solution.py:438
  170.6 6.4 %block_grads.2 = (bf16[512,512]{1,0:T(8,128)(2,1)}, bf16[512,512]{1,0:T(8,128)(2,1)}) custom-call(s32[16,128]{1,0:T(8,128)} %list_columns.1.cols, s32[3]{0:T(128)} %pad_add_fusion.flags, bf16[2,32,64,160]{3,2,1,0:T(8,128)(2,1)} %flip_rows.1.turned, bf16[2,48,4096]{2,1,0:T(8,128)(2,1)} %backward_layers.2.rest_0_, ...), custom_call_target="tpu_custom_call" | custom-call | flops 5500000256 | bytes 1048576 | tf_op jit(solution)/shard_map/block_grads/pallas_call | solution.py:484
  177.7 8.9 %block_grads.3 = (bf16[512,512]{1,0:T(8,128)(2,1)}, bf16[512,512]{1,0:T(8,128)(2,1)}, bf16[512,512]{1,0:T(8,128)(2,1)}, bf16[512,512]{1,0:T(8,128)(2,1)}, bf16[5...) custom-call(s32[16,128]{1,0:T(8,128)} %list_columns.1.cols, s32[3]{0:T(128)} %pad_add_fusion.flags, ...), custom_call_target="tpu_custom_call" | custom-call | flops 7699999744 | bytes 1048576 | tf_op jit(solution)/shard_map/block_grads/pallas_call | solution.py:484
  186.6 5.0 %collective-permute-done.23 = bf16[512,512]{1,0:T(8,128)(2,1)S(1)} collective-permute-done((bf16[512,512]{1,0:T(8,128)(2,1)}, bf16[512,512]{1,0:T(8,128)(2,1)S(1)}, u32[]{:S(2)}, u32[]{:S(2)}) %collective-permute-start.23) | collective-permute-done | bytes 524320 | tf_op jit(solution)/shard_map/ppermute | solution.py:588
  193.2 1.5 collective-permute-start.27
  194.7 11.6 %collective-permute-done.24 = bf16[512,512]{1,0:T(8,128)(2,1)S(1)} collective-permute-done((bf16[512,512]{1,0:T(8,128)(2,1)S(1)}, bf16[512,512]{1,0:T(8,128)(2,1)S(1)}, u32[]{:S(2)}, u32[]{:S(2)}) %collective-permute-start.24) | collective-permute-done | bytes 524320 | tf_op jit(solution)/shard_map/ppermute | solution.py:582
  207.7 3.4 %collective-permute-start.26 = (bf16[512,512]{1,0:T(8,128)(2,1)S(1)}, bf16[512,512]{1,0:T(8,128)(2,1)S(1)}, u32[]{:S(2)}, u32[]{:S(2)}) collective-permute-start(bf16[512,512]{1,0:T(8,128)(2,1)S(1)} %add_convert_fusion.2), channel_id=1, source_target_pairs={{0,2},{1,3},{2,6},{3,7},{6,4},{7,5},{4,0},{5,1},{8,10},{9,11},{10,... | collective-permute-start | bytes 1572872 | tf_op jit(solution)/shard_map/ppermute | solution.py:582
  211.8 7.0 %collective-permute-done.27 = bf16[512,512]{1,0:T(8,128)(2,1)S(1)} collective-permute-done((bf16[512,512]{1,0:T(8,128)(2,1)S(1)}, bf16[512,512]{1,0:T(8,128)(2,1)S(1)}, u32[]{:S(2)}, u32[]{:S(2)}) %collective-permute-start.27) | collective-permute-done | bytes 524320 | tf_op jit(solution)/shard_map/ppermute | solution.py:588
  220.3 2.1 collective-permute-start.28
  222.4 6.0 %collective-permute-done.29 = bf16[512,512]{1,0:T(8,128)(2,1)S(1)} collective-permute-done((bf16[512,512]{1,0:T(8,128)(2,1)S(1)}, bf16[512,512]{1,0:T(8,128)(2,1)S(1)}, u32[]{:S(2)}, u32[]{:S(2)}) %collective-permute-start.29) | collective-permute-done | bytes 524320 | tf_op jit(solution)/shard_map/ppermute | solution.py:588
  228.4 3.4 %collective-permute-done.28 = bf16[512,512]{1,0:T(8,128)(2,1)S(1)} collective-permute-done((bf16[512,512]{1,0:T(8,128)(2,1)S(1)}, bf16[512,512]{1,0:T(8,128)(2,1)S(1)}, u32[]{:S(2)}, u32[]{:S(2)}) %collective-permute-start.28) | collective-permute-done | bytes 524320 | tf_op jit(solution)/shard_map/ppermute | solution.py:582
  (118 shorter events, 35.1 us)
Async XLA Ops:
  6.2 68.8 %copy-start.2 = (bf16[528,512]{1,0:T(8,128)(2,1)}, bf16[528,512]{1,0:T(8,128)(2,1)S(1)}, u32[]{:S(2)}) copy-start(bf16[528,512]{1,0:T(8,128)(2,1)S(1)} %fusion.2.refs_0_.rest_2_.rest_3_.rest_0_) | copy-start | bytes 1622020
  6.2 5.9 %collective-permute-start = (bf16[528,512]{1,0:T(8,128)(2,1)S(1)}, bf16[528,512]{1,0:T(8,128)(2,1)S(1)}, u32[]{:S(2)}, u32[]{:S(2)}) collective-permute-start(bf16[528,512]{1,0:T(8,128)(2,1)S(1)} %fusion.2.refs_0_.rest_2_.rest_3_.rest_0_), channel_id=1, source_target_pairs={{0,1},{1,0},{2,3},{3,2},{4,5},{5,4},{6,7},{7,6},{8,9},{9,8},{10,11... | collective-permute-start | bytes 1622024 | tf_op jit(solution)/shard_map/ppermute | solution.py:585
  6.8 15.4 %collective-permute-start.1 = (bf16[528,512]{1,0:T(8,128)(2,1)S(1)}, bf16[528,512]{1,0:T(8,128)(2,1)S(1)}, u32[]{:S(2)}, u32[]{:S(2)}) collective-permute-start(bf16[528,512]{1,0:T(8,128)(2,1)S(1)} %fusion.2.refs_0_.rest_2_.rest_3_.rest_0_), channel_id=1, source_target_pairs={{0,8},{8,0},{1,9},{9,1},{2,10},{10,2},{3,11},{11,3},{4,12},{12,4},... | collective-permute-start | bytes 1622024 | tf_op jit(solution)/shard_map/ppermute | solution.py:588
  9.3 15.2 %collective-permute-start.2 = (bf16[528,512]{1,0:T(8,128)(2,1)S(1)}, bf16[528,512]{1,0:T(8,128)(2,1)S(1)}, u32[]{:S(2)}, u32[]{:S(2)}) collective-permute-start(bf16[528,512]{1,0:T(8,128)(2,1)S(1)} %fusion.2.refs_0_.rest_2_.rest_3_.rest_0_), channel_id=1, source_target_pairs={{0,2},{1,3},{2,6},{3,7},{6,4},{7,5},{4,0},{5,1},{8,10},{9,11},{10,... | collective-permute-start | bytes 1622024 | tf_op jit(solution)/shard_map/ppermute | solution.py:582
  12.2 62.9 %copy-start.3 = (bf16[528,512]{1,0:T(8,128)(2,1)}, bf16[528,512]{1,0:T(8,128)(2,1)S(1)}, u32[]{:S(2)}) copy-start(bf16[528,512]{1,0:T(8,128)(2,1)S(1)} %collective-permute-done.refs_4_.rest_10_.rest_11_.rest_8_) | copy-start | bytes 1622020
  24.6 3.4 %collective-permute-start.4 = (bf16[528,512]{1,0:T(8,128)(2,1)S(1)}, bf16[528,512]{1,0:T(8,128)(2,1)}, u32[]{:S(2)}, u32[]{:S(2)}) collective-permute-start(bf16[528,512]{1,0:T(8,128)(2,1)S(1)} %collective-permute-done.2.refs_1_.rest_4_.rest_5_.rest_2_), channel_id=1, source_target_pairs={{0,1},{1,0},{2,3},{3,2},{4,5},{5,4},{6,7},{7,6},{8,9},{9,8},{10,11... | collective-permute-start | bytes 1622024 | tf_op jit(solution)/shard_map/ppermute | solution.py:585
  24.6 14.8 %collective-permute-start.5 = (bf16[528,512]{1,0:T(8,128)(2,1)S(1)}, bf16[528,512]{1,0:T(8,128)(2,1)}, u32[]{:S(2)}, u32[]{:S(2)}) collective-permute-start(bf16[528,512]{1,0:T(8,128)(2,1)S(1)} %collective-permute-done.2.refs_1_.rest_4_.rest_5_.rest_2_), channel_id=1, source_target_pairs={{0,8},{8,0},{1,9},{9,1},{2,10},{10,2},{3,11},{11,3},{4,12},{12,4},... | collective-permute-start | bytes 1622024 | tf_op jit(solution)/shard_map/ppermute | solution.py:588
  25.1 15.4 %collective-permute-start.6 = (bf16[528,512]{1,0:T(8,128)(2,1)S(1)}, bf16[528,512]{1,0:T(8,128)(2,1)}, u32[]{:S(2)}, u32[]{:S(2)}) collective-permute-start(bf16[528,512]{1,0:T(8,128)(2,1)S(1)} %collective-permute-done.2.refs_1_.rest_4_.rest_5_.rest_2_), channel_id=1, source_target_pairs={{0,2},{1,3},{2,6},{3,7},{6,4},{7,5},{4,0},{5,1},{8,10},{9,11},{10,... | collective-permute-start | bytes 1622024 | tf_op jit(solution)/shard_map/ppermute | solution.py:582
  25.9 2.1 collective-permute-start.3
  40.5 4.5 %collective-permute-start.8 = (bf16[528,512]{1,0:T(8,128)(2,1)}, bf16[528,512]{1,0:T(8,128)(2,1)}, u32[]{:S(2)}, u32[]{:S(2)}) collective-permute-start(bf16[528,512]{1,0:T(8,128)(2,1)} %collective-permute-done.6.refs_2_.rest_6_.rest_7_.rest_4_), channel_id=1, source_target_pairs={{0,1},{1,0},{2,3},{3,2},{4,5},{5,4},{6,7},{7,6},{8,9},{9,8},{10,11... | collective-permute-start | bytes 1622024 | tf_op jit(solution)/shard_map/ppermute | solution.py:585
  40.5 15.0 %collective-permute-start.9 = (bf16[528,512]{1,0:T(8,128)(2,1)}, bf16[528,512]{1,0:T(8,128)(2,1)}, u32[]{:S(2)}, u32[]{:S(2)}) collective-permute-start(bf16[528,512]{1,0:T(8,128)(2,1)} %collective-permute-done.6.refs_2_.rest_6_.rest_7_.rest_4_), channel_id=1, source_target_pairs={{0,8},{8,0},{1,9},{9,1},{2,10},{10,2},{3,11},{11,3},{4,12},{12,4},... | collective-permute-start | bytes 1622024 | tf_op jit(solution)/shard_map/ppermute | solution.py:588
  42.0 15.6 %collective-permute-start.10 = (bf16[528,512]{1,0:T(8,128)(2,1)}, bf16[528,512]{1,0:T(8,128)(2,1)}, u32[]{:S(2)}, u32[]{:S(2)}) collective-permute-start(bf16[528,512]{1,0:T(8,128)(2,1)} %collective-permute-done.6.refs_2_.rest_6_.rest_7_.rest_4_), channel_id=1, source_target_pairs={{0,2},{1,3},{2,6},{3,7},{6,4},{7,5},{4,0},{5,1},{8,10},{9,11},{10,... | collective-permute-start | bytes 1622024 | tf_op jit(solution)/shard_map/ppermute | solution.py:582
  42.7 2.3 collective-permute-start.7
  57.6 2.9 %collective-permute-start.12 = (bf16[528,512]{1,0:T(8,128)(2,1)}, bf16[528,512]{1,0:T(8,128)(2,1)S(1)}, u32[]{:S(2)}, u32[]{:S(2)}) collective-permute-start(bf16[528,512]{1,0:T(8,128)(2,1)} %collective-permute-done.10.refs_3_.rest_8_.rest_9_.rest_6_), channel_id=1, source_target_pairs={{0,1},{1,0},{2,3},{3,2},{4,5},{5,4},{6,7},{7,6},{8,9},{9,8},{10,11... | collective-permute-start | bytes 1622024 | tf_op jit(solution)/shard_map/ppermute | solution.py:585
  57.6 14.9 %collective-permute-start.13 = (bf16[528,512]{1,0:T(8,128)(2,1)}, bf16[528,512]{1,0:T(8,128)(2,1)S(1)}, u32[]{:S(2)}, u32[]{:S(2)}) collective-permute-start(bf16[528,512]{1,0:T(8,128)(2,1)} %collective-permute-done.10.refs_3_.rest_8_.rest_9_.rest_6_), channel_id=1, source_target_pairs={{0,8},{8,0},{1,9},{9,1},{2,10},{10,2},{3,11},{11,3},{4,12},{12,4},... | collective-permute-start | bytes 1622024 | tf_op jit(solution)/shard_map/ppermute | solution.py:588
  58.1 2.4 %collective-permute-start.11 = (bf16[528,512]{1,0:T(8,128)(2,1)}, bf16[528,512]{1,0:T(8,128)(2,1)S(1)}, u32[]{:S(2)}, u32[]{:S(2)}) collective-permute-start(bf16[528,512]{1,0:T(8,128)(2,1)} %collective-permute-done.9.refs_10_.rest_7_.rest_8_.rest_5_), channel_id=1, source_target_pairs={{0,1},{1,0},{2,3},{3,2},{4,5},{5,4},{6,7},{7,6},{8,9},{9,8},{10,11... | collective-permute-start | bytes 1622024 | tf_op jit(solution)/shard_map/ppermute | solution.py:585
  72.5 2.5 %collective-permute-start.14 = (bf16[528,512]{1,0:T(8,128)(2,1)S(1)}, bf16[528,512]{1,0:T(8,128)(2,1)S(1)}, u32[]{:S(2)}, u32[]{:S(2)}) collective-permute-start(bf16[528,512]{1,0:T(8,128)(2,1)S(1)} %collective-permute-done.13.refs_11_.rest_9_.rest_10_.rest_7_), channel_id=1, source_target_pairs={{0,1},{1,0},{2,3},{3,2},{4,5},{5,4},{6,7},{7,6},{8,9},{9,8},{10,11... | collective-permute-start | bytes 1622024 | tf_op jit(solution)/shard_map/ppermute | solution.py:585
  88.7 14.7 %collective-permute-start.15 = (bf16[48,4096]{1,0:T(8,128)(2,1)}, bf16[48,4096]{1,0:T(8,128)(2,1)S(1)}, u32[]{:S(2)}, u32[]{:S(2)}) collective-permute-start(bf16[48,4096]{1,0:T(8,128)(2,1)} %forward_layers.2), channel_id=1, source_target_pairs={{0,16},{1,17},{2,18},{3,19},{4,20},{5,21},{6,22},{7,23},{8,24},{9,... | collective-permute-start | bytes 1179656 | tf_op jit(solution)/shard_map/ppermute | solution.py:625
  102.1 23.6 %collective-permute-start.17 = (bf16[32,4096]{1,0:T(8,128)(2,1)}, bf16[32,4096]{1,0:T(8,128)(2,1)S(1)}, u32[]{:S(2)}, u32[]{:S(2)}) collective-permute-start(bf16[32,4096]{1,0:T(8,128)(2,1)} %forward_layers.3), channel_id=1, source_target_pairs={{0,16},{1,17},{2,18},{3,19},{4,20},{5,21},{6,22},{7,23},{8,24},{9,... | collective-permute-start | bytes 786440 | tf_op jit(solution)/shard_map/ppermute | solution.py:625
  124.3 22.0 %collective-permute-start.16 = (bf16[48,4096]{1,0:T(8,128)(2,1)}, bf16[48,4096]{1,0:T(8,128)(2,1)S(1)}, u32[]{:S(2)}, u32[]{:S(2)}) collective-permute-start(bf16[48,4096]{1,0:T(8,128)(2,1)} %get-tuple-element.67), channel_id=1, source_target_pairs={{16,0},{17,1},{18,2},{19,3},{20,4},{21,5},{22,6},{23,7},{24,8},{25... | collective-permute-start | bytes 1179656 | tf_op jit(solution)/shard_map/ppermute | solution.py:625
  144.4 10.4 %collective-permute-start.18 = (bf16[32,4096]{1,0:T(8,128)(2,1)}, bf16[32,4096]{1,0:T(8,128)(2,1)S(1)}, u32[]{:S(2)}, u32[]{:S(2)}) collective-permute-start(bf16[32,4096]{1,0:T(8,128)(2,1)} %get-tuple-element.70), channel_id=1, source_target_pairs={{16,0},{17,1},{18,2},{19,3},{20,4},{21,5},{22,6},{23,7},{24,8},{25... | collective-permute-start | bytes 786440 | tf_op jit(solution)/shard_map/ppermute | solution.py:625
  145.7 16.2 %collective-permute-start.22 = (bf16[2,32,4096]{2,1,0:T(8,128)(2,1)}, bf16[2,32,4096]{2,1,0:T(8,128)(2,1)S(1)}, u32[]{:S(2)}, u32[]{:S(2)}) collective-permute-start(bf16[2,32,4096]{2,1,0:T(8,128)(2,1)} %get-tuple-element.68.stash.refs_1_), channel_id=1, source_target_pairs={{0,1},{1,0},{2,3},{3,2},{4,5},{5,4},{6,7},{7,6},{8,9},{9,8},{10,11... | collective-permute-start | bytes 1572872 | tf_op jit(solution)/shard_map/ppermute | solution.py:585
  145.9 16.0 %collective-permute-start.21 = (bf16[2,48,4096]{2,1,0:T(8,128)(2,1)S(1)}, bf16[2,48,4096]{2,1,0:T(8,128)(2,1)S(1)}, u32[]{:S(2)}, u32[]{:S(2)}) collective-permute-start(bf16[2,48,4096]{2,1,0:T(8,128)(2,1)S(1)} %copy-done.14), channel_id=1, source_target_pairs={{0,1},{1,0},{2,3},{3,2},{4,5},{5,4},{6,7},{7,6},{8,9},{9,8},{10,11... | collective-permute-start | bytes 2359304 | tf_op jit(solution)/shard_map/ppermute | solution.py:585
  153.8 15.1 %collective-permute-start.19 = (bf16[2,48,4096]{2,1,0:T(8,128)(2,1)}, bf16[2,48,4096]{2,1,0:T(8,128)(2,1)S(1)}, u32[]{:S(2)}, u32[]{:S(2)}) collective-permute-start(bf16[2,48,4096]{2,1,0:T(8,128)(2,1)} %backward_layers.2.rest_0_), channel_id=1, source_target_pairs={{0,1},{1,0},{2,3},{3,2},{4,5},{5,4},{6,7},{7,6},{8,9},{9,8},{10,11... | collective-permute-start | bytes 2359304 | tf_op jit(solution)/shard_map/ppermute | solution.py:585
  161.8 7.2 %collective-permute-start.20 = (bf16[2,32,4096]{2,1,0:T(8,128)(2,1)}, bf16[2,32,4096]{2,1,0:T(8,128)(2,1)S(1)}, u32[]{:S(2)}, u32[]{:S(2)}) collective-permute-start(bf16[2,32,4096]{2,1,0:T(8,128)(2,1)} %backward_layers.3.rest_1_), channel_id=1, source_target_pairs={{0,1},{1,0},{2,3},{3,2},{4,5},{5,4},{6,7},{7,6},{8,9},{9,8},{10,11... | collective-permute-start | bytes 1572872 | tf_op jit(solution)/shard_map/ppermute | solution.py:585
  177.0 14.6 %collective-permute-start.23 = (bf16[512,512]{1,0:T(8,128)(2,1)}, bf16[512,512]{1,0:T(8,128)(2,1)S(1)}, u32[]{:S(2)}, u32[]{:S(2)}) collective-permute-start(bf16[512,512]{1,0:T(8,128)(2,1)} %get-tuple-element.72), channel_id=1, source_target_pairs={{0,8},{8,0},{1,9},{9,1},{2,10},{10,2},{3,11},{11,3},{4,12},{12,4},... | collective-permute-start | bytes 1572872 | tf_op jit(solution)/shard_map/ppermute | solution.py:588
  191.8 14.5 %collective-permute-start.24 = (bf16[512,512]{1,0:T(8,128)(2,1)S(1)}, bf16[512,512]{1,0:T(8,128)(2,1)S(1)}, u32[]{:S(2)}, u32[]{:S(2)}) collective-permute-start(bf16[512,512]{1,0:T(8,128)(2,1)S(1)} %add_convert_fusion.3), channel_id=1, source_target_pairs={{0,2},{1,3},{2,6},{3,7},{6,4},{7,5},{4,0},{5,1},{8,10},{9,11},{10,... | collective-permute-start | bytes 1572872 | tf_op jit(solution)/shard_map/ppermute | solution.py:582
  192.6 14.9 %collective-permute-start.25 = (bf16[512,512]{1,0:T(8,128)(2,1)S(1)}, bf16[512,512]{1,0:T(8,128)(2,1)S(1)}, u32[]{:S(2)}, u32[]{:S(2)}) collective-permute-start(bf16[512,512]{1,0:T(8,128)(2,1)S(1)} %copy-done.21), channel_id=1, source_target_pairs={{0,8},{8,0},{1,9},{9,1},{2,10},{10,2},{3,11},{11,3},{4,12},{12,4},... | collective-permute-start | bytes 1572872 | tf_op jit(solution)/shard_map/ppermute | solution.py:588
  193.2 25.5 %collective-permute-start.27 = (bf16[512,512]{1,0:T(8,128)(2,1)S(1)}, bf16[512,512]{1,0:T(8,128)(2,1)S(1)}, u32[]{:S(2)}, u32[]{:S(2)}) collective-permute-start(bf16[512,512]{1,0:T(8,128)(2,1)S(1)} %copy-done.19), channel_id=1, source_target_pairs={{0,8},{8,0},{1,9},{9,1},{2,10},{10,2},{3,11},{11,3},{4,12},{12,4},... | collective-permute-start | bytes 1572872 | tf_op jit(solution)/shard_map/ppermute | solution.py:588
  207.7 12.4 %collective-permute-start.26 = (bf16[512,512]{1,0:T(8,128)(2,1)S(1)}, bf16[512,512]{1,0:T(8,128)(2,1)S(1)}, u32[]{:S(2)}, u32[]{:S(2)}) collective-permute-start(bf16[512,512]{1,0:T(8,128)(2,1)S(1)} %add_convert_fusion.2), channel_id=1, source_target_pairs={{0,2},{1,3},{2,6},{3,7},{6,4},{7,5},{4,0},{5,1},{8,10},{9,11},{10,... | collective-permute-start | bytes 1572872 | tf_op jit(solution)/shard_map/ppermute | solution.py:582
  211.2 17.2 %collective-permute-start.29 = (bf16[512,512]{1,0:T(8,128)(2,1)S(1)}, bf16[512,512]{1,0:T(8,128)(2,1)S(1)}, u32[]{:S(2)}, u32[]{:S(2)}) collective-permute-start(bf16[512,512]{1,0:T(8,128)(2,1)S(1)} %copy-done.17), channel_id=1, source_target_pairs={{0,8},{8,0},{1,9},{9,1},{2,10},{10,2},{3,11},{11,3},{4,12},{12,4},... | collective-permute-start | bytes 1572872 | tf_op jit(solution)/shard_map/ppermute | solution.py:588
  220.3 11.4 %collective-permute-start.28 = (bf16[512,512]{1,0:T(8,128)(2,1)S(1)}, bf16[512,512]{1,0:T(8,128)(2,1)S(1)}, u32[]{:S(2)}, u32[]{:S(2)}) collective-permute-start(bf16[512,512]{1,0:T(8,128)(2,1)S(1)} %add_convert_fusion.1), channel_id=1, source_target_pairs={{0,2},{1,3},{2,6},{3,7},{6,4},{7,5},{4,0},{5,1},{8,10},{9,11},{10,... | collective-permute-start | bytes 1572872 | tf_op jit(solution)/shard_map/ppermute | solution.py:582
  (25 other events, 320.1 us)
where the time goes:
time: 235 us; the launch traced here: 234 us
  Pallas kernels  94.5 us (40%)
  waiting for transfers between devices  87.9 us (37%)
  starting transfers between devices  26.9 us (11%)
  local copies, waits for them, and re-layouts  18.4 us (8%)
  other arithmetic  6.3 us (3%)
    ppermute x8, waiting for transfers between devices, partner(): lax.ppermute(array, 'side', [(i, sides - 1 - i) for i in range(sides)])  63.1 us
    pallas_call x4, Pallas kernels, forward_pass(): pl.pallas_call(functools.partial(forward_kernel, rows, slots, len(straigh...  59.2 us
    ppermute x6, waiting for transfers between devices, ring(): return lax.ppermute(array, 'dp', hops)  21.9 us
    pallas_call x2, Pallas kernels, block_grad_pass(): pl.pallas_call(functools.partial(block_grad_kernel, rows, slots, tuple(ch...  15.2 us
    pallas_call x2, Pallas kernels, backward_pass(): pl.pallas_call(functools.partial(backward_kernel, rows, slots, len(across...  13.1 us
    ppermute x6, starting transfers between devices, ring(): return lax.ppermute(array, 'dp', hops)  9.51 us
    ppermute x8, starting transfers between devices, partner(): lax.ppermute(array, 'side', [(i, sides - 1 - i) for i in range(sides)])  8.38 us
    ppermute x4, starting transfers between devices, hop(): return lax.ppermute(array, 'stage', route)  7.49 us
  transfers between devices with their start and end apart: 30, of which 18 were waited for; matrix products, arithmetic and copies ran while one was open for 4% of the time, Pallas kernels for 32%

commit v1 on v0

--- a/solution.py
+++ b/solution.py
@@ -10,7 +10,7 @@
 BLK = 64
 LANES = 128
 EPSILON = 1e-05
-VMEM_LIMIT = 54 * 1024 * 1024
+MIB = 1024 * 1024
 STEP_ROWS = 8
 
 TAIL = 16
@@ -342,7 +342,7 @@
         out_specs=[IN_VMEM] * len(outs),
         out_shape=outs,
         scratch_shapes=scratch,
-        compiler_params=pltpu.CompilerParams(vmem_limit_bytes=VMEM_LIMIT),
+        compiler_params=pltpu.CompilerParams(vmem_limit_bytes=(16 if goal is None else 20) * MIB),
         cost_estimate=about(8 if goal is None else 14),
         name="forward_layers" if goal is None else "turning_layers",
     )(*meta, *ins, *pieces)
@@ -391,7 +391,7 @@
             pltpu.VMEM((blocks // 2, tokens, LANES), jnp.float32),
             landed,
         ],
-        compiler_params=pltpu.CompilerParams(vmem_limit_bytes=VMEM_LIMIT),
+        compiler_params=pltpu.CompilerParams(vmem_limit_bytes=18 * MIB),
         cost_estimate=about(4 * depth),
         name="backward_layers",
     )(*meta, stash, loss_grad, moved, *across)
@@ -444,7 +444,7 @@
             pltpu.VMEM((2, tokens, feats), jnp.bfloat16),
             pltpu.SemaphoreType.DMA((len(stashes),)),
         ],
-        compiler_params=pltpu.CompilerParams(vmem_limit_bytes=VMEM_LIMIT),
+        compiler_params=pltpu.CompilerParams(vmem_limit_bytes=12 * MIB),
         cost_estimate=about(4),
         name="flip_rows",
     )(bases, *stashes)
@@ -496,7 +496,7 @@
             pltpu.SemaphoreType.DMA((len(cotangents),)),
             pltpu.SemaphoreType.DMA((len(chosen),)),
         ],
-        compiler_params=pltpu.CompilerParams(vmem_limit_bytes=VMEM_LIMIT),
+        compiler_params=pltpu.CompilerParams(vmem_limit_bytes=18 * MIB),
         cost_estimate=about(4 + len(chosen)),
         name="block_grads",
     )(cols, flags, turned, *cotangents)
@@ -528,7 +528,7 @@
             pltpu.VMEM((count, TAIL, slots * BLK), jnp.bfloat16),
             pltpu.SemaphoreType.DMA((count,)),
         ],
-        compiler_params=pltpu.CompilerParams(vmem_limit_bytes=VMEM_LIMIT),
+        compiler_params=pltpu.CompilerParams(vmem_limit_bytes=4 * MIB),
         cost_estimate=about(2),
         name="list_columns",
     )(*pieces)

time: 235 us -> 214 us (0.911)
  Pallas kernels: 94.5 us -> 76.3 us
  local copies, waits for them, and re-layouts: 18.4 us -> 9.15 us
  waiting for transfers between devices: 87.9 us -> 96.3 us
    unnamed x54 -> x8, local copies, waits for them, and re-layouts: 7.07 us -> 0.02 us
    pallas_call x2, Pallas kernels: 15.2 us -> 9.16 us  [block_grad_pass(): pl.pallas_call(functools.partial(block_grad_kernel, rows, slots, tuple(ch...]
    pallas_call x4, Pallas kernels: 59.2 us -> 53.4 us  [forward_pass(): pl.pallas_call(functools.partial(forward_kernel, rows, slots, len(straigh...]
    ppermute x8, waiting for transfers between devices: 63.1 us -> 66.5 us  [partner(): lax.ppermute(array, 'side', [(i, sides - 1 - i) for i in range(sides)])]
    pallas_call x1, Pallas kernels: 5.39 us -> 2.44 us  [flip_pass(): pl.pallas_call(functools.partial(flip_kernel, rows, chosen), in_specs=[IN...]
    ppermute x12, waiting for transfers between devices: 2.06 us -> 4.93 us  [sibling(): return lax.ppermute(array, 'dp', [(i, i ^ 1) for i in range(dp_count)])]
    pallas_call x2, Pallas kernels: 13.1 us -> 10.3 us  [backward_pass(): pl.pallas_call(functools.partial(backward_kernel, rows, slots, len(across...]
  transfers between devices with their start and end apart: 30 -> 30, of which waited for: 18 -> 19; matrix products, arithmetic and copies ran while one was open for 4% -> 2% of each run, Pallas kernels for 32% -> 29%
where the time goes in v1:
time: 214 us
  waiting for transfers between devices  96.3 us (45%)
  Pallas kernels  76.3 us (36%)
  starting transfers between devices  26.6 us (12%)
  local copies, waits for them, and re-layouts  9.15 us (4%)
  other arithmetic  5.09 us (2%)
    ppermute x8, waiting for transfers between devices, partner(): lax.ppermute(array, 'side', [(i, sides - 1 - i) for i in range(sides)])  66.5 us
    pallas_call x4, Pallas kernels, forward_pass(): pl.pallas_call(functools.partial(forward_kernel, rows, slots, len(straigh...  53.4 us
    ppermute x6, waiting for transfers between devices, ring(): return lax.ppermute(array, 'dp', hops)  22.1 us
    pallas_call x2, Pallas kernels, backward_pass(): pl.pallas_call(functools.partial(backward_kernel, rows, slots, len(across...  10.3 us
    ppermute x6, starting transfers between devices, ring(): return lax.ppermute(array, 'dp', hops)  9.46 us
    pallas_call x2, Pallas kernels, block_grad_pass(): pl.pallas_call(functools.partial(block_grad_kernel, rows, slots, tuple(ch...  9.16 us
    ppermute x8, starting transfers between devices, partner(): lax.ppermute(array, 'side', [(i, sides - 1 - i) for i in range(sides)])  8.24 us
    ppermute x4, starting transfers between devices, hop(): return lax.ppermute(array, 'stage', route)  7.34 us
  transfers between devices with their start and end apart: 30, of which 19 were waited for; matrix products, arithmetic and copies ran while one was open for 2% of the time, Pallas kernels for 29%

profile of v1, /device:TPU:0, one launch (start us, length us, event | category | flops | bytes accessed | tf_op | source)
XLA Modules:
  0.0 213.7 jit_solution(8550377790239505076)
XLA Ops:
  0.9 2.1 squeeze.6
  3.7 1.4 reshape.113
  6.7 2.6 %collective-permute-start.1 = (bf16[528,512]{1,0:T(8,128)(2,1)S(1)}, bf16[528,512]{1,0:T(8,128)(2,1)S(1)}, u32[]{:S(2)}, u32[]{:S(2)}) collective-permute-start(bf16[528,512]{1,0:T(8,128)(2,1)S(1)} %fusion.2.refs_0_.rest_2_.rest_3_.rest_0_), channel_id=1, source_target_pairs={{0,8},{8,0},{1,9},{9,1},{2,10},{10,2},{3,11},{11,3},{4,12},{12,4},... | collective-permute-start | bytes 1622024 | tf_op jit(solution)/shard_map/ppermute | solution.py:588
  9.3 1.6 collective-permute-start.2
  12.1 10.0 %collective-permute-done.1.refs_8_.rest_3_.rest_4_.rest_1_ = bf16[528,512]{1,0:T(8,128)(2,1)S(1)} collective-permute-done((bf16[528,512]{1,0:T(8,128)(2,1)S(1)}, bf16[528,512]{1,0:T(8,128)(2,1)S(1)}, u32[]{:S(2)}, u32[]{:S(2)}) %collective-permute-start.1) | collective-permute-done | bytes 540704 | tf_op jit(solution)/shard_map/ppermute | solution.py:588
  22.2 2.4 %collective-permute-done.2.refs_1_.rest_4_.rest_5_.rest_2_ = bf16[528,512]{1,0:T(8,128)(2,1)S(1)} collective-permute-done((bf16[528,512]{1,0:T(8,128)(2,1)S(1)}, bf16[528,512]{1,0:T(8,128)(2,1)S(1)}, u32[]{:S(2)}, u32[]{:S(2)}) %collective-permute-start.2) | collective-permute-done | bytes 540704 | tf_op jit(solution)/shard_map/ppermute | solution.py:582
  27.9 11.4 %collective-permute-done.5.refs_9_.rest_5_.rest_6_.rest_3_ = bf16[528,512]{1,0:T(8,128)(2,1)} collective-permute-done((bf16[528,512]{1,0:T(8,128)(2,1)S(1)}, bf16[528,512]{1,0:T(8,128)(2,1)}, u32[]{:S(2)}, u32[]{:S(2)}) %collective-permute-start.5) | collective-permute-done | bytes 540704 | tf_op jit(solution)/shard_map/ppermute | solution.py:588
  40.5 1.5 collective-permute-start.9
  45.0 10.5 %collective-permute-done.9.refs_10_.rest_7_.rest_8_.rest_5_ = bf16[528,512]{1,0:T(8,128)(2,1)} collective-permute-done((bf16[528,512]{1,0:T(8,128)(2,1)}, bf16[528,512]{1,0:T(8,128)(2,1)}, u32[]{:S(2)}, u32[]{:S(2)}) %collective-permute-start.9) | collective-permute-done | bytes 540704 | tf_op jit(solution)/shard_map/ppermute | solution.py:588
  55.5 2.2 %collective-permute-done.10.refs_3_.rest_8_.rest_9_.rest_6_ = bf16[528,512]{1,0:T(8,128)(2,1)} collective-permute-done((bf16[528,512]{1,0:T(8,128)(2,1)}, bf16[528,512]{1,0:T(8,128)(2,1)}, u32[]{:S(2)}, u32[]{:S(2)}) %collective-permute-start.10) | collective-permute-done | bytes 540704 | tf_op jit(solution)/shard_map/ppermute | solution.py:582
  58.4 2.1 collective-permute-done.11.refs_14_.rest_15_.rest_16_.rest_13_
  60.5 12.0 %collective-permute-done.13.refs_11_.rest_9_.rest_10_.rest_7_ = bf16[528,512]{1,0:T(8,128)(2,1)S(1)} collective-permute-done((bf16[528,512]{1,0:T(8,128)(2,1)}, bf16[528,512]{1,0:T(8,128)(2,1)S(1)}, u32[]{:S(2)}, u32[]{:S(2)}) %collective-permute-start.13) | collective-permute-done | bytes 540704 | tf_op jit(solution)/shard_map/ppermute | solution.py:588
  75.5 9.9 %forward_layers.2 = bf16[48,4096]{1,0:T(8,128)(2,1)S(1)} custom-call(s32[16,128]{1,0:T(8,128)S(1)} %list_columns.1.cols, s32[8]{0:T(128)S(1)} %add_multiply_fusion.bases, s32[3]{0:T(128)S(1)} %pad_add_fusion.flags, bf16[48,4096]{1,0:T(8,128)(2,1)S(1)} %constant_dynamic-slice_fusion.1.rest_0_.rest_1_, ...), custom_call_target="tpu_custom_call" | custom-call | flops 8800000000 | bytes 1048576 | tf_op jit(solution)/shard_map/forward_layers/pallas_call | solution.py:339
  85.4 3.5 %collective-permute-start.15 = (bf16[48,4096]{1,0:T(8,128)(2,1)S(1)}, bf16[48,4096]{1,0:T(8,128)(2,1)S(1)}, u32[]{:S(2)}, u32[]{:S(2)}) collective-permute-start(bf16[48,4096]{1,0:T(8,128)(2,1)S(1)} %forward_layers.2), channel_id=1, source_target_pairs={{0,16},{1,17},{2,18},{3,19},{4,20},{5,21},{6,22},{7,23},{8,24},{9,... | collective-permute-start | bytes 1179656 | tf_op jit(solution)/shard_map/ppermute | solution.py:625
  88.9 8.7 %forward_layers.3 = bf16[32,4096]{1,0:T(8,128)(2,1)S(1)} custom-call(s32[16,128]{1,0:T(8,128)S(1)} %list_columns.1.cols, s32[8]{0:T(128)S(1)} %add_multiply_fusion.bases, s32[3]{0:T(128)S(1)} %pad_add_fusion.flags, bf16[32,4096]{1,0:T(8,128)(2,1)S(1)} %copy-done.1, bf16[32,4096]{1,0:T(8,128)(2,1)S(1)} %copy-done.1, ...), custom_call_target="tpu_custom_call" | custom-call | flops 8800000000 | bytes 1048576 | tf_op jit(solution)/shard_map/forward_layers/pallas_call | solution.py:339
  98.9 18.4 %turning_layers.2 = (bf16[2,48,4096]{2,1,0:T(8,128)(2,1)S(1)}, bf16[48,4096]{1,0:T(8,128)(2,1)S(1)}, bf16[48,4096]{1,0:T(8,128)(2,1)S(1)}) custom-call(s32[16,128]{1,0:T(8,128)S(1)} %list_columns.1.cols, s32[8]{0:T(128)S(1)} %add_multiply_fusion.bases, s32[3]{0:T(128)S(1)} %pad_add_fusion.flags, ...), custom_call_target="tpu_custom_call" | custom-call | flops 15399999488 | bytes 1048576 | tf_op jit(solution)/shard_map/turning_layers/pallas_call | solution.py:339
  118.6 16.4 %turning_layers.3 = (bf16[2,32,4096]{2,1,0:T(8,128)(2,1)S(1)}, bf16[32,4096]{1,0:T(8,128)(2,1)S(1)}, bf16[32,4096]{1,0:T(8,128)(2,1)S(1)}) custom-call(s32[16,128]{1,0:T(8,128)S(1)} %list_columns.1.cols, s32[8]{0:T(128)S(1)} %add_multiply_fusion.bases, s32[3]{0:T(128)S(1)} %pad_add_fusion.flags, bf16[32,4096]{1,0:T(8,128)(2,1)S(1)} %copy-done.1, ...), custom_call_target="tpu_custom_call" | custom-call | flops 15399999488 | bytes 1048576 | tf_op jit(solution)/shard_map/turning_layers/pallas_call | solution.py:339
  136.9 5.2 %backward_layers.2.rest_0_ = bf16[2,48,4096]{2,1,0:T(8,128)(2,1)S(1)} custom-call(s32[16,128]{1,0:T(8,128)S(1)} %list_columns.1.cols, s32[8]{0:T(128)S(1)} %add_multiply_fusion.bases, s32[3]{0:T(128)S(1)} %pad_add_fusion.flags, bf16[2,48,4096]{2,1,0:T(8,128)(2,1)S(1)} %get-tuple-element.65.stash.refs_0_, bf16[48,4096]{1,0:T(8,128)(2,1)S(1)} %get-tuple-element.66.loss_grad, ...), custom_call_target="tpu_custom_call" | custom-call | flops 4400000000 | bytes 1048576 | tf_op jit(solution)/shard_map/backward_layers/pallas_call | solution.py:382
  142.3 2.8 %collective-permute-done.18.moved = bf16[32,4096]{1,0:T(8,128)(2,1)S(1)} collective-permute-done((bf16[32,4096]{1,0:T(8,128)(2,1)S(1)}, bf16[32,4096]{1,0:T(8,128)(2,1)S(1)}, u32[]{:S(2)}, u32[]{:S(2)}) %collective-permute-start.18) | collective-permute-done | bytes 262176 | tf_op jit(solution)/shard_map/ppermute | solution.py:625
  145.0 5.1 %backward_layers.3.rest_1_ = bf16[2,32,4096]{2,1,0:T(8,128)(2,1)S(1)} custom-call(s32[16,128]{1,0:T(8,128)S(1)} %list_columns.1.cols, s32[8]{0:T(128)S(1)} %add_multiply_fusion.bases, s32[3]{0:T(128)S(1)} %pad_add_fusion.flags, bf16[2,32,4096]{2,1,0:T(8,128)(2,1)S(1)} %get-tuple-element.68.stash.refs_1_, bf16[32,4096]{1,0:T(8,128)(2,1)S(1)} %get-tuple-element.69.loss_grad, ...), custom_call_target="tpu_custom_call" | custom-call | flops 4400000000 | bytes 1048576 | tf_op jit(solution)/shard_map/backward_layers/pallas_call | solution.py:382
  150.2 2.4 %flip_rows.1.turned = bf16[2,32,64,160]{3,2,1,0:T(8,128)(2,1)S(1)} custom-call(s32[8]{0:T(128)S(1)} %add_multiply_fusion.bases, bf16[2,48,4096]{2,1,0:T(8,128)(2,1)S(1)} %get-tuple-element.65.stash.refs_0_, bf16[2,32,4096]{2,1,0:T(8,128)(2,1)S(1)} %get-tuple-element.68.stash.refs_1_, bf16[2,48,4096]{2,1,0:T(8,128)(2,1)S(1)} %collective-permute-done.21.refs_2_, ...), custom_call_target="tpu_custom_call" | custom-call | flops 4400000000 | bytes 1048576 | tf_op jit(solution)/shard_map/flip_rows/pallas_call | solution.py:438
  152.7 3.8 %block_grads.2 = (bf16[512,512]{1,0:T(8,128)(2,1)S(1)}, bf16[512,512]{1,0:T(8,128)(2,1)S(1)}) custom-call(s32[16,128]{1,0:T(8,128)S(1)} %list_columns.1.cols, s32[3]{0:T(128)S(1)} %pad_add_fusion.flags, bf16[2,32,64,160]{3,2,1,0:T(8,128)(2,1)S(1)} %flip_rows.1.turned, bf16[2,48,4096]{2,1,0:T(8,128)(2,1)S(1)} %backward_layers.2.rest_0_, ...), custom_call_target="tpu_custom_call" | custom-call | flops 5500000256 | bytes 1048576 | tf_op jit(solution)/shard_map/block_grads/pallas_call | solution.py:484
  157.1 5.4 %block_grads.3 = (bf16[512,512]{1,0:T(8,128)(2,1)S(1)}, bf16[512,512]{1,0:T(8,128)(2,1)S(1)}, bf16[512,512]{1,0:T(8,128)(2,1)S(1)}, bf16[512,512]{1,0:T(8,128)(2...) custom-call(s32[16,128]{1,0:T(8,128)S(1)} %list_columns.1.cols, s32[3]{0:T(128)S(1)} %pad_add_fusion.flags, ...), custom_call_target="tpu_custom_call" | custom-call | flops 7699999744 | bytes 1048576 | tf_op jit(solution)/shard_map/block_grads/pallas_call | solution.py:484
  162.5 8.4 %collective-permute-done.23 = bf16[512,512]{1,0:T(8,128)(2,1)S(1)} collective-permute-done((bf16[512,512]{1,0:T(8,128)(2,1)S(1)}, bf16[512,512]{1,0:T(8,128)(2,1)S(1)}, u32[]{:S(2)}, u32[]{:S(2)}) %collective-permute-start.23) | collective-permute-done | bytes 524320 | tf_op jit(solution)/shard_map/ppermute | solution.py:588
  172.4 1.5 collective-permute-start.27
  173.9 11.6 %collective-permute-done.24 = bf16[512,512]{1,0:T(8,128)(2,1)S(1)} collective-permute-done((bf16[512,512]{1,0:T(8,128)(2,1)S(1)}, bf16[512,512]{1,0:T(8,128)(2,1)S(1)}, u32[]{:S(2)}, u32[]{:S(2)}) %collective-permute-start.24) | collective-permute-done | bytes 524320 | tf_op jit(solution)/shard_map/ppermute | solution.py:582
  186.9 3.4 %collective-permute-start.26 = (bf16[512,512]{1,0:T(8,128)(2,1)S(1)}, bf16[512,512]{1,0:T(8,128)(2,1)S(1)}, u32[]{:S(2)}, u32[]{:S(2)}) collective-permute-start(bf16[512,512]{1,0:T(8,128)(2,1)S(1)} %add_convert_fusion.2), channel_id=1, source_target_pairs={{0,2},{1,3},{2,6},{3,7},{6,4},{7,5},{4,0},{5,1},{8,10},{9,11},{10,... | collective-permute-start | bytes 1572872 | tf_op jit(solution)/shard_map/ppermute | solution.py:582
  190.9 7.1 %collective-permute-done.27 = bf16[512,512]{1,0:T(8,128)(2,1)S(1)} collective-permute-done((bf16[512,512]{1,0:T(8,128)(2,1)S(1)}, bf16[512,512]{1,0:T(8,128)(2,1)S(1)}, u32[]{:S(2)}, u32[]{:S(2)}) %collective-permute-start.27) | collective-permute-done | bytes 524320 | tf_op jit(solution)/shard_map/ppermute | solution.py:588
  197.9 1.4 collective-permute-done.26
  199.5 2.1 collective-permute-start.28
  201.6 5.9 %collective-permute-done.29 = bf16[512,512]{1,0:T(8,128)(2,1)S(1)} collective-permute-done((bf16[512,512]{1,0:T(8,128)(2,1)S(1)}, bf16[512,512]{1,0:T(8,128)(2,1)S(1)}, u32[]{:S(2)}, u32[]{:S(2)}) %collective-permute-start.29) | collective-permute-done | bytes 524320 | tf_op jit(solution)/shard_map/ppermute | solution.py:588
  207.5 3.4 %collective-permute-done.28 = bf16[512,512]{1,0:T(8,128)(2,1)S(1)} collective-permute-done((bf16[512,512]{1,0:T(8,128)(2,1)S(1)}, bf16[512,512]{1,0:T(8,128)(2,1)S(1)}, u32[]{:S(2)}, u32[]{:S(2)}) %collective-permute-start.28) | collective-permute-done | bytes 524320 | tf_op jit(solution)/shard_map/ppermute | solution.py:582
  (72 shorter events, 27.4 us)
Async XLA Ops:
  0.0 26.5 %copy-start = (bf16[2,80,4096]{2,1,0:T(8,128)(2,1)S(1)}, bf16[2,80,4096]{2,1,0:T(8,128)(2,1)}, u32[]{:S(2)}) copy-start(bf16[2,80,4096]{2,1,0:T(8,128)(2,1)} %param.7) | copy-start | bytes 3932164
  6.2 5.9 %collective-permute-start = (bf16[528,512]{1,0:T(8,128)(2,1)S(1)}, bf16[528,512]{1,0:T(8,128)(2,1)S(1)}, u32[]{:S(2)}, u32[]{:S(2)}) collective-permute-start(bf16[528,512]{1,0:T(8,128)(2,1)S(1)} %fusion.2.refs_0_.rest_2_.rest_3_.rest_0_), channel_id=1, source_target_pairs={{0,1},{1,0},{2,3},{3,2},{4,5},{5,4},{6,7},{7,6},{8,9},{9,8},{10,11... | collective-permute-start | bytes 1622024 | tf_op jit(solution)/shard_map/ppermute | solution.py:585
  6.7 15.4 %collective-permute-start.1 = (bf16[528,512]{1,0:T(8,128)(2,1)S(1)}, bf16[528,512]{1,0:T(8,128)(2,1)S(1)}, u32[]{:S(2)}, u32[]{:S(2)}) collective-permute-start(bf16[528,512]{1,0:T(8,128)(2,1)S(1)} %fusion.2.refs_0_.rest_2_.rest_3_.rest_0_), channel_id=1, source_target_pairs={{0,8},{8,0},{1,9},{9,1},{2,10},{10,2},{3,11},{11,3},{4,12},{12,4},... | collective-permute-start | bytes 1622024 | tf_op jit(solution)/shard_map/ppermute | solution.py:588
  9.3 15.2 %collective-permute-start.2 = (bf16[528,512]{1,0:T(8,128)(2,1)S(1)}, bf16[528,512]{1,0:T(8,128)(2,1)S(1)}, u32[]{:S(2)}, u32[]{:S(2)}) collective-permute-start(bf16[528,512]{1,0:T(8,128)(2,1)S(1)} %fusion.2.refs_0_.rest_2_.rest_3_.rest_0_), channel_id=1, source_target_pairs={{0,2},{1,3},{2,6},{3,7},{6,4},{7,5},{4,0},{5,1},{8,10},{9,11},{10,... | collective-permute-start | bytes 1622024 | tf_op jit(solution)/shard_map/ppermute | solution.py:582
  24.6 3.4 %collective-permute-start.4 = (bf16[528,512]{1,0:T(8,128)(2,1)S(1)}, bf16[528,512]{1,0:T(8,128)(2,1)}, u32[]{:S(2)}, u32[]{:S(2)}) collective-permute-start(bf16[528,512]{1,0:T(8,128)(2,1)S(1)} %collective-permute-done.2.refs_1_.rest_4_.rest_5_.rest_2_), channel_id=1, source_target_pairs={{0,1},{1,0},{2,3},{3,2},{4,5},{5,4},{6,7},{7,6},{8,9},{9,8},{10,11... | collective-permute-start | bytes 1622024 | tf_op jit(solution)/shard_map/ppermute | solution.py:585
  24.6 14.8 %collective-permute-start.5 = (bf16[528,512]{1,0:T(8,128)(2,1)S(1)}, bf16[528,512]{1,0:T(8,128)(2,1)}, u32[]{:S(2)}, u32[]{:S(2)}) collective-permute-start(bf16[528,512]{1,0:T(8,128)(2,1)S(1)} %collective-permute-done.2.refs_1_.rest_4_.rest_5_.rest_2_), channel_id=1, source_target_pairs={{0,8},{8,0},{1,9},{9,1},{2,10},{10,2},{3,11},{11,3},{4,12},{12,4},... | collective-permute-start | bytes 1622024 | tf_op jit(solution)/shard_map/ppermute | solution.py:588
  25.0 15.4 %collective-permute-start.6 = (bf16[528,512]{1,0:T(8,128)(2,1)S(1)}, bf16[528,512]{1,0:T(8,128)(2,1)}, u32[]{:S(2)}, u32[]{:S(2)}) collective-permute-start(bf16[528,512]{1,0:T(8,128)(2,1)S(1)} %collective-permute-done.2.refs_1_.rest_4_.rest_5_.rest_2_), channel_id=1, source_target_pairs={{0,2},{1,3},{2,6},{3,7},{6,4},{7,5},{4,0},{5,1},{8,10},{9,11},{10,... | collective-permute-start | bytes 1622024 | tf_op jit(solution)/shard_map/ppermute | solution.py:582
  25.9 2.1 collective-permute-start.3
  40.5 4.5 %collective-permute-start.8 = (bf16[528,512]{1,0:T(8,128)(2,1)}, bf16[528,512]{1,0:T(8,128)(2,1)}, u32[]{:S(2)}, u32[]{:S(2)}) collective-permute-start(bf16[528,512]{1,0:T(8,128)(2,1)} %collective-permute-done.6.refs_2_.rest_6_.rest_7_.rest_4_), channel_id=1, source_target_pairs={{0,1},{1,0},{2,3},{3,2},{4,5},{5,4},{6,7},{7,6},{8,9},{9,8},{10,11... | collective-permute-start | bytes 1622024 | tf_op jit(solution)/shard_map/ppermute | solution.py:585
  40.5 15.0 %collective-permute-start.9 = (bf16[528,512]{1,0:T(8,128)(2,1)}, bf16[528,512]{1,0:T(8,128)(2,1)}, u32[]{:S(2)}, u32[]{:S(2)}) collective-permute-start(bf16[528,512]{1,0:T(8,128)(2,1)} %collective-permute-done.6.refs_2_.rest_6_.rest_7_.rest_4_), channel_id=1, source_target_pairs={{0,8},{8,0},{1,9},{9,1},{2,10},{10,2},{3,11},{11,3},{4,12},{12,4},... | collective-permute-start | bytes 1622024 | tf_op jit(solution)/shard_map/ppermute | solution.py:588
  42.0 15.6 %collective-permute-start.10 = (bf16[528,512]{1,0:T(8,128)(2,1)}, bf16[528,512]{1,0:T(8,128)(2,1)}, u32[]{:S(2)}, u32[]{:S(2)}) collective-permute-start(bf16[528,512]{1,0:T(8,128)(2,1)} %collective-permute-done.6.refs_2_.rest_6_.rest_7_.rest_4_), channel_id=1, source_target_pairs={{0,2},{1,3},{2,6},{3,7},{6,4},{7,5},{4,0},{5,1},{8,10},{9,11},{10,... | collective-permute-start | bytes 1622024 | tf_op jit(solution)/shard_map/ppermute | solution.py:582
  42.7 2.3 %collective-permute-start.7 = (bf16[528,512]{1,0:T(8,128)(2,1)}, bf16[528,512]{1,0:T(8,128)(2,1)}, u32[]{:S(2)}, u32[]{:S(2)}) collective-permute-start(bf16[528,512]{1,0:T(8,128)(2,1)} %collective-permute-done.5.refs_9_.rest_5_.rest_6_.rest_3_), channel_id=1, source_target_pairs={{0,1},{1,0},{2,3},{3,2},{4,5},{5,4},{6,7},{7,6},{8,9},{9,8},{10,11... | collective-permute-start | bytes 1622024 | tf_op jit(solution)/shard_map/ppermute | solution.py:585
  57.6 2.9 %collective-permute-start.12 = (bf16[528,512]{1,0:T(8,128)(2,1)}, bf16[528,512]{1,0:T(8,128)(2,1)S(1)}, u32[]{:S(2)}, u32[]{:S(2)}) collective-permute-start(bf16[528,512]{1,0:T(8,128)(2,1)} %collective-permute-done.10.refs_3_.rest_8_.rest_9_.rest_6_), channel_id=1, source_target_pairs={{0,1},{1,0},{2,3},{3,2},{4,5},{5,4},{6,7},{7,6},{8,9},{9,8},{10,11... | collective-permute-start | bytes 1622024 | tf_op jit(solution)/shard_map/ppermute | solution.py:585
  57.6 14.9 %collective-permute-start.13 = (bf16[528,512]{1,0:T(8,128)(2,1)}, bf16[528,512]{1,0:T(8,128)(2,1)S(1)}, u32[]{:S(2)}, u32[]{:S(2)}) collective-permute-start(bf16[528,512]{1,0:T(8,128)(2,1)} %collective-permute-done.10.refs_3_.rest_8_.rest_9_.rest_6_), channel_id=1, source_target_pairs={{0,8},{8,0},{1,9},{9,1},{2,10},{10,2},{3,11},{11,3},{4,12},{12,4},... | collective-permute-start | bytes 1622024 | tf_op jit(solution)/shard_map/ppermute | solution.py:588
  58.1 2.4 %collective-permute-start.11 = (bf16[528,512]{1,0:T(8,128)(2,1)}, bf16[528,512]{1,0:T(8,128)(2,1)S(1)}, u32[]{:S(2)}, u32[]{:S(2)}) collective-permute-start(bf16[528,512]{1,0:T(8,128)(2,1)} %collective-permute-done.9.refs_10_.rest_7_.rest_8_.rest_5_), channel_id=1, source_target_pairs={{0,1},{1,0},{2,3},{3,2},{4,5},{5,4},{6,7},{7,6},{8,9},{9,8},{10,11... | collective-permute-start | bytes 1622024 | tf_op jit(solution)/shard_map/ppermute | solution.py:585
  72.5 1.9 collective-permute-start.14
  75.5 13.4 %copy-start.1 = (bf16[32,4096]{1,0:T(8,128)(2,1)S(1)}, bf16[32,4096]{1,0:T(8,128)(2,1)}, u32[]{:S(2)}) copy-start(bf16[32,4096]{1,0:T(8,128)(2,1)} %constant_dynamic-slice_fusion.3.rest_0_.rest_1_) | copy-start | bytes 786436
  85.4 13.5 %collective-permute-start.15 = (bf16[48,4096]{1,0:T(8,128)(2,1)S(1)}, bf16[48,4096]{1,0:T(8,128)(2,1)S(1)}, u32[]{:S(2)}, u32[]{:S(2)}) collective-permute-start(bf16[48,4096]{1,0:T(8,128)(2,1)S(1)} %forward_layers.2), channel_id=1, source_target_pairs={{0,16},{1,17},{2,18},{3,19},{4,20},{5,21},{6,22},{7,23},{8,24},{9,... | collective-permute-start | bytes 1179656 | tf_op jit(solution)/shard_map/ppermute | solution.py:625
  97.6 21.1 %collective-permute-start.17 = (bf16[32,4096]{1,0:T(8,128)(2,1)S(1)}, bf16[32,4096]{1,0:T(8,128)(2,1)S(1)}, u32[]{:S(2)}, u32[]{:S(2)}) collective-permute-start(bf16[32,4096]{1,0:T(8,128)(2,1)S(1)} %forward_layers.3), channel_id=1, source_target_pairs={{0,16},{1,17},{2,18},{3,19},{4,20},{5,21},{6,22},{7,23},{8,24},{9,... | collective-permute-start | bytes 786440 | tf_op jit(solution)/shard_map/ppermute | solution.py:625
  117.3 19.6 %collective-permute-start.16 = (bf16[48,4096]{1,0:T(8,128)(2,1)S(1)}, bf16[48,4096]{1,0:T(8,128)(2,1)S(1)}, u32[]{:S(2)}, u32[]{:S(2)}) collective-permute-start(bf16[48,4096]{1,0:T(8,128)(2,1)S(1)} %get-tuple-element.67), channel_id=1, source_target_pairs={{16,0},{17,1},{18,2},{19,3},{20,4},{21,5},{22,6},{23,7},{24,8},{25... | collective-permute-start | bytes 1179656 | tf_op jit(solution)/shard_map/ppermute | solution.py:625
  135.1 10.0 %collective-permute-start.18 = (bf16[32,4096]{1,0:T(8,128)(2,1)S(1)}, bf16[32,4096]{1,0:T(8,128)(2,1)S(1)}, u32[]{:S(2)}, u32[]{:S(2)}) collective-permute-start(bf16[32,4096]{1,0:T(8,128)(2,1)S(1)} %get-tuple-element.70), channel_id=1, source_target_pairs={{16,0},{17,1},{18,2},{19,3},{20,4},{21,5},{22,6},{23,7},{24,8},{25... | collective-permute-start | bytes 786440 | tf_op jit(solution)/shard_map/ppermute | solution.py:625
  136.4 13.8 %collective-permute-start.22 = (bf16[2,32,4096]{2,1,0:T(8,128)(2,1)S(1)}, bf16[2,32,4096]{2,1,0:T(8,128)(2,1)S(1)}, u32[]{:S(2)}, u32[]{:S(2)}) collective-permute-start(bf16[2,32,4096]{2,1,0:T(8,128)(2,1)S(1)} %get-tuple-element.68.stash.refs_1_), channel_id=1, source_target_pairs={{0,1},{1,0},{2,3},{3,2},{4,5},{5,4},{6,7},{7,6},{8,9},{9,8},{10,11... | collective-permute-start | bytes 1572872 | tf_op jit(solution)/shard_map/ppermute | solution.py:585
  136.4 13.8 %collective-permute-start.21 = (bf16[2,48,4096]{2,1,0:T(8,128)(2,1)S(1)}, bf16[2,48,4096]{2,1,0:T(8,128)(2,1)S(1)}, u32[]{:S(2)}, u32[]{:S(2)}) collective-permute-start(bf16[2,48,4096]{2,1,0:T(8,128)(2,1)S(1)} %get-tuple-element.65.stash.refs_0_), channel_id=1, source_target_pairs={{0,1},{1,0},{2,3},{3,2},{4,5},{5,4},{6,7},{7,6},{8,9},{9,8},{10,11... | collective-permute-start | bytes 2359304 | tf_op jit(solution)/shard_map/ppermute | solution.py:585
  142.1 10.5 %collective-permute-start.19 = (bf16[2,48,4096]{2,1,0:T(8,128)(2,1)S(1)}, bf16[2,48,4096]{2,1,0:T(8,128)(2,1)S(1)}, u32[]{:S(2)}, u32[]{:S(2)}) collective-permute-start(bf16[2,48,4096]{2,1,0:T(8,128)(2,1)S(1)} %backward_layers.2.rest_0_), channel_id=1, source_target_pairs={{0,1},{1,0},{2,3},{3,2},{4,5},{5,4},{6,7},{7,6},{8,9},{9,8},{10,11... | collective-permute-start | bytes 2359304 | tf_op jit(solution)/shard_map/ppermute | solution.py:585
  150.1 2.6 %collective-permute-start.20 = (bf16[2,32,4096]{2,1,0:T(8,128)(2,1)S(1)}, bf16[2,32,4096]{2,1,0:T(8,128)(2,1)S(1)}, u32[]{:S(2)}, u32[]{:S(2)}) collective-permute-start(bf16[2,32,4096]{2,1,0:T(8,128)(2,1)S(1)} %backward_layers.3.rest_1_), channel_id=1, source_target_pairs={{0,1},{1,0},{2,3},{3,2},{4,5},{5,4},{6,7},{7,6},{8,9},{9,8},{10,11... | collective-permute-start | bytes 1572872 | tf_op jit(solution)/shard_map/ppermute | solution.py:585
  156.5 14.4 %collective-permute-start.23 = (bf16[512,512]{1,0:T(8,128)(2,1)S(1)}, bf16[512,512]{1,0:T(8,128)(2,1)S(1)}, u32[]{:S(2)}, u32[]{:S(2)}) collective-permute-start(bf16[512,512]{1,0:T(8,128)(2,1)S(1)} %get-tuple-element.72), channel_id=1, source_target_pairs={{0,8},{8,0},{1,9},{9,1},{2,10},{10,2},{3,11},{11,3},{4,12},{12,4},... | collective-permute-start | bytes 1572872 | tf_op jit(solution)/shard_map/ppermute | solution.py:588
  171.0 14.5 %collective-permute-start.24 = (bf16[512,512]{1,0:T(8,128)(2,1)S(1)}, bf16[512,512]{1,0:T(8,128)(2,1)S(1)}, u32[]{:S(2)}, u32[]{:S(2)}) collective-permute-start(bf16[512,512]{1,0:T(8,128)(2,1)S(1)} %add_convert_fusion.3), channel_id=1, source_target_pairs={{0,2},{1,3},{2,6},{3,7},{6,4},{7,5},{4,0},{5,1},{8,10},{9,11},{10,... | collective-permute-start | bytes 1572872 | tf_op jit(solution)/shard_map/ppermute | solution.py:582
  171.8 14.9 %collective-permute-start.25 = (bf16[512,512]{1,0:T(8,128)(2,1)S(1)}, bf16[512,512]{1,0:T(8,128)(2,1)S(1)}, u32[]{:S(2)}, u32[]{:S(2)}) collective-permute-start(bf16[512,512]{1,0:T(8,128)(2,1)S(1)} %get-tuple-element.88), channel_id=1, source_target_pairs={{0,8},{8,0},{1,9},{9,1},{2,10},{10,2},{3,11},{11,3},{4,12},{12,4},... | collective-permute-start | bytes 1572872 | tf_op jit(solution)/shard_map/ppermute | solution.py:588
  172.4 25.5 %collective-permute-start.27 = (bf16[512,512]{1,0:T(8,128)(2,1)S(1)}, bf16[512,512]{1,0:T(8,128)(2,1)S(1)}, u32[]{:S(2)}, u32[]{:S(2)}) collective-permute-start(bf16[512,512]{1,0:T(8,128)(2,1)S(1)} %get-tuple-element.91), channel_id=1, source_target_pairs={{0,8},{8,0},{1,9},{9,1},{2,10},{10,2},{3,11},{11,3},{4,12},{12,4},... | collective-permute-start | bytes 1572872 | tf_op jit(solution)/shard_map/ppermute | solution.py:588
  186.9 12.4 %collective-permute-start.26 = (bf16[512,512]{1,0:T(8,128)(2,1)S(1)}, bf16[512,512]{1,0:T(8,128)(2,1)S(1)}, u32[]{:S(2)}, u32[]{:S(2)}) collective-permute-start(bf16[512,512]{1,0:T(8,128)(2,1)S(1)} %add_convert_fusion.2), channel_id=1, source_target_pairs={{0,2},{1,3},{2,6},{3,7},{6,4},{7,5},{4,0},{5,1},{8,10},{9,11},{10,... | collective-permute-start | bytes 1572872 | tf_op jit(solution)/shard_map/ppermute | solution.py:582
  190.3 17.2 %collective-permute-start.29 = (bf16[512,512]{1,0:T(8,128)(2,1)S(1)}, bf16[512,512]{1,0:T(8,128)(2,1)S(1)}, u32[]{:S(2)}, u32[]{:S(2)}) collective-permute-start(bf16[512,512]{1,0:T(8,128)(2,1)S(1)} %get-tuple-element.94), channel_id=1, source_target_pairs={{0,8},{8,0},{1,9},{9,1},{2,10},{10,2},{3,11},{11,3},{4,12},{12,4},... | collective-permute-start | bytes 1572872 | tf_op jit(solution)/shard_map/ppermute | solution.py:588
  199.5 11.5 %collective-permute-start.28 = (bf16[512,512]{1,0:T(8,128)(2,1)S(1)}, bf16[512,512]{1,0:T(8,128)(2,1)S(1)}, u32[]{:S(2)}, u32[]{:S(2)}) collective-permute-start(bf16[512,512]{1,0:T(8,128)(2,1)S(1)} %add_convert_fusion.1), channel_id=1, source_target_pairs={{0,2},{1,3},{2,6},{3,7},{6,4},{7,5},{4,0},{5,1},{8,10},{9,11},{10,... | collective-permute-start | bytes 1572872 | tf_op jit(solution)/shard_map/ppermute | solution.py:582
  (2 other events, 10.1 us)

commit v2 on v1

--- a/solution.py
+++ b/solution.py
@@ -109,16 +109,21 @@
             right = held[role, unit, row * BLK : (row + 2) * BLK]
             return jnp.dot(left, right, preferred_element_type=jnp.float32)
 
+        def columns_of(index):
+            inner, row = items[index]
+            line = role * units + step * per_step + inner
+            return [cols[line, row * slots + place] for place in range(2 * slots)]
+
         upcoming = product_of(0)
+        ahead = columns_of(0)
         for index, (inner, row) in enumerate(items):
-            product = upcoming
+            product, listed = upcoming, ahead
             if index + 1 < len(items):
                 upcoming = product_of(index + 1)
+                ahead = columns_of(index + 1)
             for which in range(2):
-                line = role * units + step * per_step + inner
-                flat = (row + which) * slots
                 for begin in range(0, slots, 4):
-                    at = [cols[line, flat + slot] for slot in range(begin, min(begin + 4, slots))]
+                    at = listed[which * slots + begin : which * slots + min(begin + 4, slots)]
                     added = []
                     for offset in range(len(at)):
                         slot = begin + offset
@@ -226,13 +231,13 @@
     over_pairs(feats, finish, 0)
 
 
-def block_grad_layer(layer, role, cols, flipped, lows, highs, out, chosen, units, rows, slots):
+def block_grad_layer(begin, role, cols, flipped, lows, highs, out, chosen, units, rows, slots):
     items = [(which, row) for which in range(len(chosen)) for row in range(rows)]
 
     def operands(index):
         which, row = items[index]
         picked = pick_columns(lows, highs, cols, role * units + chosen[which], row * slots, slots)
-        return flipped[layer, which * rows + row], picked
+        return flipped[begin + which * rows + row], picked
 
     upcoming = operands(0)
     for index, (which, row) in enumerate(items):
@@ -397,22 +402,25 @@
     )(*meta, stash, loss_grad, moved, *across)
 
 
-def join_tokens(sources, joined, arrived):
+def join_tokens(sources, joined, arrived, layer):
     copies = []
     begin = 0
     for index, source in enumerate(sources):
         span = pl.ds(begin, source.shape[1])
-        copies.append(pltpu.make_async_copy(source, joined.at[:, span], arrived.at[index]))
+        copies.append(
+            pltpu.make_async_copy(source.at[layer], joined.at[layer, span], arrived.at[layer, index])
+        )
         begin += source.shape[1]
     for copy in copies:
         copy.start()
-    for copy in copies:
-        copy.wait()
+    return copies
 
 
 def flip_kernel(rows, chosen, bases, *refs):
     *sources, flipped, joined, arrived = refs
-    join_tokens(sources, joined, arrived)
+    loads = [join_tokens(sources, joined, arrived, layer) for layer in range(2)]
+    for load in loads[0] + loads[1]:
+        load.wait()
 
     def run(layer, carry):
         hidden = joined.at[layer]
@@ -442,7 +450,7 @@
         out_shape=jax.ShapeDtypeStruct((2, chosen * rows, BLK, tokens), jnp.bfloat16),
         scratch_shapes=[
             pltpu.VMEM((2, tokens, feats), jnp.bfloat16),
-            pltpu.SemaphoreType.DMA((len(stashes),)),
+            pltpu.SemaphoreType.DMA((2, len(stashes))),
         ],
         compiler_params=pltpu.CompilerParams(vmem_limit_bytes=12 * MIB),
         cost_estimate=about(4),
@@ -450,54 +458,58 @@
     )(bases, *stashes)
 
 
-def block_grad_kernel(rows, slots, chosen, units, parts, cols, flags, turned, *rest):
+def block_grad_kernel(rows, slots, jobs, units, parts, cols, flags, turned, *rest):
     sources, rest = rest[:parts], rest[parts:]
-    outs = rest[: 2 * len(chosen)]
-    joined, flipped, lows, highs, arrived, fetched = rest[2 * len(chosen) :]
-    fetches = [
-        pltpu.make_async_copy(
-            turned.at[:, pl.ds(unit * rows, rows)],
-            flipped.at[:, pl.ds(which * rows, rows)],
-            fetched.at[which],
+    total = sum(len(chosen) for _, chosen in jobs)
+    outs = rest[:total]
+    joined, flipped, lows, highs, arrived, fetched = rest[total:]
+    layers = [jnp.abs(role - flags[0]) for role, _ in jobs]
+    fetches = []
+    begin = 0
+    for layer, (_, chosen) in zip(layers, jobs):
+        fetches.append(join_tokens(sources, joined, arrived, layer))
+        for which, unit in enumerate(chosen):
+            copy = pltpu.make_async_copy(
+                turned.at[layer, pl.ds(unit * rows, rows)],
+                flipped.at[pl.ds((begin + which) * rows, rows)],
+                fetched.at[begin + which],
+            )
+            copy.start()
+            fetches[-1].append(copy)
+        begin += len(chosen)
+    begin = 0
+    for turn, (role, chosen) in enumerate(jobs):
+        for fetch in fetches[turn]:
+            fetch.wait()
+        spread(joined.at[layers[turn]], lows, highs)
+        block_grad_layer(
+            begin * rows, role, cols, flipped, lows, highs, outs[begin:], chosen, units, rows, slots
         )
-        for which, unit in enumerate(chosen)
-    ]
-    for fetch in fetches:
-        fetch.start()
-    join_tokens(sources, joined, arrived)
-    for fetch in fetches:
-        fetch.wait()
-    for role in (1, 0):
-        layer = jnp.abs(role - flags[0])
-        spread(joined.at[layer], lows, highs)
-        block_grad_layer(
-            layer, role, cols, flipped, lows, highs, outs[role::2], chosen, units, rows, slots
-        )
-
-
-def block_grad_pass(turned, cotangents, meta, rows, slots, chosen):
+        begin += len(chosen)
+
+
+def block_grad_pass(turned, cotangents, meta, rows, slots, jobs):
     tokens = turned.shape[3]
     feats = cotangents[0].shape[2]
     blocks = feats // BLK
     cols, bases, flags = meta
+    total = sum(len(chosen) for _, chosen in jobs)
     out = jax.ShapeDtypeStruct((rows * BLK, slots * BLK), jnp.bfloat16)
     return pl.pallas_call(
-        functools.partial(
-            block_grad_kernel, rows, slots, tuple(chosen), bases.shape[0], len(cotangents)
-        ),
+        functools.partial(block_grad_kernel, rows, slots, jobs, bases.shape[0], len(cotangents)),
         in_specs=[IN_SMEM] * 2 + [IN_HBM] * (1 + len(cotangents)),
-        out_specs=[IN_VMEM] * (2 * len(chosen)),
-        out_shape=[out] * (2 * len(chosen)),
+        out_specs=[IN_VMEM] * total,
+        out_shape=[out] * total,
         scratch_shapes=[
             pltpu.VMEM((2, tokens, feats), jnp.bfloat16),
-            pltpu.VMEM((2, len(chosen) * rows, BLK, tokens), jnp.bfloat16),
+            pltpu.VMEM((total * rows, BLK, tokens), jnp.bfloat16),
             pltpu.VMEM((blocks, tokens, LANES), jnp.bfloat16),
             pltpu.VMEM((blocks, tokens, LANES), jnp.bfloat16),
-            pltpu.SemaphoreType.DMA((len(cotangents),)),
-            pltpu.SemaphoreType.DMA((len(chosen),)),
+            pltpu.SemaphoreType.DMA((2, len(cotangents))),
+            pltpu.SemaphoreType.DMA((total,)),
         ],
         compiler_params=pltpu.CompilerParams(vmem_limit_bytes=18 * MIB),
-        cost_estimate=about(4 + len(chosen)),
+        cost_estimate=about(3 + total // 2),
         name="block_grads",
     )(cols, flags, turned, *cotangents)
 
@@ -595,18 +607,20 @@
 
     owns, others, far_owns, far_others = [own], [], [], []
     for slot in range(places):
-        moving = {"other": partner(owns[slot]), "far_own": sibling(owns[slot])}
+        moving = {}
         if slot + 1 < places:
-            moving["own"] = ring(owns[slot])
+            moving["a_own"] = ring(owns[slot])
+        moving["b_other"] = partner(owns[slot])
         if slot:
-            moving["far_other"] = sibling(others[slot - 1])
+            moving["c_far_other"] = sibling(others[slot - 1])
+        moving["d_far_own"] = sibling(owns[slot])
         moving = lax.optimization_barrier(moving)
-        others.append(moving["other"])
-        far_owns.append(moving["far_own"])
+        others.append(moving["b_other"])
+        far_owns.append(moving["d_far_own"])
         if slot + 1 < places:
-            owns.append(moving["own"])
+            owns.append(moving["a_own"])
         if slot:
-            far_others.append(moving["far_other"])
+            far_others.append(moving["c_far_other"])
     far_others.append(sibling(others[-1]))
     own_units, other_units = owns + far_owns, others + far_others
     pieces = [piece for pair in zip(own_units, other_units) for piece in pair]
@@ -650,6 +664,7 @@
             ]
         moved = [hop(result[i], -1) for i in ways]
     flipped = flip_pass(stashes + [sibling(stash) for stash in stashes], bases, rows, places)
+    stashes[-1], flipped = lax.optimization_barrier((stashes[-1], flipped))
     cotangents = [
         backward_pass(stashes[i], loss_grads[i], moved[i], pieces, meta, rows, slots, 1) for i in ways
     ]
@@ -657,13 +672,17 @@
     order = list(range(1, places)) + [0]
 
     cotangents = cotangents + [sibling(part) for part in cotangents]
-    kept, outgoing = block_grad_pass(flipped, cotangents, meta, rows, slots, order[:1])
-    cotangents, tied = lax.optimization_barrier((cotangents, outgoing))
-    late = block_grad_pass(flipped, cotangents, meta, rows, slots, order[1:])
-    coming, late = lax.optimization_barrier((partner(tied), late))
+    early, late = order[:1], order[1:]
+    (outgoing,) = block_grad_pass(flipped, cotangents, meta, rows, slots, ((1, tuple(early)),))
+    cotangents, outgoing = lax.optimization_barrier((cotangents, outgoing))
+    jobs = ((1, tuple(late)), (0, tuple(order)))
+    grads = block_grad_pass(flipped, cotangents, meta, rows, slots, jobs)
+    coming, grads = lax.optimization_barrier((partner(outgoing), grads))
+    leaving, staying = grads[: len(late)], grads[len(late) :]
+    kept = staying[0]
     travelling = add_rounded(kept, coming)
     for index in range(places - 1):
-        kept, outgoing = late[2 * index], late[2 * index + 1]
+        kept, outgoing = staying[index + 1], leaving[index]
         passed, coming = lax.optimization_barrier((ring(travelling), partner(outgoing)))
         total = kept.astype(jnp.float32) + coming.astype(jnp.float32) + passed.astype(jnp.float32)
         travelling = total.astype(jnp.bfloat16)

time: 214 us -> 203 us (0.949)
  waiting for transfers between devices: 96.3 us -> 78.6 us
  starting transfers between devices: 26.6 us -> 32.1 us
    ppermute x8, waiting for transfers between devices: 66.5 us -> 35.9 us  [partner(): lax.ppermute(array, 'side', [(i, sides - 1 - i) for i in range(sides)])]
    ppermute x6, waiting for transfers between devices: 22.1 us -> 39.3 us  [ring(): return lax.ppermute(array, 'dp', hops)]
    ppermute x8, starting transfers between devices: 8.24 us -> 11.1 us  [partner(): lax.ppermute(array, 'side', [(i, sides - 1 - i) for i in range(sides)])]
    ppermute x12, waiting for transfers between devices: 4.93 us -> 2.73 us  [sibling(): return lax.ppermute(array, 'dp', [(i, i ^ 1) for i in range(dp_count)])]
  transfers between devices with their start and end apart: 30 -> 30, of which waited for: 19 -> 16; matrix products, arithmetic and copies ran while one was open for 2% -> 3% of each run, Pallas kernels for 29% -> 31%
where the time goes in v2:
time: 203 us; the launch traced here: 202 us
  waiting for transfers between devices  78.6 us (39%)
  Pallas kernels  77.1 us (38%)
  starting transfers between devices  32.1 us (16%)
  local copies, waits for them, and re-layouts  9.15 us (5%)
  other arithmetic  5.09 us (3%)
    pallas_call x4, Pallas kernels, forward_pass(): pl.pallas_call(functools.partial(forward_kernel, rows, slots, len(straigh...  53.5 us
    ppermute x6, waiting for transfers between devices, ring(): return lax.ppermute(array, 'dp', hops)  39.3 us
    ppermute x8, waiting for transfers between devices, partner(): lax.ppermute(array, 'side', [(i, sides - 1 - i) for i in range(sides)])  35.9 us
    ppermute x6, starting transfers between devices, ring(): return lax.ppermute(array, 'dp', hops)  11.4 us
    ppermute x8, starting transfers between devices, partner(): lax.ppermute(array, 'side', [(i, sides - 1 - i) for i in range(sides)])  11.1 us
    pallas_call x2, Pallas kernels, backward_pass(): pl.pallas_call(functools.partial(backward_kernel, rows, slots, len(across...  10.3 us
    pallas_call x2, Pallas kernels, block_grad_pass(): pl.pallas_call(functools.partial(block_grad_kernel, rows, slots, jobs, ba...  9.11 us
    ppermute x4, starting transfers between devices, hop(): return lax.ppermute(array, 'stage', route)  7.33 us
  transfers between devices with their start and end apart: 30, of which 16 were waited for; matrix products, arithmetic and copies ran while one was open for 3% of the time, Pallas kernels for 31%

profile of v2, /device:TPU:0, one launch (start us, length us, event | category | flops | bytes accessed | tf_op | source)
XLA Modules:
  0.0 202.3 jit_solution(6550680043931237242)
XLA Ops:
  0.9 2.1 %squeeze.6 = bf16[8,8,64,64]{3,2,1,0:T(8,128)(2,1)S(1)} reshape(bf16[1,8,8,4096]{3,2,1,0:T(8,128)(2,1)} %param.9) | data formatting | bytes 1048576 | tf_op jit(solution)/shard_map/squeeze | solution.py:603
  6.2 3.1 %collective-permute-start = (bf16[528,512]{1,0:T(8,128)(2,1)S(1)}, bf16[528,512]{1,0:T(8,128)(2,1)S(1)}, u32[]{:S(2)}, u32[]{:S(2)}) collective-permute-start(bf16[528,512]{1,0:T(8,128)(2,1)S(1)} %fusion.2.refs_0_.rest_2_.rest_3_.rest_0_), channel_id=1, source_target_pairs={{0,2},{1,3},{2,6},{3,7},{6,4},{7,5},{4,0},{5,1},{8,10},{9,11},{10,... | collective-permute-start | bytes 1622024 | tf_op jit(solution)/shard_map/ppermute | solution.py:594
  9.3 1.5 collective-permute-start.1
  12.0 10.5 %collective-permute-done.refs_1_.rest_4_.rest_5_.rest_2_ = bf16[528,512]{1,0:T(8,128)(2,1)S(1)} collective-permute-done((bf16[528,512]{1,0:T(8,128)(2,1)S(1)}, bf16[528,512]{1,0:T(8,128)(2,1)S(1)}, u32[]{:S(2)}, u32[]{:S(2)}) %collective-permute-start) | collective-permute-done | bytes 540704 | tf_op jit(solution)/shard_map/ppermute | solution.py:594
  23.0 2.6 %collective-permute-start.3 = (bf16[528,512]{1,0:T(8,128)(2,1)S(1)}, bf16[528,512]{1,0:T(8,128)(2,1)}, u32[]{:S(2)}, u32[]{:S(2)}) collective-permute-start(bf16[528,512]{1,0:T(8,128)(2,1)S(1)} %collective-permute-done.refs_1_.rest_4_.rest_5_.rest_2_), channel_id=1, source_target_pairs={{0,2},{1,3},{2,6},{3,7},{6,4},{7,5},{4,0},{5,1},{8,10},{9,11},{10,... | collective-permute-start | bytes 1622024 | tf_op jit(solution)/shard_map/ppermute | solution.py:594
  29.0 8.1 %collective-permute-done.3.refs_2_.rest_6_.rest_7_.rest_4_ = bf16[528,512]{1,0:T(8,128)(2,1)} collective-permute-done((bf16[528,512]{1,0:T(8,128)(2,1)S(1)}, bf16[528,512]{1,0:T(8,128)(2,1)}, u32[]{:S(2)}, u32[]{:S(2)}) %collective-permute-start.3) | collective-permute-done | bytes 540704 | tf_op jit(solution)/shard_map/ppermute | solution.py:594
  38.3 1.5 collective-permute-start.7
  39.8 1.5 collective-permute-start.8
  42.8 8.4 %collective-permute-done.7.refs_3_.rest_8_.rest_9_.rest_6_ = bf16[528,512]{1,0:T(8,128)(2,1)} collective-permute-done((bf16[528,512]{1,0:T(8,128)(2,1)}, bf16[528,512]{1,0:T(8,128)(2,1)}, u32[]{:S(2)}, u32[]{:S(2)}) %collective-permute-start.7) | collective-permute-done | bytes 540704 | tf_op jit(solution)/shard_map/ppermute | solution.py:594
  52.2 1.5 collective-permute-start.11
  54.3 8.9 %collective-permute-done.11.refs_11_.rest_9_.rest_10_.rest_7_ = bf16[528,512]{1,0:T(8,128)(2,1)S(1)} collective-permute-done((bf16[528,512]{1,0:T(8,128)(2,1)}, bf16[528,512]{1,0:T(8,128)(2,1)S(1)}, u32[]{:S(2)}, u32[]{:S(2)}) %collective-permute-start.11) | collective-permute-done | bytes 540704 | tf_op jit(solution)/shard_map/ppermute | solution.py:600
  66.2 10.0 %forward_layers.2 = bf16[48,4096]{1,0:T(8,128)(2,1)S(1)} custom-call(s32[16,128]{1,0:T(8,128)S(1)} %list_columns.1.cols, s32[8]{0:T(128)S(1)} %add_multiply_fusion.bases, s32[3]{0:T(128)S(1)} %pad_add_fusion.flags, bf16[48,4096]{1,0:T(8,128)(2,1)S(1)} %constant_dynamic-slice_fusion.1.rest_0_.rest_1_, ...), custom_call_target="tpu_custom_call" | custom-call | flops 8800000000 | bytes 1048576 | tf_op jit(solution)/shard_map/forward_layers/pallas_call | solution.py:344
  76.2 3.5 %collective-permute-start.15 = (bf16[48,4096]{1,0:T(8,128)(2,1)S(1)}, bf16[48,4096]{1,0:T(8,128)(2,1)S(1)}, u32[]{:S(2)}, u32[]{:S(2)}) collective-permute-start(bf16[48,4096]{1,0:T(8,128)(2,1)S(1)} %forward_layers.2), channel_id=1, source_target_pairs={{0,16},{1,17},{2,18},{3,19},{4,20},{5,21},{6,22},{7,23},{8,24},{9,... | collective-permute-start | bytes 1179656 | tf_op jit(solution)/shard_map/ppermute | solution.py:639
  79.7 8.7 %forward_layers.3 = bf16[32,4096]{1,0:T(8,128)(2,1)S(1)} custom-call(s32[16,128]{1,0:T(8,128)S(1)} %list_columns.1.cols, s32[8]{0:T(128)S(1)} %add_multiply_fusion.bases, s32[3]{0:T(128)S(1)} %pad_add_fusion.flags, bf16[32,4096]{1,0:T(8,128)(2,1)S(1)} %copy-done.1, bf16[32,4096]{1,0:T(8,128)(2,1)S(1)} %copy-done.1, ...), custom_call_target="tpu_custom_call" | custom-call | flops 8800000000 | bytes 1048576 | tf_op jit(solution)/shard_map/forward_layers/pallas_call | solution.py:344
  89.7 18.5 %turning_layers.2 = (bf16[2,48,4096]{2,1,0:T(8,128)(2,1)S(1)}, bf16[48,4096]{1,0:T(8,128)(2,1)S(1)}, bf16[48,4096]{1,0:T(8,128)(2,1)S(1)}) custom-call(s32[16,128]{1,0:T(8,128)S(1)} %list_columns.1.cols, s32[8]{0:T(128)S(1)} %add_multiply_fusion.bases, s32[3]{0:T(128)S(1)} %pad_add_fusion.flags, ...), custom_call_target="tpu_custom_call" | custom-call | flops 15399999488 | bytes 1048576 | tf_op jit(solution)/shard_map/turning_layers/pallas_call | solution.py:344
  109.6 16.4 %turning_layers.3 = (bf16[2,32,4096]{2,1,0:T(8,128)(2,1)S(1)}, bf16[32,4096]{1,0:T(8,128)(2,1)S(1)}, bf16[32,4096]{1,0:T(8,128)(2,1)S(1)}) custom-call(s32[16,128]{1,0:T(8,128)S(1)} %list_columns.1.cols, s32[8]{0:T(128)S(1)} %add_multiply_fusion.bases, s32[3]{0:T(128)S(1)} %pad_add_fusion.flags, bf16[32,4096]{1,0:T(8,128)(2,1)S(1)} %copy-done.1, ...), custom_call_target="tpu_custom_call" | custom-call | flops 15399999488 | bytes 1048576 | tf_op jit(solution)/shard_map/turning_layers/pallas_call | solution.py:344
  127.8 5.2 %backward_layers.2.rest_0_ = bf16[2,48,4096]{2,1,0:T(8,128)(2,1)S(1)} custom-call(s32[16,128]{1,0:T(8,128)S(1)} %list_columns.1.cols, s32[8]{0:T(128)S(1)} %add_multiply_fusion.bases, s32[3]{0:T(128)S(1)} %pad_add_fusion.flags, bf16[2,48,4096]{2,1,0:T(8,128)(2,1)S(1)} %get-tuple-element.67.stash.refs_0_, bf16[48,4096]{1,0:T(8,128)(2,1)S(1)} %get-tuple-element.68.loss_grad, ...), custom_call_target="tpu_custom_call" | custom-call | flops 4400000000 | bytes 1048576 | tf_op jit(solution)/shard_map/backward_layers/pallas_call | solution.py:387
  133.2 3.1 %flip_rows.1.turned = bf16[2,32,64,160]{3,2,1,0:T(8,128)(2,1)S(1)} custom-call(s32[8]{0:T(128)S(1)} %add_multiply_fusion.bases, bf16[2,48,4096]{2,1,0:T(8,128)(2,1)S(1)} %get-tuple-element.67.stash.refs_0_, bf16[2,32,4096]{2,1,0:T(8,128)(2,1)S(1)} %get-tuple-element.71.refs_1_.stash, bf16[2,48,4096]{2,1,0:T(8,128)(2,1)S(1)} %collective-permute-done.18.refs_2_, ...), custom_call_target="tpu_custom_call" | custom-call | flops 4400000000 | bytes 1048576 | tf_op jit(solution)/shard_map/flip_rows/pallas_call | solution.py:446
  137.0 5.1 %backward_layers.3.rest_1_ = bf16[2,32,4096]{2,1,0:T(8,128)(2,1)S(1)} custom-call(s32[16,128]{1,0:T(8,128)S(1)} %list_columns.1.cols, s32[8]{0:T(128)S(1)} %add_multiply_fusion.bases, s32[3]{0:T(128)S(1)} %pad_add_fusion.flags, bf16[2,32,4096]{2,1,0:T(8,128)(2,1)S(1)} %get-tuple-element.71.refs_1_.stash, bf16[32,4096]{1,0:T(8,128)(2,1)S(1)} %get-tuple-element.72.loss_grad, ...), custom_call_target="tpu_custom_call" | custom-call | flops 4400000000 | bytes 1048576 | tf_op jit(solution)/shard_map/backward_layers/pallas_call | solution.py:387
  142.1 1.9 collective-permute-done.22.rest_3_
  144.0 2.6 %block_grads.2 = bf16[512,512]{1,0:T(8,128)(2,1)S(1)} custom-call(s32[16,128]{1,0:T(8,128)S(1)} %list_columns.1.cols, s32[3]{0:T(128)S(1)} %pad_add_fusion.flags, bf16[2,32,64,160]{3,2,1,0:T(8,128)(2,1)S(1)} %flip_rows.1.turned, bf16[2,48,4096]{2,1,0:T(8,128)(2,1)S(1)} %backward_layers.2.rest_0_, bf16[2,32,4096]{2,1,0:T(8,128)(2,1)S(1)} %backward_layers.3.rest_1_, ...), custom_call_target="tpu_custom_call" | custom-call | flops 3300000000 | bytes 1048576 | tf_op jit(solution)/shard_map/block_grads/pallas_call | solution.py:498
  146.6 1.6 collective-permute-start.23
  148.2 6.5 %block_grads.3 = (bf16[512,512]{1,0:T(8,128)(2,1)S(1)}, bf16[512,512]{1,0:T(8,128)(2,1)S(1)}, bf16[512,512]{1,0:T(8,128)(2,1)S(1)}, bf16[512,512]{1,0:T(8,128)(2...) custom-call(s32[16,128]{1,0:T(8,128)S(1)} %list_columns.1.cols, ...), custom_call_target="tpu_custom_call" | custom-call | flops 6600000000 | bytes 1048576 | tf_op jit(solution)/shard_map/block_grads/pallas_call | solution.py:498
  154.7 6.0 %collective-permute-done.23 = bf16[512,512]{1,0:T(8,128)(2,1)S(1)} collective-permute-done((bf16[512,512]{1,0:T(8,128)(2,1)S(1)}, bf16[512,512]{1,0:T(8,128)(2,1)S(1)}, u32[]{:S(2)}, u32[]{:S(2)}) %collective-permute-start.23) | collective-permute-done | bytes 524320 | tf_op jit(solution)/shard_map/ppermute | solution.py:600
  160.8 1.6 collective-permute-start.24
  162.4 1.5 collective-permute-start.25
  164.4 10.5 %collective-permute-done.24 = bf16[512,512]{1,0:T(8,128)(2,1)S(1)} collective-permute-done((bf16[512,512]{1,0:T(8,128)(2,1)S(1)}, bf16[512,512]{1,0:T(8,128)(2,1)S(1)}, u32[]{:S(2)}, u32[]{:S(2)}) %collective-permute-start.24) | collective-permute-done | bytes 524320 | tf_op jit(solution)/shard_map/ppermute | solution.py:594
  174.9 2.3 %collective-permute-done.25 = bf16[512,512]{1,0:T(8,128)(2,1)S(1)} collective-permute-done((bf16[512,512]{1,0:T(8,128)(2,1)S(1)}, bf16[512,512]{1,0:T(8,128)(2,1)S(1)}, u32[]{:S(2)}, u32[]{:S(2)}) %collective-permute-start.25) | collective-permute-done | bytes 524320 | tf_op jit(solution)/shard_map/ppermute | solution.py:600
  178.8 1.5 collective-permute-start.29
  180.3 8.2 %collective-permute-done.27 = bf16[512,512]{1,0:T(8,128)(2,1)S(1)} collective-permute-done((bf16[512,512]{1,0:T(8,128)(2,1)S(1)}, bf16[512,512]{1,0:T(8,128)(2,1)S(1)}, u32[]{:S(2)}, u32[]{:S(2)}) %collective-permute-start.27) | collective-permute-done | bytes 524320 | tf_op jit(solution)/shard_map/ppermute | solution.py:600
  190.0 7.7 %collective-permute-done.29 = bf16[512,512]{1,0:T(8,128)(2,1)S(1)} collective-permute-done((bf16[512,512]{1,0:T(8,128)(2,1)S(1)}, bf16[512,512]{1,0:T(8,128)(2,1)S(1)}, u32[]{:S(2)}, u32[]{:S(2)}) %collective-permute-start.29) | collective-permute-done | bytes 524320 | tf_op jit(solution)/shard_map/ppermute | solution.py:600
  197.7 1.9 collective-permute-done.28
  (72 shorter events, 28.4 us)
Async XLA Ops:
  0.0 28.3 %copy-start = (bf16[2,80,4096]{2,1,0:T(8,128)(2,1)S(1)}, bf16[2,80,4096]{2,1,0:T(8,128)(2,1)}, u32[]{:S(2)}) copy-start(bf16[2,80,4096]{2,1,0:T(8,128)(2,1)} %param.7) | copy-start | bytes 3932164
  6.2 16.4 %collective-permute-start = (bf16[528,512]{1,0:T(8,128)(2,1)S(1)}, bf16[528,512]{1,0:T(8,128)(2,1)S(1)}, u32[]{:S(2)}, u32[]{:S(2)}) collective-permute-start(bf16[528,512]{1,0:T(8,128)(2,1)S(1)} %fusion.2.refs_0_.rest_2_.rest_3_.rest_0_), channel_id=1, source_target_pairs={{0,2},{1,3},{2,6},{3,7},{6,4},{7,5},{4,0},{5,1},{8,10},{9,11},{10,... | collective-permute-start | bytes 1622024 | tf_op jit(solution)/shard_map/ppermute | solution.py:594
  9.3 13.7 %collective-permute-start.1 = (bf16[528,512]{1,0:T(8,128)(2,1)S(1)}, bf16[528,512]{1,0:T(8,128)(2,1)S(1)}, u32[]{:S(2)}, u32[]{:S(2)}) collective-permute-start(bf16[528,512]{1,0:T(8,128)(2,1)S(1)} %fusion.2.refs_0_.rest_2_.rest_3_.rest_0_), channel_id=1, source_target_pairs={{0,8},{8,0},{1,9},{9,1},{2,10},{10,2},{3,11},{11,3},{4,12},{12,4},... | collective-permute-start | bytes 1622024 | tf_op jit(solution)/shard_map/ppermute | solution.py:600
  10.8 12.2 %collective-permute-start.2 = (bf16[528,512]{1,0:T(8,128)(2,1)S(1)}, bf16[528,512]{1,0:T(8,128)(2,1)S(1)}, u32[]{:S(2)}, u32[]{:S(2)}) collective-permute-start(bf16[528,512]{1,0:T(8,128)(2,1)S(1)} %fusion.2.refs_0_.rest_2_.rest_3_.rest_0_), channel_id=1, source_target_pairs={{0,1},{1,0},{2,3},{3,2},{4,5},{5,4},{6,7},{7,6},{8,9},{9,8},{10,11... | collective-permute-start | bytes 1622024 | tf_op jit(solution)/shard_map/ppermute | solution.py:597
  23.0 14.0 %collective-permute-start.3 = (bf16[528,512]{1,0:T(8,128)(2,1)S(1)}, bf16[528,512]{1,0:T(8,128)(2,1)}, u32[]{:S(2)}, u32[]{:S(2)}) collective-permute-start(bf16[528,512]{1,0:T(8,128)(2,1)S(1)} %collective-permute-done.refs_1_.rest_4_.rest_5_.rest_2_), channel_id=1, source_target_pairs={{0,2},{1,3},{2,6},{3,7},{6,4},{7,5},{4,0},{5,1},{8,10},{9,11},{10,... | collective-permute-start | bytes 1622024 | tf_op jit(solution)/shard_map/ppermute | solution.py:594
  25.6 12.7 %collective-permute-start.4 = (bf16[528,512]{1,0:T(8,128)(2,1)S(1)}, bf16[528,512]{1,0:T(8,128)(2,1)}, u32[]{:S(2)}, u32[]{:S(2)}) collective-permute-start(bf16[528,512]{1,0:T(8,128)(2,1)S(1)} %collective-permute-done.refs_1_.rest_4_.rest_5_.rest_2_), channel_id=1, source_target_pairs={{0,8},{8,0},{1,9},{9,1},{2,10},{10,2},{3,11},{11,3},{4,12},{12,4},... | collective-permute-start | bytes 1622024 | tf_op jit(solution)/shard_map/ppermute | solution.py:600
  27.1 11.2 %collective-permute-start.6 = (bf16[528,512]{1,0:T(8,128)(2,1)S(1)}, bf16[528,512]{1,0:T(8,128)(2,1)}, u32[]{:S(2)}, u32[]{:S(2)}) collective-permute-start(bf16[528,512]{1,0:T(8,128)(2,1)S(1)} %collective-permute-done.refs_1_.rest_4_.rest_5_.rest_2_), channel_id=1, source_target_pairs={{0,1},{1,0},{2,3},{3,2},{4,5},{5,4},{6,7},{7,6},{8,9},{9,8},{10,11... | collective-permute-start | bytes 1622024 | tf_op jit(solution)/shard_map/ppermute | solution.py:597
  27.1 11.2 %collective-permute-start.5 = (bf16[528,512]{1,0:T(8,128)(2,1)S(1)}, bf16[528,512]{1,0:T(8,128)(2,1)}, u32[]{:S(2)}, u32[]{:S(2)}) collective-permute-start(bf16[528,512]{1,0:T(8,128)(2,1)S(1)} %collective-permute-done.1.refs_8_.rest_3_.rest_4_.rest_1_), channel_id=1, source_target_pairs={{0,1},{1,0},{2,3},{3,2},{4,5},{5,4},{6,7},{7,6},{8,9},{9,8},{10,11... | collective-permute-start | bytes 1622024 | tf_op jit(solution)/shard_map/ppermute | solution.py:597
  38.3 12.8 %collective-permute-start.7 = (bf16[528,512]{1,0:T(8,128)(2,1)}, bf16[528,512]{1,0:T(8,128)(2,1)}, u32[]{:S(2)}, u32[]{:S(2)}) collective-permute-start(bf16[528,512]{1,0:T(8,128)(2,1)} %collective-permute-done.3.refs_2_.rest_6_.rest_7_.rest_4_), channel_id=1, source_target_pairs={{0,2},{1,3},{2,6},{3,7},{6,4},{7,5},{4,0},{5,1},{8,10},{9,11},{10,... | collective-permute-start | bytes 1622024 | tf_op jit(solution)/shard_map/ppermute | solution.py:594
  39.8 12.4 %collective-permute-start.8 = (bf16[528,512]{1,0:T(8,128)(2,1)}, bf16[528,512]{1,0:T(8,128)(2,1)}, u32[]{:S(2)}, u32[]{:S(2)}) collective-permute-start(bf16[528,512]{1,0:T(8,128)(2,1)} %collective-permute-done.3.refs_2_.rest_6_.rest_7_.rest_4_), channel_id=1, source_target_pairs={{0,8},{8,0},{1,9},{9,1},{2,10},{10,2},{3,11},{11,3},{4,12},{12,4},... | collective-permute-start | bytes 1622024 | tf_op jit(solution)/shard_map/ppermute | solution.py:600
  41.3 10.9 %collective-permute-start.10 = (bf16[528,512]{1,0:T(8,128)(2,1)}, bf16[528,512]{1,0:T(8,128)(2,1)}, u32[]{:S(2)}, u32[]{:S(2)}) collective-permute-start(bf16[528,512]{1,0:T(8,128)(2,1)} %collective-permute-done.3.refs_2_.rest_6_.rest_7_.rest_4_), channel_id=1, source_target_pairs={{0,1},{1,0},{2,3},{3,2},{4,5},{5,4},{6,7},{7,6},{8,9},{9,8},{10,11... | collective-permute-start | bytes 1622024 | tf_op jit(solution)/shard_map/ppermute | solution.py:597
  41.3 10.9 %collective-permute-start.9 = (bf16[528,512]{1,0:T(8,128)(2,1)}, bf16[528,512]{1,0:T(8,128)(2,1)}, u32[]{:S(2)}, u32[]{:S(2)}) collective-permute-start(bf16[528,512]{1,0:T(8,128)(2,1)} %collective-permute-done.4.refs_9_.rest_5_.rest_6_.rest_3_), channel_id=1, source_target_pairs={{0,1},{1,0},{2,3},{3,2},{4,5},{5,4},{6,7},{7,6},{8,9},{9,8},{10,11... | collective-permute-start | bytes 1622024 | tf_op jit(solution)/shard_map/ppermute | solution.py:597
  52.2 11.0 %collective-permute-start.11 = (bf16[528,512]{1,0:T(8,128)(2,1)}, bf16[528,512]{1,0:T(8,128)(2,1)S(1)}, u32[]{:S(2)}, u32[]{:S(2)}) collective-permute-start(bf16[528,512]{1,0:T(8,128)(2,1)} %collective-permute-done.7.refs_3_.rest_8_.rest_9_.rest_6_), channel_id=1, source_target_pairs={{0,8},{8,0},{1,9},{9,1},{2,10},{10,2},{3,11},{11,3},{4,12},{12,4},... | collective-permute-start | bytes 1622024 | tf_op jit(solution)/shard_map/ppermute | solution.py:600
  53.7 9.5 %collective-permute-start.13 = (bf16[528,512]{1,0:T(8,128)(2,1)}, bf16[528,512]{1,0:T(8,128)(2,1)S(1)}, u32[]{:S(2)}, u32[]{:S(2)}) collective-permute-start(bf16[528,512]{1,0:T(8,128)(2,1)} %collective-permute-done.7.refs_3_.rest_8_.rest_9_.rest_6_), channel_id=1, source_target_pairs={{0,1},{1,0},{2,3},{3,2},{4,5},{5,4},{6,7},{7,6},{8,9},{9,8},{10,11... | collective-permute-start | bytes 1622024 | tf_op jit(solution)/shard_map/ppermute | solution.py:597
  53.7 9.5 %collective-permute-start.12 = (bf16[528,512]{1,0:T(8,128)(2,1)}, bf16[528,512]{1,0:T(8,128)(2,1)S(1)}, u32[]{:S(2)}, u32[]{:S(2)}) collective-permute-start(bf16[528,512]{1,0:T(8,128)(2,1)} %collective-permute-done.8.refs_10_.rest_7_.rest_8_.rest_5_), channel_id=1, source_target_pairs={{0,1},{1,0},{2,3},{3,2},{4,5},{5,4},{6,7},{7,6},{8,9},{9,8},{10,11... | collective-permute-start | bytes 1622024 | tf_op jit(solution)/shard_map/ppermute | solution.py:597
  63.3 1.9 collective-permute-start.14
  66.2 13.5 %copy-start.1 = (bf16[32,4096]{1,0:T(8,128)(2,1)S(1)}, bf16[32,4096]{1,0:T(8,128)(2,1)}, u32[]{:S(2)}) copy-start(bf16[32,4096]{1,0:T(8,128)(2,1)} %constant_dynamic-slice_fusion.3.rest_0_.rest_1_) | copy-start | bytes 786436
  76.2 13.5 %collective-permute-start.15 = (bf16[48,4096]{1,0:T(8,128)(2,1)S(1)}, bf16[48,4096]{1,0:T(8,128)(2,1)S(1)}, u32[]{:S(2)}, u32[]{:S(2)}) collective-permute-start(bf16[48,4096]{1,0:T(8,128)(2,1)S(1)} %forward_layers.2), channel_id=1, source_target_pairs={{0,16},{1,17},{2,18},{3,19},{4,20},{5,21},{6,22},{7,23},{8,24},{9,... | collective-permute-start | bytes 1179656 | tf_op jit(solution)/shard_map/ppermute | solution.py:639
  88.4 21.2 %collective-permute-start.17 = (bf16[32,4096]{1,0:T(8,128)(2,1)S(1)}, bf16[32,4096]{1,0:T(8,128)(2,1)S(1)}, u32[]{:S(2)}, u32[]{:S(2)}) collective-permute-start(bf16[32,4096]{1,0:T(8,128)(2,1)S(1)} %forward_layers.3), channel_id=1, source_target_pairs={{0,16},{1,17},{2,18},{3,19},{4,20},{5,21},{6,22},{7,23},{8,24},{9,... | collective-permute-start | bytes 786440 | tf_op jit(solution)/shard_map/ppermute | solution.py:639
  108.2 19.6 %collective-permute-start.16 = (bf16[48,4096]{1,0:T(8,128)(2,1)S(1)}, bf16[48,4096]{1,0:T(8,128)(2,1)S(1)}, u32[]{:S(2)}, u32[]{:S(2)}) collective-permute-start(bf16[48,4096]{1,0:T(8,128)(2,1)S(1)} %get-tuple-element.69), channel_id=1, source_target_pairs={{16,0},{17,1},{18,2},{19,3},{20,4},{21,5},{22,6},{23,7},{24,8},{25... | collective-permute-start | bytes 1179656 | tf_op jit(solution)/shard_map/ppermute | solution.py:639
  109.5 23.7 %collective-permute-start.18 = (bf16[2,48,4096]{2,1,0:T(8,128)(2,1)S(1)}, bf16[2,48,4096]{2,1,0:T(8,128)(2,1)S(1)}, u32[]{:S(2)}, u32[]{:S(2)}) collective-permute-start(bf16[2,48,4096]{2,1,0:T(8,128)(2,1)S(1)} %get-tuple-element.67.stash.refs_0_), channel_id=1, source_target_pairs={{0,1},{1,0},{2,3},{3,2},{4,5},{5,4},{6,7},{7,6},{8,9},{9,8},{10,11... | collective-permute-start | bytes 2359304 | tf_op jit(solution)/shard_map/ppermute | solution.py:597
  126.0 7.2 %collective-permute-start.19 = (bf16[2,32,4096]{2,1,0:T(8,128)(2,1)S(1)}, bf16[2,32,4096]{2,1,0:T(8,128)(2,1)S(1)}, u32[]{:S(2)}, u32[]{:S(2)}) collective-permute-start(bf16[2,32,4096]{2,1,0:T(8,128)(2,1)S(1)} %get-tuple-element.71.refs_1_.stash), channel_id=1, source_target_pairs={{0,1},{1,0},{2,3},{3,2},{4,5},{5,4},{6,7},{7,6},{8,9},{9,8},{10,11... | collective-permute-start | bytes 1572872 | tf_op jit(solution)/shard_map/ppermute | solution.py:597
  126.5 10.4 %collective-permute-start.20 = (bf16[32,4096]{1,0:T(8,128)(2,1)S(1)}, bf16[32,4096]{1,0:T(8,128)(2,1)S(1)}, u32[]{:S(2)}, u32[]{:S(2)}) collective-permute-start(bf16[32,4096]{1,0:T(8,128)(2,1)S(1)} %get-tuple-element.73), channel_id=1, source_target_pairs={{16,0},{17,1},{18,2},{19,3},{20,4},{21,5},{22,6},{23,7},{24,8},{25... | collective-permute-start | bytes 786440 | tf_op jit(solution)/shard_map/ppermute | solution.py:639
  133.0 9.1 %collective-permute-start.21 = (bf16[2,48,4096]{2,1,0:T(8,128)(2,1)S(1)}, bf16[2,48,4096]{2,1,0:T(8,128)(2,1)S(1)}, u32[]{:S(2)}, u32[]{:S(2)}) collective-permute-start(bf16[2,48,4096]{2,1,0:T(8,128)(2,1)S(1)} %backward_layers.2.rest_0_), channel_id=1, source_target_pairs={{0,1},{1,0},{2,3},{3,2},{4,5},{5,4},{6,7},{7,6},{8,9},{9,8},{10,11... | collective-permute-start | bytes 2359304 | tf_op jit(solution)/shard_map/ppermute | solution.py:597
  142.0 2.0 collective-permute-start.22
  146.6 14.0 %collective-permute-start.23 = (bf16[512,512]{1,0:T(8,128)(2,1)S(1)}, bf16[512,512]{1,0:T(8,128)(2,1)S(1)}, u32[]{:S(2)}, u32[]{:S(2)}) collective-permute-start(bf16[512,512]{1,0:T(8,128)(2,1)S(1)} %block_grads.2), channel_id=1, source_target_pairs={{0,8},{8,0},{1,9},{9,1},{2,10},{10,2},{3,11},{11,3},{4,12},{12,4},... | collective-permute-start | bytes 1572872 | tf_op jit(solution)/shard_map/ppermute | solution.py:600
  160.8 14.1 %collective-permute-start.24 = (bf16[512,512]{1,0:T(8,128)(2,1)S(1)}, bf16[512,512]{1,0:T(8,128)(2,1)S(1)}, u32[]{:S(2)}, u32[]{:S(2)}) collective-permute-start(bf16[512,512]{1,0:T(8,128)(2,1)S(1)} %add_convert_fusion.3), channel_id=1, source_target_pairs={{0,2},{1,3},{2,6},{3,7},{6,4},{7,5},{4,0},{5,1},{8,10},{9,11},{10,... | collective-permute-start | bytes 1572872 | tf_op jit(solution)/shard_map/ppermute | solution.py:594
  162.4 14.9 %collective-permute-start.25 = (bf16[512,512]{1,0:T(8,128)(2,1)S(1)}, bf16[512,512]{1,0:T(8,128)(2,1)S(1)}, u32[]{:S(2)}, u32[]{:S(2)}) collective-permute-start(bf16[512,512]{1,0:T(8,128)(2,1)S(1)} %get-tuple-element.92), channel_id=1, source_target_pairs={{0,8},{8,0},{1,9},{9,1},{2,10},{10,2},{3,11},{11,3},{4,12},{12,4},... | collective-permute-start | bytes 1572872 | tf_op jit(solution)/shard_map/ppermute | solution.py:600
  163.8 24.6 %collective-permute-start.27 = (bf16[512,512]{1,0:T(8,128)(2,1)S(1)}, bf16[512,512]{1,0:T(8,128)(2,1)S(1)}, u32[]{:S(2)}, u32[]{:S(2)}) collective-permute-start(bf16[512,512]{1,0:T(8,128)(2,1)S(1)} %get-tuple-element.95), channel_id=1, source_target_pairs={{0,8},{8,0},{1,9},{9,1},{2,10},{10,2},{3,11},{11,3},{4,12},{12,4},... | collective-permute-start | bytes 1572872 | tf_op jit(solution)/shard_map/ppermute | solution.py:600
  177.4 11.0 %collective-permute-start.26 = (bf16[512,512]{1,0:T(8,128)(2,1)S(1)}, bf16[512,512]{1,0:T(8,128)(2,1)S(1)}, u32[]{:S(2)}, u32[]{:S(2)}) collective-permute-start(bf16[512,512]{1,0:T(8,128)(2,1)S(1)} %add_convert_fusion.2), channel_id=1, source_target_pairs={{0,2},{1,3},{2,6},{3,7},{6,4},{7,5},{4,0},{5,1},{8,10},{9,11},{10,... | collective-permute-start | bytes 1572872 | tf_op jit(solution)/shard_map/ppermute | solution.py:594
  178.8 18.9 %collective-permute-start.29 = (bf16[512,512]{1,0:T(8,128)(2,1)S(1)}, bf16[512,512]{1,0:T(8,128)(2,1)S(1)}, u32[]{:S(2)}, u32[]{:S(2)}) collective-permute-start(bf16[512,512]{1,0:T(8,128)(2,1)S(1)} %get-tuple-element.98), channel_id=1, source_target_pairs={{0,8},{8,0},{1,9},{9,1},{2,10},{10,2},{3,11},{11,3},{4,12},{12,4},... | collective-permute-start | bytes 1572872 | tf_op jit(solution)/shard_map/ppermute | solution.py:600
  188.7 10.9 %collective-permute-start.28 = (bf16[512,512]{1,0:T(8,128)(2,1)S(1)}, bf16[512,512]{1,0:T(8,128)(2,1)S(1)}, u32[]{:S(2)}, u32[]{:S(2)}) collective-permute-start(bf16[512,512]{1,0:T(8,128)(2,1)S(1)} %add_convert_fusion.1), channel_id=1, source_target_pairs={{0,2},{1,3},{2,6},{3,7},{6,4},{7,5},{4,0},{5,1},{8,10},{9,11},{10,... | collective-permute-start | bytes 1572872 | tf_op jit(solution)/shard_map/ppermute | solution.py:594
  (2 other events, 10.0 us)

commit v3 on v2

--- a/solution.py
+++ b/solution.py
@@ -56,26 +56,30 @@
     return lax.rsqrt(jnp.sum(total, axis=-1, keepdims=True) / feats + EPSILON)
 
 
-def start_loads(pieces, held, arrived, roles):
-    units = held.shape[1]
+def start_loads(pieces, held, arrived, roles, layout):
     for role in roles:
-        for unit in range(units):
-            pltpu.make_async_copy(
-                pieces[2 * unit + role], held.at[role, unit], arrived.at[role, unit]
-            ).start()
-
-
-def start_loads_in_order(side, pieces, held, arrived, layers):
+        for unit, parts in enumerate(layout[role]):
+            for index, begin in parts:
+                piece = pieces[index]
+                pltpu.make_async_copy(
+                    piece,
+                    held.at[role, unit, pl.ds(begin, piece.shape[0])],
+                    arrived.at[role, unit],
+                ).start()
+
+
+def start_loads_in_order(side, pieces, held, arrived, layers, layout):
     for value in range(2):
         pl.when(side == value)(
             functools.partial(
-                start_loads, pieces, held, arrived, [abs(layer - value) for layer in layers]
+                start_loads, pieces, held, arrived, [abs(layer - value) for layer in layers], layout
             )
         )
 
 
-def wait_load(pieces, held, arrived, role, unit):
-    pltpu.make_async_copy(pieces[0], held.at[role, unit], arrived.at[role, unit]).wait()
+def wait_load(held, arrived, role, unit):
+    whole = held.at[role, unit]
+    pltpu.make_async_copy(whole, whole, arrived.at[role, unit]).wait()
 
 
 def forward_layer(role, wait, cols, bases, current, held, parts, sums, rows, slots):
@@ -244,8 +248,11 @@
         left, right = upcoming
         if index + 1 < len(items):
             upcoming = operands(index + 1)
-        result = jnp.dot(left, right, preferred_element_type=jnp.float32)
-        out[which][row * BLK : (row + 1) * BLK] = result.astype(jnp.bfloat16)
+        result = jnp.dot(left, right, preferred_element_type=jnp.float32).astype(jnp.bfloat16)
+        target = out[which]
+        if isinstance(target, tuple):
+            target, row = target[row // (rows // 2)], row % (rows // 2)
+        target[row * BLK : (row + 1) * BLK] = result
 
 
 def choose(flag, first, second, target):
@@ -258,7 +265,7 @@
         target[...] = second[...]
 
 
-def forward_kernel(rows, slots, count, scale, cols, bases, flags, *rest):
+def forward_kernel(rows, slots, count, layout, scale, cols, bases, flags, *rest):
     turning = scale is not None
     start, moved = rest[:2]
     rest = rest[2:]
@@ -269,9 +276,9 @@
         stash, loss_grad, final, held, parts, sums, arrived, lows, highs, back = rest
     else:
         final, held, parts, sums, arrived = rest
-    start_loads_in_order(flags[0], straight, held, arrived, (0, 1))
+    start_loads_in_order(flags[0], straight, held, arrived, (0, 1), layout)
     choose(flags[1], start, moved, final)
-    wait = functools.partial(wait_load, straight, held, arrived)
+    wait = functools.partial(wait_load, held, arrived)
 
     def run_forward(layer, carry):
         if turning:
@@ -314,16 +321,18 @@
     return jax.ShapeDtypeStruct((tokens, feats), jnp.bfloat16)
 
 
-def unit_scratch(pieces):
-    units = len(pieces) // 2
-    return [pltpu.VMEM((2, units) + pieces[0].shape, jnp.bfloat16), pltpu.SemaphoreType.DMA((2, units))]
-
-
-def forward_pass(start, moved, goal, scale, straight, meta, rows, slots):
+def unit_scratch(layout, rows, slots):
+    units = len(layout[0])
+    shape = (2, units, rows * BLK + TAIL, slots * BLK)
+    return [pltpu.VMEM(shape, jnp.bfloat16), pltpu.SemaphoreType.DMA((2, units))]
+
+
+def forward_pass(start, moved, goal, scale, weights, meta, rows, slots):
+    straight, layout = weights
     tokens, feats = start.shape
     blocks = feats // BLK
     stack = jax.ShapeDtypeStruct((2, tokens, feats), jnp.bfloat16)
-    held, arrived = unit_scratch(straight)
+    held, arrived = unit_scratch(layout, rows, slots)
     scratch = [
         held,
         pltpu.VMEM((blocks, tokens, LANES), jnp.bfloat16),
@@ -342,7 +351,9 @@
             pltpu.VMEM((blocks // 2, tokens, LANES), jnp.float32),
         ]
     return pl.pallas_call(
-        functools.partial(forward_kernel, rows, slots, len(straight), None if goal is None else scale),
+        functools.partial(
+            forward_kernel, rows, slots, len(straight), layout, None if goal is None else scale
+        ),
         in_specs=[IN_SMEM] * 3 + [IN_VMEM] * len(ins) + [IN_HBM] * len(pieces),
         out_specs=[IN_VMEM] * len(outs),
         out_shape=outs,
@@ -353,16 +364,17 @@
     )(*meta, *ins, *pieces)
 
 
-def backward_kernel(rows, slots, count, depth, cols, bases, flags, stash, loss_grad, moved, *rest):
+def backward_kernel(rows, slots, count, layout, depth, cols, bases, flags, stash, loss_grad, moved, *rest):
     across, rest = rest[:count], rest[count:]
     outs, crossed, lows, highs, back, landed = rest
     if depth == 1:
         first, second = outs.at[1], outs.at[0]
     else:
         first = second = outs
-    start_loads_in_order(flags[0], across, crossed, landed, (1,) if depth == 1 else (1, 0))
+    order = (1,) if depth == 1 else (1, 0)
+    start_loads_in_order(flags[0], across, crossed, landed, order, layout)
     choose(flags[2], loss_grad, moved, first)
-    wait = functools.partial(wait_load, across, crossed, landed)
+    wait = functools.partial(wait_load, crossed, landed)
 
     def run_back(layer):
         spread(first, lows, highs)
@@ -376,16 +388,17 @@
         run_back(0)
 
 
-def backward_pass(stash, loss_grad, moved, across, meta, rows, slots, depth):
+def backward_pass(stash, loss_grad, moved, weights, meta, rows, slots, depth):
+    across, layout = weights
     _, tokens, feats = stash.shape
     blocks = feats // BLK
-    crossed, landed = unit_scratch(across)
+    crossed, landed = unit_scratch(layout, rows, slots)
     if depth == 1:
         out = jax.ShapeDtypeStruct((2, tokens, feats), jnp.bfloat16)
     else:
         out = state_of(tokens, feats)
     return pl.pallas_call(
-        functools.partial(backward_kernel, rows, slots, len(across), depth),
+        functools.partial(backward_kernel, rows, slots, len(across), layout, depth),
         in_specs=[IN_SMEM] * 3 + [IN_VMEM] * 3 + [IN_HBM] * len(across),
         out_specs=IN_VMEM,
         out_shape=out,
@@ -458,11 +471,11 @@
     )(bases, *stashes)
 
 
-def block_grad_kernel(rows, slots, jobs, units, parts, cols, flags, turned, *rest):
+def block_grad_kernel(rows, slots, jobs, halved, units, parts, cols, flags, turned, *rest):
     sources, rest = rest[:parts], rest[parts:]
     total = sum(len(chosen) for _, chosen in jobs)
-    outs = rest[:total]
-    joined, flipped, lows, highs, arrived, fetched = rest[total:]
+    outs = [tuple(rest[:2])] if halved else rest[:total]
+    joined, flipped, lows, highs, arrived, fetched = rest[-6:]
     layers = [jnp.abs(role - flags[0]) for role, _ in jobs]
     fetches = []
     begin = 0
@@ -488,18 +501,21 @@
         begin += len(chosen)
 
 
-def block_grad_pass(turned, cotangents, meta, rows, slots, jobs):
+def block_grad_pass(turned, cotangents, meta, rows, slots, jobs, halved=False):
     tokens = turned.shape[3]
     feats = cotangents[0].shape[2]
     blocks = feats // BLK
     cols, bases, flags = meta
     total = sum(len(chosen) for _, chosen in jobs)
-    out = jax.ShapeDtypeStruct((rows * BLK, slots * BLK), jnp.bfloat16)
+    tall = rows // 2 * BLK if halved else rows * BLK
+    outs = [jax.ShapeDtypeStruct((tall, slots * BLK), jnp.bfloat16)] * (2 if halved else total)
     return pl.pallas_call(
-        functools.partial(block_grad_kernel, rows, slots, jobs, bases.shape[0], len(cotangents)),
+        functools.partial(
+            block_grad_kernel, rows, slots, jobs, halved, bases.shape[0], len(cotangents)
+        ),
         in_specs=[IN_SMEM] * 2 + [IN_HBM] * (1 + len(cotangents)),
-        out_specs=[IN_VMEM] * total,
-        out_shape=[out] * total,
+        out_specs=[IN_VMEM] * len(outs),
+        out_shape=outs,
         scratch_shapes=[
             pltpu.VMEM((2, tokens, feats), jnp.bfloat16),
             pltpu.VMEM((total * rows, BLK, tokens), jnp.bfloat16),
@@ -514,26 +530,29 @@
     )(cols, flags, turned, *cotangents)
 
 
-def list_kernel(rows, pieces_count, *refs):
-    pieces, (listed, tails, arrived) = refs[:pieces_count], refs[pieces_count:]
-    copies = [
-        pltpu.make_async_copy(piece.at[pl.ds(rows * BLK, TAIL)], tails.at[i], arrived.at[i])
-        for i, piece in enumerate(pieces)
-    ]
+def list_kernel(tail_pieces, *refs):
+    pieces, (listed, tails, arrived) = refs[:-3], refs[-3:]
+    copies = []
+    for line, index in enumerate(tail_pieces):
+        piece = pieces[index]
+        last = piece.at[pl.ds(piece.shape[0] - TAIL, TAIL)]
+        copies.append(pltpu.make_async_copy(last, tails.at[line], arrived.at[line]))
     for copy in copies:
         copy.start()
-    for i, copy in enumerate(copies):
+    for line, copy in enumerate(copies):
         copy.wait()
-        line = tails[i].astype(jnp.float32)[:1, : listed.shape[1]]
-        listed[i : i + 1] = line.astype(jnp.int32)
-
-
-def list_pass(pieces, rows, slots):
-    count = len(pieces)
+        entry = tails[line].astype(jnp.float32)[:1, : listed.shape[1]]
+        listed[line : line + 1] = entry.astype(jnp.int32)
+
+
+def list_pass(weights, rows, slots):
+    pieces, layout = weights
+    tail_pieces = tuple(parts[-1][0] for role in range(2) for parts in layout[role])
+    count = len(tail_pieces)
     lanes = -(-rows * slots // LANES) * LANES
     return pl.pallas_call(
-        functools.partial(list_kernel, rows, count),
-        in_specs=[IN_HBM] * count,
+        functools.partial(list_kernel, tail_pieces),
+        in_specs=[IN_HBM] * len(pieces),
         out_specs=IN_VMEM,
         out_shape=jax.ShapeDtypeStruct((count, lanes), jnp.int32),
         scratch_shapes=[
@@ -599,32 +618,48 @@
     def partner(array):
         return lax.ppermute(array, "side", [(i, sides - 1 - i) for i in range(sides)])
 
-    live = jnp.arange(slots, dtype=jnp.int32)[None, :] < counts[0][:, None]
-    kept = jnp.where(live[:, :, None], blocks[0], jnp.zeros_like(blocks[0]))
+    slot_of = lax.broadcasted_iota(jnp.int32, (rows, BLK, slots * BLK), 2) // BLK
+    live = (slot_of < counts[0][:, None, None]).reshape(rows * BLK, slots * BLK)
     listed = columns[0].reshape(1, rows * slots).astype(jnp.bfloat16)
     tail = jnp.pad(listed, ((0, TAIL - 1), (0, slots * BLK - rows * slots)))
-    own = jnp.concatenate([to_rows(kept), tail], axis=0)
-
+    straight = to_rows(blocks[0])
+    own = jnp.concatenate([jnp.where(live, straight, jnp.zeros_like(straight)), tail], axis=0)
+
+    half = rows // 2 * BLK
     owns, others, far_owns, far_others = [own], [], [], []
     for slot in range(places):
+        last = slot + 1 == places
         moving = {}
-        if slot + 1 < places:
+        if not last:
             moving["a_own"] = ring(owns[slot])
-        moving["b_other"] = partner(owns[slot])
+            moving["b_other"] = [partner(owns[slot])]
+        elif slot:
+            moving["b_other"] = [ring(others[-1][0][:half]), partner(owns[slot][half:])]
+        else:
+            moving["b_other"] = [partner(owns[slot])]
         if slot:
-            moving["c_far_other"] = sibling(others[slot - 1])
+            moving["c_far_other"] = [sibling(part) for part in others[-1]]
         moving["d_far_own"] = sibling(owns[slot])
         moving = lax.optimization_barrier(moving)
         others.append(moving["b_other"])
         far_owns.append(moving["d_far_own"])
-        if slot + 1 < places:
+        if not last:
             owns.append(moving["a_own"])
         if slot:
             far_others.append(moving["c_far_other"])
-    far_others.append(sibling(others[-1]))
-    own_units, other_units = owns + far_owns, others + far_others
-    pieces = [piece for pair in zip(own_units, other_units) for piece in pair]
-    cols = list_pass(own_units + other_units, rows, slots)
+    far_others.append([sibling(part) for part in others[-1]])
+    pieces, layout = [], []
+    for units in ([[piece] for piece in owns + far_owns], others + far_others):
+        layout.append([])
+        for parts in units:
+            begin = 0
+            layout[-1].append([])
+            for part in parts:
+                layout[-1][-1].append((len(pieces), begin))
+                pieces.append(part)
+                begin += part.shape[0]
+    weights = (pieces, layout)
+    cols = list_pass(weights, rows, slots)
     turns = jnp.array(around, jnp.int32)[(rank - jnp.arange(places)) % places]
     bases = jnp.concatenate([turns * 2 + core, turns * 2 + 1 - core]).astype(jnp.int32) * rows
     flags = jnp.stack([side, stage == 0, stage == stages - 1]).astype(jnp.int32)
@@ -646,12 +681,12 @@
     moved = list(start)
     for step in range(stages - 1):
         final = [
-            forward_pass(start[i], moved[i], None, None, pieces, meta, rows, slots)[0]
+            forward_pass(start[i], moved[i], None, None, weights, meta, rows, slots)[0]
             for i in ways
         ]
         moved = [hop(final[i], 1) for i in ways]
     turned = [
-        forward_pass(start[i], moved[i], goal[i], loss_scale, pieces, meta, rows, slots)
+        forward_pass(start[i], moved[i], goal[i], loss_scale, weights, meta, rows, slots)
         for i in ways
     ]
     stashes, loss_grads, result = [list(column) for column in zip(*turned)]
@@ -659,35 +694,45 @@
     for step in range(stages - 1):
         if step:
             result = [
-                backward_pass(stashes[i], loss_grads[i], moved[i], pieces, meta, rows, slots, 2)
+                backward_pass(stashes[i], loss_grads[i], moved[i], weights, meta, rows, slots, 2)
                 for i in ways
             ]
         moved = [hop(result[i], -1) for i in ways]
     flipped = flip_pass(stashes + [sibling(stash) for stash in stashes], bases, rows, places)
     stashes[-1], flipped = lax.optimization_barrier((stashes[-1], flipped))
     cotangents = [
-        backward_pass(stashes[i], loss_grads[i], moved[i], pieces, meta, rows, slots, 1) for i in ways
+        backward_pass(stashes[i], loss_grads[i], moved[i], weights, meta, rows, slots, 1) for i in ways
     ]
 
     order = list(range(1, places)) + [0]
 
     cotangents = cotangents + [sibling(part) for part in cotangents]
     early, late = order[:1], order[1:]
-    (outgoing,) = block_grad_pass(flipped, cotangents, meta, rows, slots, ((1, tuple(early)),))
-    cotangents, outgoing = lax.optimization_barrier((cotangents, outgoing))
+    first = block_grad_pass(flipped, cotangents, meta, rows, slots, ((1, tuple(early)),), True)
+    cotangents, first = lax.optimization_barrier((cotangents, first))
     jobs = ((1, tuple(late)), (0, tuple(order)))
     grads = block_grad_pass(flipped, cotangents, meta, rows, slots, jobs)
-    coming, grads = lax.optimization_barrier((partner(outgoing), grads))
-    leaving, staying = grads[: len(late)], grads[len(late) :]
-    kept = staying[0]
-    travelling = add_rounded(kept, coming)
+    if places > 1:
+        moving = lax.optimization_barrier((ring(first[1]), partner(first[0]), grads))
+    else:
+        moving = lax.optimization_barrier((partner(first[1]), partner(first[0]), grads))
+    lower, upper, grads = moving
+    leaving, staying = list(grads[: len(late)]), grads[len(late) :]
+    if places > 1:
+        upper = jnp.concatenate([upper, jnp.zeros_like(lower)], axis=0)
+        travelling = add_rounded(staying[0], upper)
+        leaving[0] = add_rounded(leaving[0], jnp.concatenate([jnp.zeros_like(lower), lower], axis=0))
+    else:
+        travelling = add_rounded(staying[0], jnp.concatenate([upper, lower], axis=0))
     for index in range(places - 1):
         kept, outgoing = staying[index + 1], leaving[index]
-        passed, coming = lax.optimization_barrier((ring(travelling), partner(outgoing)))
+        passed, coming, leaving = lax.optimization_barrier(
+            (ring(travelling), partner(outgoing), leaving)
+        )
         total = kept.astype(jnp.float32) + coming.astype(jnp.float32) + passed.astype(jnp.float32)
         travelling = total.astype(jnp.bfloat16)
-    result = from_rows(travelling, slots)
-    return jnp.where(live[:, :, None], result, jnp.zeros_like(result))[None]
+    travelling = jnp.where(live, travelling, jnp.zeros_like(travelling))
+    return from_rows(travelling, slots)[None]
 
 
 def add_rounded(left, right):

time: 203 us -> 205 us (level)
  local copies, waits for them, and re-layouts: 9.15 us -> 18.6 us
  waiting for transfers between devices: 78.6 us -> 71.4 us
  starting transfers between devices: 32.1 us -> 34.7 us
  other arithmetic: 5.09 us -> 2.6 us
    ppermute x8, waiting for transfers between devices: 35.9 us -> 2.96 us  [partner(): lax.ppermute(array, 'side', [(i, sides - 1 - i) for i in range(sides)])]
    ppermute x6 -> x8, waiting for transfers between devices: 39.3 us -> 64.2 us  [ring(): return lax.ppermute(array, 'dp', hops)]
    unnamed x8 -> x38, local copies, waits for them, and re-layouts: 0.02 us -> 6.35 us
    another operation x0 -> x3, local copies, waits for them, and re-layouts: none -> 4.36 us  [the longest x2 2.75 us: to_rows(): split = blocks.reshape(rows, slots, BLK, BLK)]
    ppermute x6 -> x8, starting transfers between devices: 11.4 us -> 13.7 us  [ring(): return lax.ppermute(array, 'dp', hops)]
    squeeze x1 -> x0, local copies, waits for them, and re-layouts: 2.06 us -> none  [body(): kept = jnp.where(live[:, :, None], blocks[0], jnp.zeros_like(blocks[0]))]
  transfers between devices with their start and end apart: 30 -> 33, of which waited for: 16 -> 15; matrix products, arithmetic and copies ran while one was open for 3% -> 3% of each run, Pallas kernels for 31% -> 31%
where the time goes in v3:
time: 205 us
  Pallas kernels  77.2 us (38%)
  waiting for transfers between devices  71.4 us (35%)
  starting transfers between devices  34.7 us (17%)
  local copies, waits for them, and re-layouts  18.6 us (9%)
  other arithmetic  2.6 us (1%)
    ppermute x8, waiting for transfers between devices, ring(): return lax.ppermute(array, 'dp', hops)  64.2 us
    pallas_call x4, Pallas kernels, forward_pass(): pl.pallas_call(functools.partial(forward_kernel, rows, slots, len(straigh...  53.6 us
    ppermute x8, starting transfers between devices, ring(): return lax.ppermute(array, 'dp', hops)  13.7 us
    ppermute x8, starting transfers between devices, partner(): lax.ppermute(array, 'side', [(i, sides - 1 - i) for i in range(sides)])  10.7 us
    pallas_call x2, Pallas kernels, backward_pass(): pl.pallas_call(functools.partial(backward_kernel, rows, slots, len(across...  10.2 us
    pallas_call x2, Pallas kernels, block_grad_pass(): pl.pallas_call(functools.partial(block_grad_kernel, rows, slots, jobs, ha...  9.09 us
    ppermute x4, starting transfers between devices, hop(): return lax.ppermute(array, 'stage', route)  7.59 us
    unnamed x38, local copies, waits for them, and re-layouts  6.35 us
  transfers between devices with their start and end apart: 33, of which 15 were waited for; matrix products, arithmetic and copies ran while one was open for 3% of the time, Pallas kernels for 31%

profile of v3, /device:TPU:0, one launch (start us, length us, event | category | flops | bytes accessed | tf_op | source)
XLA Modules:
  0.0 204.8 jit_solution(3358895410305238161)
XLA Ops:
  0.9 2.1 %reshape_squeeze.4 = bf16[8,8,64,64]{3,2,1,0:T(8,128)(2,1)S(1)} reshape(bf16[1,8,8,4096]{3,2,1,0:T(8,128)(2,1)} %param.9) | data formatting | bytes 1048576 | tf_op jit(solution)/shard_map/reshape;squeeze | solution.py:570
  4.7 3.1 %collective-permute-start = (bf16[528,512]{1,0:T(8,128)(2,1)S(1)}, bf16[528,512]{1,0:T(8,128)(2,1)S(1)}, u32[]{:S(2)}, u32[]{:S(2)}) collective-permute-start(bf16[528,512]{1,0:T(8,128)(2,1)S(1)} %fusion.3.refs_0_.rest_2_.rest_3_.rest_0_), channel_id=1, source_target_pairs={{0,2},{1,3},{2,6},{3,7},{6,4},{7,5},{4,0},{5,1},{8,10},{9,11},{10,... | collective-permute-start | bytes 1622024 | tf_op jit(solution)/shard_map/ppermute | solution.py:613
  7.8 1.5 collective-permute-start.1
  9.3 11.8 %collective-permute-done.refs_1_.rest_3_.rest_4_.rest_1_ = bf16[528,512]{1,0:T(8,128)(2,1)S(1)} collective-permute-done((bf16[528,512]{1,0:T(8,128)(2,1)S(1)}, bf16[528,512]{1,0:T(8,128)(2,1)S(1)}, u32[]{:S(2)}, u32[]{:S(2)}) %collective-permute-start) | collective-permute-done | bytes 540704 | tf_op jit(solution)/shard_map/ppermute | solution.py:613
  21.5 2.6 %collective-permute-start.3 = (bf16[528,512]{1,0:T(8,128)(2,1)S(1)}, bf16[528,512]{1,0:T(8,128)(2,1)}, u32[]{:S(2)}, u32[]{:S(2)}) collective-permute-start(bf16[528,512]{1,0:T(8,128)(2,1)S(1)} %collective-permute-done.refs_1_.rest_3_.rest_4_.rest_1_), channel_id=1, source_target_pairs={{0,2},{1,3},{2,6},{3,7},{6,4},{7,5},{4,0},{5,1},{8,10},{9,11},{10,... | collective-permute-start | bytes 1622024 | tf_op jit(solution)/shard_map/ppermute | solution.py:613
  24.2 1.5 collective-permute-start.4
  28.3 7.4 %collective-permute-done.3.refs_2_.rest_4_.rest_5_.rest_2_ = bf16[528,512]{1,0:T(8,128)(2,1)} collective-permute-done((bf16[528,512]{1,0:T(8,128)(2,1)S(1)}, bf16[528,512]{1,0:T(8,128)(2,1)}, u32[]{:S(2)}, u32[]{:S(2)}) %collective-permute-start.3) | collective-permute-done | bytes 540704 | tf_op jit(solution)/shard_map/ppermute | solution.py:613
  36.8 1.6 collective-permute-start.7
  38.4 1.5 collective-permute-start.8
  41.0 1.8 constant_dynamic-slice_fusion.rest_2_
  42.8 6.9 %collective-permute-done.7.refs_3_.rest_5_.rest_6_.rest_3_ = bf16[528,512]{1,0:T(8,128)(2,1)S(1)} collective-permute-done((bf16[528,512]{1,0:T(8,128)(2,1)}, bf16[528,512]{1,0:T(8,128)(2,1)S(1)}, u32[]{:S(2)}, u32[]{:S(2)}) %collective-permute-start.7) | collective-permute-done | bytes 540704 | tf_op jit(solution)/shard_map/ppermute | solution.py:613
  53.1 1.5 collective-permute-start.11
  54.6 1.5 collective-permute-start.12
  56.1 1.7 constant_dynamic-slice_fusion.2.rest_2_
  57.8 4.6 %collective-permute-done.11.refs_11_.rest_13_.rest_14_.rest_11_ = bf16[256,512]{1,0:T(8,128)(2,1)} collective-permute-done((bf16[256,512]{1,0:T(8,128)(2,1)S(1)}, bf16[256,512]{1,0:T(8,128)(2,1)}, u32[]{:S(2)}, u32[]{:S(2)}) %collective-permute-start.11) | collective-permute-done | bytes 262176 | tf_op jit(solution)/shard_map/ppermute | solution.py:613
  71.3 10.0 %forward_layers.2 = bf16[48,4096]{1,0:T(8,128)(2,1)S(1)} custom-call(s32[16,128]{1,0:T(8,128)S(1)} %list_columns.1.cols, s32[8]{0:T(128)S(1)} %add_multiply_fusion.bases, s32[3]{0:T(128)S(1)} %pad_add_fusion.flags, bf16[48,4096]{1,0:T(8,128)(2,1)S(1)} %copy-done.13, bf16[48,4096]{1,0:T(8,128)(2,1)S(1)} %copy-done.13, ...), custom_call_target="tpu_custom_call" | custom-call | flops 8800000000 | bytes 1048576 | tf_op jit(solution)/shard_map/forward_layers/pallas_call | solution.py:353
  81.2 3.6 %collective-permute-start.17 = (bf16[48,4096]{1,0:T(8,128)(2,1)S(1)}, bf16[48,4096]{1,0:T(8,128)(2,1)S(1)}, u32[]{:S(2)}, u32[]{:S(2)}) collective-permute-start(bf16[48,4096]{1,0:T(8,128)(2,1)S(1)} %forward_layers.2), channel_id=1, source_target_pairs={{0,16},{1,17},{2,18},{3,19},{4,20},{5,21},{6,22},{7,23},{8,24},{9,... | collective-permute-start | bytes 1179656 | tf_op jit(solution)/shard_map/ppermute | solution.py:674
  84.8 8.7 %forward_layers.3 = bf16[32,4096]{1,0:T(8,128)(2,1)S(1)} custom-call(s32[16,128]{1,0:T(8,128)S(1)} %list_columns.1.cols, s32[8]{0:T(128)S(1)} %add_multiply_fusion.bases, s32[3]{0:T(128)S(1)} %pad_add_fusion.flags, bf16[32,4096]{1,0:T(8,128)(2,1)S(1)} %copy-done.15, bf16[32,4096]{1,0:T(8,128)(2,1)S(1)} %copy-done.15, ...), custom_call_target="tpu_custom_call" | custom-call | flops 8800000000 | bytes 1048576 | tf_op jit(solution)/shard_map/forward_layers/pallas_call | solution.py:353
  95.0 18.5 %turning_layers.2 = (bf16[2,48,4096]{2,1,0:T(8,128)(2,1)S(1)}, bf16[48,4096]{1,0:T(8,128)(2,1)S(1)}, bf16[48,4096]{1,0:T(8,128)(2,1)S(1)}) custom-call(s32[16,128]{1,0:T(8,128)S(1)} %list_columns.1.cols, s32[8]{0:T(128)S(1)} %add_multiply_fusion.bases, s32[3]{0:T(128)S(1)} %pad_add_fusion.flags, bf16[48,4096]{1,0:T(8,128)(2,1)S(1)} %copy-done.13, ...), custom_call_target="tpu_custom_call" | custom-call | flops 15399999488 | bytes 1048576 | tf_op jit(solution)/shard_map/turning_layers/pallas_call | solution.py:353
  114.9 16.4 %turning_layers.3 = (bf16[2,32,4096]{2,1,0:T(8,128)(2,1)S(1)}, bf16[32,4096]{1,0:T(8,128)(2,1)S(1)}, bf16[32,4096]{1,0:T(8,128)(2,1)S(1)}) custom-call(s32[16,128]{1,0:T(8,128)S(1)} %list_columns.1.cols, s32[8]{0:T(128)S(1)} %add_multiply_fusion.bases, s32[3]{0:T(128)S(1)} %pad_add_fusion.flags, bf16[32,4096]{1,0:T(8,128)(2,1)S(1)} %copy-done.15, ...), custom_call_target="tpu_custom_call" | custom-call | flops 15399999488 | bytes 1048576 | tf_op jit(solution)/shard_map/turning_layers/pallas_call | solution.py:353
  133.2 5.2 %backward_layers.2.rest_0_ = bf16[2,48,4096]{2,1,0:T(8,128)(2,1)S(1)} custom-call(s32[16,128]{1,0:T(8,128)S(1)} %list_columns.1.cols, s32[8]{0:T(128)S(1)} %add_multiply_fusion.bases, s32[3]{0:T(128)S(1)} %pad_add_fusion.flags, bf16[2,48,4096]{2,1,0:T(8,128)(2,1)S(1)} %get-tuple-element.76.stash.refs_0_, bf16[48,4096]{1,0:T(8,128)(2,1)S(1)} %get-tuple-element.77.loss_grad, ...), custom_call_target="tpu_custom_call" | custom-call | flops 4400000000 | bytes 1048576 | tf_op jit(solution)/shard_map/backward_layers/pallas_call | solution.py:400
  138.5 3.1 %flip_rows.1.turned = bf16[2,32,64,160]{3,2,1,0:T(8,128)(2,1)S(1)} custom-call(s32[8]{0:T(128)S(1)} %add_multiply_fusion.bases, bf16[2,48,4096]{2,1,0:T(8,128)(2,1)S(1)} %get-tuple-element.76.stash.refs_0_, bf16[2,32,4096]{2,1,0:T(8,128)(2,1)S(1)} %get-tuple-element.80.refs_1_.stash, bf16[2,48,4096]{2,1,0:T(8,128)(2,1)S(1)} %collective-permute-done.20.refs_2_, ...), custom_call_target="tpu_custom_call" | custom-call | flops 4400000000 | bytes 1048576 | tf_op jit(solution)/shard_map/flip_rows/pallas_call | solution.py:459
  142.3 5.0 %backward_layers.3.rest_1_ = bf16[2,32,4096]{2,1,0:T(8,128)(2,1)S(1)} custom-call(s32[16,128]{1,0:T(8,128)S(1)} %list_columns.1.cols, s32[8]{0:T(128)S(1)} %add_multiply_fusion.bases, s32[3]{0:T(128)S(1)} %pad_add_fusion.flags, bf16[2,32,4096]{2,1,0:T(8,128)(2,1)S(1)} %get-tuple-element.80.refs_1_.stash, bf16[32,4096]{1,0:T(8,128)(2,1)S(1)} %get-tuple-element.81.loss_grad, ...), custom_call_target="tpu_custom_call" | custom-call | flops 4400000000 | bytes 1048576 | tf_op jit(solution)/shard_map/backward_layers/pallas_call | solution.py:400
  147.4 1.9 collective-permute-done.24.rest_3_
  149.3 2.6 %block_grads.2 = (bf16[256,512]{1,0:T(8,128)(2,1)S(1)}, bf16[256,512]{1,0:T(8,128)(2,1)S(1)}) custom-call(s32[16,128]{1,0:T(8,128)S(1)} %list_columns.1.cols, s32[3]{0:T(128)S(1)} %pad_add_fusion.flags, bf16[2,32,64,160]{3,2,1,0:T(8,128)(2,1)S(1)} %flip_rows.1.turned, bf16[2,48,4096]{2,1,0:T(8,128)(2,1)S(1)} %backward_layers.2.rest_0_, ...), custom_call_target="tpu_custom_call" | custom-call | flops 3300000000 | bytes 1048576 | tf_op jit(solution)/shard_map/block_grads/pallas_call | solution.py:512
  153.2 1.6 collective-permute-start.26
  154.8 6.5 %block_grads.3 = (bf16[512,512]{1,0:T(8,128)(2,1)S(1)}, bf16[512,512]{1,0:T(8,128)(2,1)S(1)}, bf16[512,512]{1,0:T(8,128)(2,1)S(1)}, bf16[512,512]{1,0:T(8,128)(2...) custom-call(s32[16,128]{1,0:T(8,128)S(1)} %list_columns.1.cols, ...), custom_call_target="tpu_custom_call" | custom-call | flops 6600000000 | bytes 1048576 | tf_op jit(solution)/shard_map/block_grads/pallas_call | solution.py:512
  162.4 1.6 collective-permute-start.28
  164.0 11.7 %collective-permute-done.27 = bf16[512,512]{1,0:T(8,128)(2,1)S(1)} collective-permute-done((bf16[512,512]{1,0:T(8,128)(2,1)S(1)}, bf16[512,512]{1,0:T(8,128)(2,1)S(1)}, u32[]{:S(2)}, u32[]{:S(2)}) %collective-permute-start.27) | collective-permute-done | bytes 524320 | tf_op jit(solution)/shard_map/ppermute | solution.py:613
  178.3 11.1 %collective-permute-done.29 = bf16[512,512]{1,0:T(8,128)(2,1)S(1)} collective-permute-done((bf16[512,512]{1,0:T(8,128)(2,1)S(1)}, bf16[512,512]{1,0:T(8,128)(2,1)S(1)}, u32[]{:S(2)}, u32[]{:S(2)}) %collective-permute-start.29) | collective-permute-done | bytes 524320 | tf_op jit(solution)/shard_map/ppermute | solution.py:613
  191.3 10.8 %collective-permute-done.31 = bf16[512,512]{1,0:T(8,128)(2,1)S(1)} collective-permute-done((bf16[512,512]{1,0:T(8,128)(2,1)S(1)}, bf16[512,512]{1,0:T(8,128)(2,1)S(1)}, u32[]{:S(2)}, u32[]{:S(2)}) %collective-permute-start.31) | collective-permute-done | bytes 524320 | tf_op jit(solution)/shard_map/ppermute | solution.py:613
  203.2 1.6 broadcast_in_dim_reshape.3
  (114 shorter events, 33.7 us)
Async XLA Ops:
  4.7 16.4 %collective-permute-start = (bf16[528,512]{1,0:T(8,128)(2,1)S(1)}, bf16[528,512]{1,0:T(8,128)(2,1)S(1)}, u32[]{:S(2)}, u32[]{:S(2)}) collective-permute-start(bf16[528,512]{1,0:T(8,128)(2,1)S(1)} %fusion.3.refs_0_.rest_2_.rest_3_.rest_0_), channel_id=1, source_target_pairs={{0,2},{1,3},{2,6},{3,7},{6,4},{7,5},{4,0},{5,1},{8,10},{9,11},{10,... | collective-permute-start | bytes 1622024 | tf_op jit(solution)/shard_map/ppermute | solution.py:613
  7.8 13.7 %collective-permute-start.1 = (bf16[528,512]{1,0:T(8,128)(2,1)S(1)}, bf16[528,512]{1,0:T(8,128)(2,1)S(1)}, u32[]{:S(2)}, u32[]{:S(2)}) collective-permute-start(bf16[528,512]{1,0:T(8,128)(2,1)S(1)} %fusion.3.refs_0_.rest_2_.rest_3_.rest_0_), channel_id=1, source_target_pairs={{0,8},{8,0},{1,9},{9,1},{2,10},{10,2},{3,11},{11,3},{4,12},{12,4},... | collective-permute-start | bytes 1622024 | tf_op jit(solution)/shard_map/ppermute | solution.py:619
  9.3 12.2 %collective-permute-start.2 = (bf16[528,512]{1,0:T(8,128)(2,1)S(1)}, bf16[528,512]{1,0:T(8,128)(2,1)S(1)}, u32[]{:S(2)}, u32[]{:S(2)}) collective-permute-start(bf16[528,512]{1,0:T(8,128)(2,1)S(1)} %fusion.3.refs_0_.rest_2_.rest_3_.rest_0_), channel_id=1, source_target_pairs={{0,1},{1,0},{2,3},{3,2},{4,5},{5,4},{6,7},{7,6},{8,9},{9,8},{10,11... | collective-permute-start | bytes 1622024 | tf_op jit(solution)/shard_map/ppermute | solution.py:616
  21.5 14.1 %collective-permute-start.3 = (bf16[528,512]{1,0:T(8,128)(2,1)S(1)}, bf16[528,512]{1,0:T(8,128)(2,1)}, u32[]{:S(2)}, u32[]{:S(2)}) collective-permute-start(bf16[528,512]{1,0:T(8,128)(2,1)S(1)} %collective-permute-done.refs_1_.rest_3_.rest_4_.rest_1_), channel_id=1, source_target_pairs={{0,2},{1,3},{2,6},{3,7},{6,4},{7,5},{4,0},{5,1},{8,10},{9,11},{10,... | collective-permute-start | bytes 1622024 | tf_op jit(solution)/shard_map/ppermute | solution.py:613
  24.2 12.7 %collective-permute-start.4 = (bf16[528,512]{1,0:T(8,128)(2,1)S(1)}, bf16[528,512]{1,0:T(8,128)(2,1)}, u32[]{:S(2)}, u32[]{:S(2)}) collective-permute-start(bf16[528,512]{1,0:T(8,128)(2,1)S(1)} %collective-permute-done.refs_1_.rest_3_.rest_4_.rest_1_), channel_id=1, source_target_pairs={{0,8},{8,0},{1,9},{9,1},{2,10},{10,2},{3,11},{11,3},{4,12},{12,4},... | collective-permute-start | bytes 1622024 | tf_op jit(solution)/shard_map/ppermute | solution.py:619
  25.7 11.2 %collective-permute-start.6 = (bf16[528,512]{1,0:T(8,128)(2,1)S(1)}, bf16[528,512]{1,0:T(8,128)(2,1)}, u32[]{:S(2)}, u32[]{:S(2)}) collective-permute-start(bf16[528,512]{1,0:T(8,128)(2,1)S(1)} %collective-permute-done.refs_1_.rest_3_.rest_4_.rest_1_), channel_id=1, source_target_pairs={{0,1},{1,0},{2,3},{3,2},{4,5},{5,4},{6,7},{7,6},{8,9},{9,8},{10,11... | collective-permute-start | bytes 1622024 | tf_op jit(solution)/shard_map/ppermute | solution.py:616
  25.7 11.2 %collective-permute-start.5 = (bf16[528,512]{1,0:T(8,128)(2,1)S(1)}, bf16[528,512]{1,0:T(8,128)(2,1)}, u32[]{:S(2)}, u32[]{:S(2)}) collective-permute-start(bf16[528,512]{1,0:T(8,128)(2,1)S(1)} %collective-permute-done.1.refs_8_.rest_10_.rest_11_.rest_8_), channel_id=1, source_target_pairs={{0,1},{1,0},{2,3},{3,2},{4,5},{5,4},{6,7},{7,6},{8,9},{9,8},{10,11... | collective-permute-start | bytes 1622024 | tf_op jit(solution)/shard_map/ppermute | solution.py:616
  36.8 12.8 %collective-permute-start.7 = (bf16[528,512]{1,0:T(8,128)(2,1)}, bf16[528,512]{1,0:T(8,128)(2,1)S(1)}, u32[]{:S(2)}, u32[]{:S(2)}) collective-permute-start(bf16[528,512]{1,0:T(8,128)(2,1)} %collective-permute-done.3.refs_2_.rest_4_.rest_5_.rest_2_), channel_id=1, source_target_pairs={{0,2},{1,3},{2,6},{3,7},{6,4},{7,5},{4,0},{5,1},{8,10},{9,11},{10,... | collective-permute-start | bytes 1622024 | tf_op jit(solution)/shard_map/ppermute | solution.py:613
  38.4 11.9 %collective-permute-start.8 = (bf16[528,512]{1,0:T(8,128)(2,1)}, bf16[528,512]{1,0:T(8,128)(2,1)S(1)}, u32[]{:S(2)}, u32[]{:S(2)}) collective-permute-start(bf16[528,512]{1,0:T(8,128)(2,1)} %collective-permute-done.3.refs_2_.rest_4_.rest_5_.rest_2_), channel_id=1, source_target_pairs={{0,8},{8,0},{1,9},{9,1},{2,10},{10,2},{3,11},{11,3},{4,12},{12,4},... | collective-permute-start | bytes 1622024 | tf_op jit(solution)/shard_map/ppermute | solution.py:619
  39.9 11.2 %collective-permute-start.10 = (bf16[528,512]{1,0:T(8,128)(2,1)}, bf16[528,512]{1,0:T(8,128)(2,1)S(1)}, u32[]{:S(2)}, u32[]{:S(2)}) collective-permute-start(bf16[528,512]{1,0:T(8,128)(2,1)} %collective-permute-done.3.refs_2_.rest_4_.rest_5_.rest_2_), channel_id=1, source_target_pairs={{0,1},{1,0},{2,3},{3,2},{4,5},{5,4},{6,7},{7,6},{8,9},{9,8},{10,11... | collective-permute-start | bytes 1622024 | tf_op jit(solution)/shard_map/ppermute | solution.py:616
  39.9 10.4 %collective-permute-start.9 = (bf16[528,512]{1,0:T(8,128)(2,1)}, bf16[528,512]{1,0:T(8,128)(2,1)S(1)}, u32[]{:S(2)}, u32[]{:S(2)}) collective-permute-start(bf16[528,512]{1,0:T(8,128)(2,1)} %collective-permute-done.4.refs_9_.rest_11_.rest_12_.rest_9_), channel_id=1, source_target_pairs={{0,1},{1,0},{2,3},{3,2},{4,5},{5,4},{6,7},{7,6},{8,9},{9,8},{10,11... | collective-permute-start | bytes 1622024 | tf_op jit(solution)/shard_map/ppermute | solution.py:616
  51.9 11.1 %collective-permute-start.13 = (bf16[528,512]{1,0:T(8,128)(2,1)S(1)}, bf16[528,512]{1,0:T(8,128)(2,1)}, u32[]{:S(2)}, u32[]{:S(2)}) collective-permute-start(bf16[528,512]{1,0:T(8,128)(2,1)S(1)} %collective-permute-done.8.refs_10_.rest_12_.rest_13_.rest_10_), channel_id=1, source_target_pairs={{0,1},{1,0},{2,3},{3,2},{4,5},{5,4},{6,7},{7,6},{8,9},{9,8},{10,11... | collective-permute-start | bytes 1622024 | tf_op jit(solution)/shard_map/ppermute | solution.py:616
  51.9 11.1 %collective-permute-start.14 = (bf16[528,512]{1,0:T(8,128)(2,1)S(1)}, bf16[528,512]{1,0:T(8,128)(2,1)}, u32[]{:S(2)}, u32[]{:S(2)}) collective-permute-start(bf16[528,512]{1,0:T(8,128)(2,1)S(1)} %collective-permute-done.7.refs_3_.rest_5_.rest_6_.rest_3_), channel_id=1, source_target_pairs={{0,1},{1,0},{2,3},{3,2},{4,5},{5,4},{6,7},{7,6},{8,9},{9,8},{10,11... | collective-permute-start | bytes 1622024 | tf_op jit(solution)/shard_map/ppermute | solution.py:616
  53.1 9.3 %collective-permute-start.11 = (bf16[256,512]{1,0:T(8,128)(2,1)S(1)}, bf16[256,512]{1,0:T(8,128)(2,1)}, u32[]{:S(2)}, u32[]{:S(2)}) collective-permute-start(bf16[256,512]{1,0:T(8,128)(2,1)S(1)} %slice.18), channel_id=1, source_target_pairs={{0,2},{1,3},{2,6},{3,7},{6,4},{7,5},{4,0},{5,1},{8,10},{9,11},{10,... | collective-permute-start | bytes 786440 | tf_op jit(solution)/shard_map/ppermute | solution.py:613
  54.6 8.4 %collective-permute-start.12 = (bf16[272,512]{1,0:T(8,128)(2,1)S(1)}, bf16[272,512]{1,0:T(8,128)(2,1)}, u32[]{:S(2)}, u32[]{:S(2)}) collective-permute-start(bf16[272,512]{1,0:T(8,128)(2,1)S(1)} %slice.19), channel_id=1, source_target_pairs={{0,8},{8,0},{1,9},{9,1},{2,10},{10,2},{3,11},{11,3},{4,12},{12,4},... | collective-permute-start | bytes 835592 | tf_op jit(solution)/shard_map/ppermute | solution.py:619
  63.1 2.3 %collective-permute-start.16 = (bf16[272,512]{1,0:T(8,128)(2,1)}, bf16[272,512]{1,0:T(8,128)(2,1)}, u32[]{:S(2)}, u32[]{:S(2)}) collective-permute-start(bf16[272,512]{1,0:T(8,128)(2,1)} %collective-permute-done.12.refs_12_.rest_14_.rest_15_.rest_12_), channel_id=1, source_target_pairs={{0,1},{1,0},{2,3},{3,2},{4,5},{5,4},{6,7},{7,6},{8,9},{9,8},{10,11... | collective-permute-start | bytes 835592 | tf_op jit(solution)/shard_map/ppermute | solution.py:616
  81.2 13.7 %collective-permute-start.17 = (bf16[48,4096]{1,0:T(8,128)(2,1)S(1)}, bf16[48,4096]{1,0:T(8,128)(2,1)S(1)}, u32[]{:S(2)}, u32[]{:S(2)}) collective-permute-start(bf16[48,4096]{1,0:T(8,128)(2,1)S(1)} %forward_layers.2), channel_id=1, source_target_pairs={{0,16},{1,17},{2,18},{3,19},{4,20},{5,21},{6,22},{7,23},{8,24},{9,... | collective-permute-start | bytes 1179656 | tf_op jit(solution)/shard_map/ppermute | solution.py:674
  93.5 21.4 %collective-permute-start.19 = (bf16[32,4096]{1,0:T(8,128)(2,1)S(1)}, bf16[32,4096]{1,0:T(8,128)(2,1)S(1)}, u32[]{:S(2)}, u32[]{:S(2)}) collective-permute-start(bf16[32,4096]{1,0:T(8,128)(2,1)S(1)} %forward_layers.3), channel_id=1, source_target_pairs={{0,16},{1,17},{2,18},{3,19},{4,20},{5,21},{6,22},{7,23},{8,24},{9,... | collective-permute-start | bytes 786440 | tf_op jit(solution)/shard_map/ppermute | solution.py:674
  113.5 19.7 %collective-permute-start.18 = (bf16[48,4096]{1,0:T(8,128)(2,1)S(1)}, bf16[48,4096]{1,0:T(8,128)(2,1)S(1)}, u32[]{:S(2)}, u32[]{:S(2)}) collective-permute-start(bf16[48,4096]{1,0:T(8,128)(2,1)S(1)} %get-tuple-element.78), channel_id=1, source_target_pairs={{16,0},{17,1},{18,2},{19,3},{20,4},{21,5},{22,6},{23,7},{24,8},{25... | collective-permute-start | bytes 1179656 | tf_op jit(solution)/shard_map/ppermute | solution.py:674
  114.8 23.7 %collective-permute-start.20 = (bf16[2,48,4096]{2,1,0:T(8,128)(2,1)S(1)}, bf16[2,48,4096]{2,1,0:T(8,128)(2,1)S(1)}, u32[]{:S(2)}, u32[]{:S(2)}) collective-permute-start(bf16[2,48,4096]{2,1,0:T(8,128)(2,1)S(1)} %get-tuple-element.76.stash.refs_0_), channel_id=1, source_target_pairs={{0,1},{1,0},{2,3},{3,2},{4,5},{5,4},{6,7},{7,6},{8,9},{9,8},{10,11... | collective-permute-start | bytes 2359304 | tf_op jit(solution)/shard_map/ppermute | solution.py:616
  131.3 7.1 %collective-permute-start.21 = (bf16[2,32,4096]{2,1,0:T(8,128)(2,1)S(1)}, bf16[2,32,4096]{2,1,0:T(8,128)(2,1)S(1)}, u32[]{:S(2)}, u32[]{:S(2)}) collective-permute-start(bf16[2,32,4096]{2,1,0:T(8,128)(2,1)S(1)} %get-tuple-element.80.refs_1_.stash), channel_id=1, source_target_pairs={{0,1},{1,0},{2,3},{3,2},{4,5},{5,4},{6,7},{7,6},{8,9},{9,8},{10,11... | collective-permute-start | bytes 1572872 | tf_op jit(solution)/shard_map/ppermute | solution.py:616
  131.9 10.4 %collective-permute-start.22 = (bf16[32,4096]{1,0:T(8,128)(2,1)S(1)}, bf16[32,4096]{1,0:T(8,128)(2,1)S(1)}, u32[]{:S(2)}, u32[]{:S(2)}) collective-permute-start(bf16[32,4096]{1,0:T(8,128)(2,1)S(1)} %get-tuple-element.82), channel_id=1, source_target_pairs={{16,0},{17,1},{18,2},{19,3},{20,4},{21,5},{22,6},{23,7},{24,8},{25... | collective-permute-start | bytes 786440 | tf_op jit(solution)/shard_map/ppermute | solution.py:674
  138.3 9.1 %collective-permute-start.23 = (bf16[2,48,4096]{2,1,0:T(8,128)(2,1)S(1)}, bf16[2,48,4096]{2,1,0:T(8,128)(2,1)S(1)}, u32[]{:S(2)}, u32[]{:S(2)}) collective-permute-start(bf16[2,48,4096]{2,1,0:T(8,128)(2,1)S(1)} %backward_layers.2.rest_0_), channel_id=1, source_target_pairs={{0,1},{1,0},{2,3},{3,2},{4,5},{5,4},{6,7},{7,6},{8,9},{9,8},{10,11... | collective-permute-start | bytes 2359304 | tf_op jit(solution)/shard_map/ppermute | solution.py:616
  147.3 2.0 collective-permute-start.24
  151.9 9.3 %collective-permute-start.25 = (bf16[256,512]{1,0:T(8,128)(2,1)S(1)}, bf16[256,512]{1,0:T(8,128)(2,1)S(1)}, u32[]{:S(2)}, u32[]{:S(2)}) collective-permute-start(bf16[256,512]{1,0:T(8,128)(2,1)S(1)} %get-tuple-element.86), channel_id=1, source_target_pairs={{0,2},{1,3},{2,6},{3,7},{6,4},{7,5},{4,0},{5,1},{8,10},{9,11},{10,... | collective-permute-start | bytes 786440 | tf_op jit(solution)/shard_map/ppermute | solution.py:613
  153.2 8.1 %collective-permute-start.26 = (bf16[256,512]{1,0:T(8,128)(2,1)S(1)}, bf16[256,512]{1,0:T(8,128)(2,1)S(1)}, u32[]{:S(2)}, u32[]{:S(2)}) collective-permute-start(bf16[256,512]{1,0:T(8,128)(2,1)S(1)} %get-tuple-element.87), channel_id=1, source_target_pairs={{0,8},{8,0},{1,9},{9,1},{2,10},{10,2},{3,11},{11,3},{4,12},{12,4},... | collective-permute-start | bytes 786440 | tf_op jit(solution)/shard_map/ppermute | solution.py:619
  161.4 14.4 %collective-permute-start.27 = (bf16[512,512]{1,0:T(8,128)(2,1)S(1)}, bf16[512,512]{1,0:T(8,128)(2,1)S(1)}, u32[]{:S(2)}, u32[]{:S(2)}) collective-permute-start(bf16[512,512]{1,0:T(8,128)(2,1)S(1)} %add_convert_fusion.4), channel_id=1, source_target_pairs={{0,2},{1,3},{2,6},{3,7},{6,4},{7,5},{4,0},{5,1},{8,10},{9,11},{10,... | collective-permute-start | bytes 1572872 | tf_op jit(solution)/shard_map/ppermute | solution.py:613
  162.4 13.3 %collective-permute-start.28 = (bf16[512,512]{1,0:T(8,128)(2,1)S(1)}, bf16[512,512]{1,0:T(8,128)(2,1)S(1)}, u32[]{:S(2)}, u32[]{:S(2)}) collective-permute-start(bf16[512,512]{1,0:T(8,128)(2,1)S(1)} %add_convert_fusion.3), channel_id=1, source_target_pairs={{0,8},{8,0},{1,9},{9,1},{2,10},{10,2},{3,11},{11,3},{4,12},{12,4},... | collective-permute-start | bytes 1572872 | tf_op jit(solution)/shard_map/ppermute | solution.py:619
  175.9 13.4 %collective-permute-start.29 = (bf16[512,512]{1,0:T(8,128)(2,1)S(1)}, bf16[512,512]{1,0:T(8,128)(2,1)S(1)}, u32[]{:S(2)}, u32[]{:S(2)}) collective-permute-start(bf16[512,512]{1,0:T(8,128)(2,1)S(1)} %add_convert_fusion.2), channel_id=1, source_target_pairs={{0,2},{1,3},{2,6},{3,7},{6,4},{7,5},{4,0},{5,1},{8,10},{9,11},{10,... | collective-permute-start | bytes 1572872 | tf_op jit(solution)/shard_map/ppermute | solution.py:613
  177.3 12.1 %collective-permute-start.30 = (bf16[512,512]{1,0:T(8,128)(2,1)S(1)}, bf16[512,512]{1,0:T(8,128)(2,1)S(1)}, u32[]{:S(2)}, u32[]{:S(2)}) collective-permute-start(bf16[512,512]{1,0:T(8,128)(2,1)S(1)} %get-tuple-element.110), channel_id=1, source_target_pairs={{0,8},{8,0},{1,9},{9,1},{2,10},{10,2},{3,11},{11,3},{4,12},{12,4},... | collective-permute-start | bytes 1572872 | tf_op jit(solution)/shard_map/ppermute | solution.py:619
  189.6 12.5 %collective-permute-start.31 = (bf16[512,512]{1,0:T(8,128)(2,1)S(1)}, bf16[512,512]{1,0:T(8,128)(2,1)S(1)}, u32[]{:S(2)}, u32[]{:S(2)}) collective-permute-start(bf16[512,512]{1,0:T(8,128)(2,1)S(1)} %add_convert_fusion.1), channel_id=1, source_target_pairs={{0,2},{1,3},{2,6},{3,7},{6,4},{7,5},{4,0},{5,1},{8,10},{9,11},{10,... | collective-permute-start | bytes 1572872 | tf_op jit(solution)/shard_map/ppermute | solution.py:613
  190.9 11.2 %collective-permute-start.32 = (bf16[512,512]{1,0:T(8,128)(2,1)S(1)}, bf16[512,512]{1,0:T(8,128)(2,1)S(1)}, u32[]{:S(2)}, u32[]{:S(2)}) collective-permute-start(bf16[512,512]{1,0:T(8,128)(2,1)S(1)} %get-tuple-element.114), channel_id=1, source_target_pairs={{0,8},{8,0},{1,9},{9,1},{2,10},{10,2},{3,11},{11,3},{4,12},{12,4},... | collective-permute-start | bytes 1572872 | tf_op jit(solution)/shard_map/ppermute | solution.py:619
  (20 other events, 143.6 us)

commit v4 on v3

--- a/solution.py
+++ b/solution.py
@@ -625,18 +625,13 @@
     straight = to_rows(blocks[0])
     own = jnp.concatenate([jnp.where(live, straight, jnp.zeros_like(straight)), tail], axis=0)
 
-    half = rows // 2 * BLK
     owns, others, far_owns, far_others = [own], [], [], []
     for slot in range(places):
         last = slot + 1 == places
         moving = {}
         if not last:
             moving["a_own"] = ring(owns[slot])
-            moving["b_other"] = [partner(owns[slot])]
-        elif slot:
-            moving["b_other"] = [ring(others[-1][0][:half]), partner(owns[slot][half:])]
-        else:
-            moving["b_other"] = [partner(owns[slot])]
+        moving["b_other"] = [partner(owns[slot])]
         if slot:
             moving["c_far_other"] = [sibling(part) for part in others[-1]]
         moving["d_far_own"] = sibling(owns[slot])

time: 205 us -> 198 us (0.966)
  local copies, waits for them, and re-layouts: 18.6 us -> 10 us
  waiting for transfers between devices: 71.4 us -> 74 us
    ppermute x8, waiting for transfers between devices: 2.96 us -> 12 us  [partner(): lax.ppermute(array, 'side', [(i, sides - 1 - i) for i in range(sides)])]
    unnamed x38 -> x8, local copies, waits for them, and re-layouts: 6.35 us -> 0.04 us
    ppermute x8 -> x7, waiting for transfers between devices: 64.2 us -> 58.7 us  [ring(): return lax.ppermute(array, 'dp', hops)]
    ppermute x8 -> x7, starting transfers between devices: 13.7 us -> 12.1 us  [ring(): return lax.ppermute(array, 'dp', hops)]
  transfers between devices with their start and end apart: 33 -> 31, of which waited for: 15 -> 15; matrix products, arithmetic and copies ran while one was open for 3% -> 2% of each run, Pallas kernels for 31% -> 32%
where the time goes in v4:
time: 198 us
  Pallas kernels  77.1 us (39%)
  waiting for transfers between devices  74 us (37%)
  starting transfers between devices  33.7 us (17%)
  local copies, waits for them, and re-layouts  10 us (5%)
  other arithmetic  2.7 us (1%)
    ppermute x7, waiting for transfers between devices, ring(): return lax.ppermute(array, 'dp', hops)  58.7 us
    pallas_call x4, Pallas kernels, forward_pass(): pl.pallas_call(functools.partial(forward_kernel, rows, slots, len(straigh...  53.6 us
    ppermute x7, starting transfers between devices, ring(): return lax.ppermute(array, 'dp', hops)  12.1 us
    ppermute x8, starting transfers between devices, partner(): lax.ppermute(array, 'side', [(i, sides - 1 - i) for i in range(sides)])  12 us
    ppermute x8, waiting for transfers between devices, partner(): lax.ppermute(array, 'side', [(i, sides - 1 - i) for i in range(sides)])  12 us
    pallas_call x2, Pallas kernels, backward_pass(): pl.pallas_call(functools.partial(backward_kernel, rows, slots, len(across...  10.3 us
    pallas_call x2, Pallas kernels, block_grad_pass(): pl.pallas_call(functools.partial(block_grad_kernel, rows, slots, jobs, ha...  9.1 us
    ppermute x4, starting transfers between devices, hop(): return lax.ppermute(array, 'stage', route)  7.33 us
  transfers between devices with their start and end apart: 31, of which 15 were waited for; matrix products, arithmetic and copies ran while one was open for 2% of the time, Pallas kernels for 32%

profile of v4, /device:TPU:0, one launch (start us, length us, event | category | flops | bytes accessed | tf_op | source)
XLA Modules:
  0.0 197.9 jit_solution(17596457556541499814)
XLA Ops:
  0.9 2.1 %reshape_squeeze.4 = bf16[8,8,64,64]{3,2,1,0:T(8,128)(2,1)S(1)} reshape(bf16[1,8,8,4096]{3,2,1,0:T(8,128)(2,1)} %param.9) | data formatting | bytes 1048576 | tf_op jit(solution)/shard_map/reshape;squeeze | solution.py:570
  4.7 3.1 %collective-permute-start = (bf16[528,512]{1,0:T(8,128)(2,1)S(1)}, bf16[528,512]{1,0:T(8,128)(2,1)S(1)}, u32[]{:S(2)}, u32[]{:S(2)}) collective-permute-start(bf16[528,512]{1,0:T(8,128)(2,1)S(1)} %fusion.3.refs_0_.rest_2_.rest_3_.rest_0_), channel_id=1, source_target_pairs={{0,2},{1,3},{2,6},{3,7},{6,4},{7,5},{4,0},{5,1},{8,10},{9,11},{10,... | collective-permute-start | bytes 1622024 | tf_op jit(solution)/shard_map/ppermute | solution.py:613
  7.8 1.5 collective-permute-start.1
  10.5 10.5 %collective-permute-done.refs_1_.rest_3_.rest_4_.rest_1_ = bf16[528,512]{1,0:T(8,128)(2,1)S(1)} collective-permute-done((bf16[528,512]{1,0:T(8,128)(2,1)S(1)}, bf16[528,512]{1,0:T(8,128)(2,1)S(1)}, u32[]{:S(2)}, u32[]{:S(2)}) %collective-permute-start) | collective-permute-done | bytes 540704 | tf_op jit(solution)/shard_map/ppermute | solution.py:613
  21.5 2.6 %collective-permute-start.3 = (bf16[528,512]{1,0:T(8,128)(2,1)S(1)}, bf16[528,512]{1,0:T(8,128)(2,1)}, u32[]{:S(2)}, u32[]{:S(2)}) collective-permute-start(bf16[528,512]{1,0:T(8,128)(2,1)S(1)} %collective-permute-done.refs_1_.rest_3_.rest_4_.rest_1_), channel_id=1, source_target_pairs={{0,2},{1,3},{2,6},{3,7},{6,4},{7,5},{4,0},{5,1},{8,10},{9,11},{10,... | collective-permute-start | bytes 1622024 | tf_op jit(solution)/shard_map/ppermute | solution.py:613
  24.1 1.5 collective-permute-start.4
  27.5 8.1 %collective-permute-done.3.refs_2_.rest_4_.rest_5_.rest_2_ = bf16[528,512]{1,0:T(8,128)(2,1)} collective-permute-done((bf16[528,512]{1,0:T(8,128)(2,1)S(1)}, bf16[528,512]{1,0:T(8,128)(2,1)}, u32[]{:S(2)}, u32[]{:S(2)}) %collective-permute-start.3) | collective-permute-done | bytes 540704 | tf_op jit(solution)/shard_map/ppermute | solution.py:613
  36.8 1.5 collective-permute-start.7
  38.3 1.5 collective-permute-start.8
  41.3 8.4 %collective-permute-done.7.refs_3_.rest_5_.rest_6_.rest_3_ = bf16[528,512]{1,0:T(8,128)(2,1)} collective-permute-done((bf16[528,512]{1,0:T(8,128)(2,1)}, bf16[528,512]{1,0:T(8,128)(2,1)}, u32[]{:S(2)}, u32[]{:S(2)}) %collective-permute-start.7) | collective-permute-done | bytes 540704 | tf_op jit(solution)/shard_map/ppermute | solution.py:613
  50.7 1.5 collective-permute-start.11
  52.8 8.9 %collective-permute-done.11.refs_11_.rest_13_.rest_14_.rest_11_ = bf16[528,512]{1,0:T(8,128)(2,1)S(1)} collective-permute-done((bf16[528,512]{1,0:T(8,128)(2,1)}, bf16[528,512]{1,0:T(8,128)(2,1)S(1)}, u32[]{:S(2)}, u32[]{:S(2)}) %collective-permute-start.11) | collective-permute-done | bytes 540704 | tf_op jit(solution)/shard_map/ppermute | solution.py:619
  64.7 10.0 %forward_layers.2 = bf16[48,4096]{1,0:T(8,128)(2,1)S(1)} custom-call(s32[16,128]{1,0:T(8,128)S(1)} %list_columns.1.cols, s32[8]{0:T(128)S(1)} %add_multiply_fusion.bases, s32[3]{0:T(128)S(1)} %pad_add_fusion.flags, bf16[48,4096]{1,0:T(8,128)(2,1)S(1)} %constant_dynamic-slice_fusion.1.rest_0_.rest_1_, ...), custom_call_target="tpu_custom_call" | custom-call | flops 8800000000 | bytes 1048576 | tf_op jit(solution)/shard_map/forward_layers/pallas_call | solution.py:353
  74.7 3.5 %collective-permute-start.15 = (bf16[48,4096]{1,0:T(8,128)(2,1)S(1)}, bf16[48,4096]{1,0:T(8,128)(2,1)S(1)}, u32[]{:S(2)}, u32[]{:S(2)}) collective-permute-start(bf16[48,4096]{1,0:T(8,128)(2,1)S(1)} %forward_layers.2), channel_id=1, source_target_pairs={{0,16},{1,17},{2,18},{3,19},{4,20},{5,21},{6,22},{7,23},{8,24},{9,... | collective-permute-start | bytes 1179656 | tf_op jit(solution)/shard_map/ppermute | solution.py:669
  78.2 8.7 %forward_layers.3 = bf16[32,4096]{1,0:T(8,128)(2,1)S(1)} custom-call(s32[16,128]{1,0:T(8,128)S(1)} %list_columns.1.cols, s32[8]{0:T(128)S(1)} %add_multiply_fusion.bases, s32[3]{0:T(128)S(1)} %pad_add_fusion.flags, bf16[32,4096]{1,0:T(8,128)(2,1)S(1)} %copy-done.1, bf16[32,4096]{1,0:T(8,128)(2,1)S(1)} %copy-done.1, ...), custom_call_target="tpu_custom_call" | custom-call | flops 8800000000 | bytes 1048576 | tf_op jit(solution)/shard_map/forward_layers/pallas_call | solution.py:353
  88.2 18.5 %turning_layers.2 = (bf16[2,48,4096]{2,1,0:T(8,128)(2,1)S(1)}, bf16[48,4096]{1,0:T(8,128)(2,1)S(1)}, bf16[48,4096]{1,0:T(8,128)(2,1)S(1)}) custom-call(s32[16,128]{1,0:T(8,128)S(1)} %list_columns.1.cols, s32[8]{0:T(128)S(1)} %add_multiply_fusion.bases, s32[3]{0:T(128)S(1)} %pad_add_fusion.flags, ...), custom_call_target="tpu_custom_call" | custom-call | flops 15399999488 | bytes 1048576 | tf_op jit(solution)/shard_map/turning_layers/pallas_call | solution.py:353
  108.1 16.4 %turning_layers.3 = (bf16[2,32,4096]{2,1,0:T(8,128)(2,1)S(1)}, bf16[32,4096]{1,0:T(8,128)(2,1)S(1)}, bf16[32,4096]{1,0:T(8,128)(2,1)S(1)}) custom-call(s32[16,128]{1,0:T(8,128)S(1)} %list_columns.1.cols, s32[8]{0:T(128)S(1)} %add_multiply_fusion.bases, s32[3]{0:T(128)S(1)} %pad_add_fusion.flags, bf16[32,4096]{1,0:T(8,128)(2,1)S(1)} %copy-done.1, ...), custom_call_target="tpu_custom_call" | custom-call | flops 15399999488 | bytes 1048576 | tf_op jit(solution)/shard_map/turning_layers/pallas_call | solution.py:353
  126.3 5.2 %backward_layers.2.rest_0_ = bf16[2,48,4096]{2,1,0:T(8,128)(2,1)S(1)} custom-call(s32[16,128]{1,0:T(8,128)S(1)} %list_columns.1.cols, s32[8]{0:T(128)S(1)} %add_multiply_fusion.bases, s32[3]{0:T(128)S(1)} %pad_add_fusion.flags, bf16[2,48,4096]{2,1,0:T(8,128)(2,1)S(1)} %get-tuple-element.74.stash.refs_0_, bf16[48,4096]{1,0:T(8,128)(2,1)S(1)} %get-tuple-element.75.loss_grad, ...), custom_call_target="tpu_custom_call" | custom-call | flops 4400000000 | bytes 1048576 | tf_op jit(solution)/shard_map/backward_layers/pallas_call | solution.py:400
  131.7 3.1 %flip_rows.1.turned = bf16[2,32,64,160]{3,2,1,0:T(8,128)(2,1)S(1)} custom-call(s32[8]{0:T(128)S(1)} %add_multiply_fusion.bases, bf16[2,48,4096]{2,1,0:T(8,128)(2,1)S(1)} %get-tuple-element.74.stash.refs_0_, bf16[2,32,4096]{2,1,0:T(8,128)(2,1)S(1)} %get-tuple-element.78.refs_1_.stash, bf16[2,48,4096]{2,1,0:T(8,128)(2,1)S(1)} %collective-permute-done.18.refs_2_, ...), custom_call_target="tpu_custom_call" | custom-call | flops 4400000000 | bytes 1048576 | tf_op jit(solution)/shard_map/flip_rows/pallas_call | solution.py:459
  135.5 5.1 %backward_layers.3.rest_1_ = bf16[2,32,4096]{2,1,0:T(8,128)(2,1)S(1)} custom-call(s32[16,128]{1,0:T(8,128)S(1)} %list_columns.1.cols, s32[8]{0:T(128)S(1)} %add_multiply_fusion.bases, s32[3]{0:T(128)S(1)} %pad_add_fusion.flags, bf16[2,32,4096]{2,1,0:T(8,128)(2,1)S(1)} %get-tuple-element.78.refs_1_.stash, bf16[32,4096]{1,0:T(8,128)(2,1)S(1)} %get-tuple-element.79.loss_grad, ...), custom_call_target="tpu_custom_call" | custom-call | flops 4400000000 | bytes 1048576 | tf_op jit(solution)/shard_map/backward_layers/pallas_call | solution.py:400
  140.6 1.9 collective-permute-done.22.rest_3_
  142.5 2.6 %block_grads.2 = (bf16[256,512]{1,0:T(8,128)(2,1)S(1)}, bf16[256,512]{1,0:T(8,128)(2,1)S(1)}) custom-call(s32[16,128]{1,0:T(8,128)S(1)} %list_columns.1.cols, s32[3]{0:T(128)S(1)} %pad_add_fusion.flags, bf16[2,32,64,160]{3,2,1,0:T(8,128)(2,1)S(1)} %flip_rows.1.turned, bf16[2,48,4096]{2,1,0:T(8,128)(2,1)S(1)} %backward_layers.2.rest_0_, ...), custom_call_target="tpu_custom_call" | custom-call | flops 3300000000 | bytes 1048576 | tf_op jit(solution)/shard_map/block_grads/pallas_call | solution.py:512
  145.1 1.6 collective-permute-start.23
  146.7 1.5 collective-permute-start.24
  148.2 6.5 %block_grads.3 = (bf16[512,512]{1,0:T(8,128)(2,1)S(1)}, bf16[512,512]{1,0:T(8,128)(2,1)S(1)}, bf16[512,512]{1,0:T(8,128)(2,1)S(1)}, bf16[512,512]{1,0:T(8,128)(2...) custom-call(s32[16,128]{1,0:T(8,128)S(1)} %list_columns.1.cols, ...), custom_call_target="tpu_custom_call" | custom-call | flops 6600000000 | bytes 1048576 | tf_op jit(solution)/shard_map/block_grads/pallas_call | solution.py:512
  156.3 1.6 collective-permute-start.26
  157.8 11.3 %collective-permute-done.25 = bf16[512,512]{1,0:T(8,128)(2,1)S(1)} collective-permute-done((bf16[512,512]{1,0:T(8,128)(2,1)S(1)}, bf16[512,512]{1,0:T(8,128)(2,1)S(1)}, u32[]{:S(2)}, u32[]{:S(2)}) %collective-permute-start.25) | collective-permute-done | bytes 524320 | tf_op jit(solution)/shard_map/ppermute | solution.py:613
  170.6 1.5 collective-permute-start.28
  172.2 10.6 %collective-permute-done.27 = bf16[512,512]{1,0:T(8,128)(2,1)S(1)} collective-permute-done((bf16[512,512]{1,0:T(8,128)(2,1)S(1)}, bf16[512,512]{1,0:T(8,128)(2,1)S(1)}, u32[]{:S(2)}, u32[]{:S(2)}) %collective-permute-start.27) | collective-permute-done | bytes 524320 | tf_op jit(solution)/shard_map/ppermute | solution.py:613
  183.9 1.5 collective-permute-start.30
  185.4 9.8 %collective-permute-done.29 = bf16[512,512]{1,0:T(8,128)(2,1)S(1)} collective-permute-done((bf16[512,512]{1,0:T(8,128)(2,1)S(1)}, bf16[512,512]{1,0:T(8,128)(2,1)S(1)}, u32[]{:S(2)}, u32[]{:S(2)}) %collective-permute-start.29) | collective-permute-done | bytes 524320 | tf_op jit(solution)/shard_map/ppermute | solution.py:613
  196.3 1.6 broadcast_in_dim_reshape.3
  (78 shorter events, 24.1 us)
Async XLA Ops:
  0.0 26.8 %copy-start = (bf16[2,80,4096]{2,1,0:T(8,128)(2,1)S(1)}, bf16[2,80,4096]{2,1,0:T(8,128)(2,1)}, u32[]{:S(2)}) copy-start(bf16[2,80,4096]{2,1,0:T(8,128)(2,1)} %param.7) | copy-start | bytes 3932164
  4.7 16.4 %collective-permute-start = (bf16[528,512]{1,0:T(8,128)(2,1)S(1)}, bf16[528,512]{1,0:T(8,128)(2,1)S(1)}, u32[]{:S(2)}, u32[]{:S(2)}) collective-permute-start(bf16[528,512]{1,0:T(8,128)(2,1)S(1)} %fusion.3.refs_0_.rest_2_.rest_3_.rest_0_), channel_id=1, source_target_pairs={{0,2},{1,3},{2,6},{3,7},{6,4},{7,5},{4,0},{5,1},{8,10},{9,11},{10,... | collective-permute-start | bytes 1622024 | tf_op jit(solution)/shard_map/ppermute | solution.py:613
  7.8 13.7 %collective-permute-start.1 = (bf16[528,512]{1,0:T(8,128)(2,1)S(1)}, bf16[528,512]{1,0:T(8,128)(2,1)S(1)}, u32[]{:S(2)}, u32[]{:S(2)}) collective-permute-start(bf16[528,512]{1,0:T(8,128)(2,1)S(1)} %fusion.3.refs_0_.rest_2_.rest_3_.rest_0_), channel_id=1, source_target_pairs={{0,8},{8,0},{1,9},{9,1},{2,10},{10,2},{3,11},{11,3},{4,12},{12,4},... | collective-permute-start | bytes 1622024 | tf_op jit(solution)/shard_map/ppermute | solution.py:619
  9.3 12.2 %collective-permute-start.2 = (bf16[528,512]{1,0:T(8,128)(2,1)S(1)}, bf16[528,512]{1,0:T(8,128)(2,1)S(1)}, u32[]{:S(2)}, u32[]{:S(2)}) collective-permute-start(bf16[528,512]{1,0:T(8,128)(2,1)S(1)} %fusion.3.refs_0_.rest_2_.rest_3_.rest_0_), channel_id=1, source_target_pairs={{0,1},{1,0},{2,3},{3,2},{4,5},{5,4},{6,7},{7,6},{8,9},{9,8},{10,11... | collective-permute-start | bytes 1622024 | tf_op jit(solution)/shard_map/ppermute | solution.py:616
  21.5 14.0 %collective-permute-start.3 = (bf16[528,512]{1,0:T(8,128)(2,1)S(1)}, bf16[528,512]{1,0:T(8,128)(2,1)}, u32[]{:S(2)}, u32[]{:S(2)}) collective-permute-start(bf16[528,512]{1,0:T(8,128)(2,1)S(1)} %collective-permute-done.refs_1_.rest_3_.rest_4_.rest_1_), channel_id=1, source_target_pairs={{0,2},{1,3},{2,6},{3,7},{6,4},{7,5},{4,0},{5,1},{8,10},{9,11},{10,... | collective-permute-start | bytes 1622024 | tf_op jit(solution)/shard_map/ppermute | solution.py:613
  24.1 12.7 %collective-permute-start.4 = (bf16[528,512]{1,0:T(8,128)(2,1)S(1)}, bf16[528,512]{1,0:T(8,128)(2,1)}, u32[]{:S(2)}, u32[]{:S(2)}) collective-permute-start(bf16[528,512]{1,0:T(8,128)(2,1)S(1)} %collective-permute-done.refs_1_.rest_3_.rest_4_.rest_1_), channel_id=1, source_target_pairs={{0,8},{8,0},{1,9},{9,1},{2,10},{10,2},{3,11},{11,3},{4,12},{12,4},... | collective-permute-start | bytes 1622024 | tf_op jit(solution)/shard_map/ppermute | solution.py:619
  25.6 11.2 %collective-permute-start.6 = (bf16[528,512]{1,0:T(8,128)(2,1)S(1)}, bf16[528,512]{1,0:T(8,128)(2,1)}, u32[]{:S(2)}, u32[]{:S(2)}) collective-permute-start(bf16[528,512]{1,0:T(8,128)(2,1)S(1)} %collective-permute-done.refs_1_.rest_3_.rest_4_.rest_1_), channel_id=1, source_target_pairs={{0,1},{1,0},{2,3},{3,2},{4,5},{5,4},{6,7},{7,6},{8,9},{9,8},{10,11... | collective-permute-start | bytes 1622024 | tf_op jit(solution)/shard_map/ppermute | solution.py:616
  25.6 11.2 %collective-permute-start.5 = (bf16[528,512]{1,0:T(8,128)(2,1)S(1)}, bf16[528,512]{1,0:T(8,128)(2,1)}, u32[]{:S(2)}, u32[]{:S(2)}) collective-permute-start(bf16[528,512]{1,0:T(8,128)(2,1)S(1)} %collective-permute-done.1.refs_8_.rest_10_.rest_11_.rest_8_), channel_id=1, source_target_pairs={{0,1},{1,0},{2,3},{3,2},{4,5},{5,4},{6,7},{7,6},{8,9},{9,8},{10,11... | collective-permute-start | bytes 1622024 | tf_op jit(solution)/shard_map/ppermute | solution.py:616
  36.8 12.8 %collective-permute-start.7 = (bf16[528,512]{1,0:T(8,128)(2,1)}, bf16[528,512]{1,0:T(8,128)(2,1)}, u32[]{:S(2)}, u32[]{:S(2)}) collective-permute-start(bf16[528,512]{1,0:T(8,128)(2,1)} %collective-permute-done.3.refs_2_.rest_4_.rest_5_.rest_2_), channel_id=1, source_target_pairs={{0,2},{1,3},{2,6},{3,7},{6,4},{7,5},{4,0},{5,1},{8,10},{9,11},{10,... | collective-permute-start | bytes 1622024 | tf_op jit(solution)/shard_map/ppermute | solution.py:613
  38.3 12.4 %collective-permute-start.8 = (bf16[528,512]{1,0:T(8,128)(2,1)}, bf16[528,512]{1,0:T(8,128)(2,1)}, u32[]{:S(2)}, u32[]{:S(2)}) collective-permute-start(bf16[528,512]{1,0:T(8,128)(2,1)} %collective-permute-done.3.refs_2_.rest_4_.rest_5_.rest_2_), channel_id=1, source_target_pairs={{0,8},{8,0},{1,9},{9,1},{2,10},{10,2},{3,11},{11,3},{4,12},{12,4},... | collective-permute-start | bytes 1622024 | tf_op jit(solution)/shard_map/ppermute | solution.py:619
  39.8 10.9 %collective-permute-start.10 = (bf16[528,512]{1,0:T(8,128)(2,1)}, bf16[528,512]{1,0:T(8,128)(2,1)}, u32[]{:S(2)}, u32[]{:S(2)}) collective-permute-start(bf16[528,512]{1,0:T(8,128)(2,1)} %collective-permute-done.3.refs_2_.rest_4_.rest_5_.rest_2_), channel_id=1, source_target_pairs={{0,1},{1,0},{2,3},{3,2},{4,5},{5,4},{6,7},{7,6},{8,9},{9,8},{10,11... | collective-permute-start | bytes 1622024 | tf_op jit(solution)/shard_map/ppermute | solution.py:616
  39.8 10.9 %collective-permute-start.9 = (bf16[528,512]{1,0:T(8,128)(2,1)}, bf16[528,512]{1,0:T(8,128)(2,1)}, u32[]{:S(2)}, u32[]{:S(2)}) collective-permute-start(bf16[528,512]{1,0:T(8,128)(2,1)} %collective-permute-done.4.refs_9_.rest_11_.rest_12_.rest_9_), channel_id=1, source_target_pairs={{0,1},{1,0},{2,3},{3,2},{4,5},{5,4},{6,7},{7,6},{8,9},{9,8},{10,11... | collective-permute-start | bytes 1622024 | tf_op jit(solution)/shard_map/ppermute | solution.py:616
  50.7 11.0 %collective-permute-start.11 = (bf16[528,512]{1,0:T(8,128)(2,1)}, bf16[528,512]{1,0:T(8,128)(2,1)S(1)}, u32[]{:S(2)}, u32[]{:S(2)}) collective-permute-start(bf16[528,512]{1,0:T(8,128)(2,1)} %collective-permute-done.7.refs_3_.rest_5_.rest_6_.rest_3_), channel_id=1, source_target_pairs={{0,8},{8,0},{1,9},{9,1},{2,10},{10,2},{3,11},{11,3},{4,12},{12,4},... | collective-permute-start | bytes 1622024 | tf_op jit(solution)/shard_map/ppermute | solution.py:619
  52.2 9.5 %collective-permute-start.13 = (bf16[528,512]{1,0:T(8,128)(2,1)}, bf16[528,512]{1,0:T(8,128)(2,1)S(1)}, u32[]{:S(2)}, u32[]{:S(2)}) collective-permute-start(bf16[528,512]{1,0:T(8,128)(2,1)} %collective-permute-done.7.refs_3_.rest_5_.rest_6_.rest_3_), channel_id=1, source_target_pairs={{0,1},{1,0},{2,3},{3,2},{4,5},{5,4},{6,7},{7,6},{8,9},{9,8},{10,11... | collective-permute-start | bytes 1622024 | tf_op jit(solution)/shard_map/ppermute | solution.py:616
  52.2 9.5 %collective-permute-start.12 = (bf16[528,512]{1,0:T(8,128)(2,1)}, bf16[528,512]{1,0:T(8,128)(2,1)S(1)}, u32[]{:S(2)}, u32[]{:S(2)}) collective-permute-start(bf16[528,512]{1,0:T(8,128)(2,1)} %collective-permute-done.8.refs_10_.rest_12_.rest_13_.rest_10_), channel_id=1, source_target_pairs={{0,1},{1,0},{2,3},{3,2},{4,5},{5,4},{6,7},{7,6},{8,9},{9,8},{10,11... | collective-permute-start | bytes 1622024 | tf_op jit(solution)/shard_map/ppermute | solution.py:616
  61.7 1.9 collective-permute-start.14
  74.7 13.5 %collective-permute-start.15 = (bf16[48,4096]{1,0:T(8,128)(2,1)S(1)}, bf16[48,4096]{1,0:T(8,128)(2,1)S(1)}, u32[]{:S(2)}, u32[]{:S(2)}) collective-permute-start(bf16[48,4096]{1,0:T(8,128)(2,1)S(1)} %forward_layers.2), channel_id=1, source_target_pairs={{0,16},{1,17},{2,18},{3,19},{4,20},{5,21},{6,22},{7,23},{8,24},{9,... | collective-permute-start | bytes 1179656 | tf_op jit(solution)/shard_map/ppermute | solution.py:669
  86.9 21.2 %collective-permute-start.17 = (bf16[32,4096]{1,0:T(8,128)(2,1)S(1)}, bf16[32,4096]{1,0:T(8,128)(2,1)S(1)}, u32[]{:S(2)}, u32[]{:S(2)}) collective-permute-start(bf16[32,4096]{1,0:T(8,128)(2,1)S(1)} %forward_layers.3), channel_id=1, source_target_pairs={{0,16},{1,17},{2,18},{3,19},{4,20},{5,21},{6,22},{7,23},{8,24},{9,... | collective-permute-start | bytes 786440 | tf_op jit(solution)/shard_map/ppermute | solution.py:669
  106.7 19.6 %collective-permute-start.16 = (bf16[48,4096]{1,0:T(8,128)(2,1)S(1)}, bf16[48,4096]{1,0:T(8,128)(2,1)S(1)}, u32[]{:S(2)}, u32[]{:S(2)}) collective-permute-start(bf16[48,4096]{1,0:T(8,128)(2,1)S(1)} %get-tuple-element.76), channel_id=1, source_target_pairs={{16,0},{17,1},{18,2},{19,3},{20,4},{21,5},{22,6},{23,7},{24,8},{25... | collective-permute-start | bytes 1179656 | tf_op jit(solution)/shard_map/ppermute | solution.py:669
  108.0 23.7 %collective-permute-start.18 = (bf16[2,48,4096]{2,1,0:T(8,128)(2,1)S(1)}, bf16[2,48,4096]{2,1,0:T(8,128)(2,1)S(1)}, u32[]{:S(2)}, u32[]{:S(2)}) collective-permute-start(bf16[2,48,4096]{2,1,0:T(8,128)(2,1)S(1)} %get-tuple-element.74.stash.refs_0_), channel_id=1, source_target_pairs={{0,1},{1,0},{2,3},{3,2},{4,5},{5,4},{6,7},{7,6},{8,9},{9,8},{10,11... | collective-permute-start | bytes 2359304 | tf_op jit(solution)/shard_map/ppermute | solution.py:616
  124.5 7.2 %collective-permute-start.19 = (bf16[2,32,4096]{2,1,0:T(8,128)(2,1)S(1)}, bf16[2,32,4096]{2,1,0:T(8,128)(2,1)S(1)}, u32[]{:S(2)}, u32[]{:S(2)}) collective-permute-start(bf16[2,32,4096]{2,1,0:T(8,128)(2,1)S(1)} %get-tuple-element.78.refs_1_.stash), channel_id=1, source_target_pairs={{0,1},{1,0},{2,3},{3,2},{4,5},{5,4},{6,7},{7,6},{8,9},{9,8},{10,11... | collective-permute-start | bytes 1572872 | tf_op jit(solution)/shard_map/ppermute | solution.py:616
  125.0 10.4 %collective-permute-start.20 = (bf16[32,4096]{1,0:T(8,128)(2,1)S(1)}, bf16[32,4096]{1,0:T(8,128)(2,1)S(1)}, u32[]{:S(2)}, u32[]{:S(2)}) collective-permute-start(bf16[32,4096]{1,0:T(8,128)(2,1)S(1)} %get-tuple-element.80), channel_id=1, source_target_pairs={{16,0},{17,1},{18,2},{19,3},{20,4},{21,5},{22,6},{23,7},{24,8},{25... | collective-permute-start | bytes 786440 | tf_op jit(solution)/shard_map/ppermute | solution.py:669
  131.6 9.1 %collective-permute-start.21 = (bf16[2,48,4096]{2,1,0:T(8,128)(2,1)S(1)}, bf16[2,48,4096]{2,1,0:T(8,128)(2,1)S(1)}, u32[]{:S(2)}, u32[]{:S(2)}) collective-permute-start(bf16[2,48,4096]{2,1,0:T(8,128)(2,1)S(1)} %backward_layers.2.rest_0_), channel_id=1, source_target_pairs={{0,1},{1,0},{2,3},{3,2},{4,5},{5,4},{6,7},{7,6},{8,9},{9,8},{10,11... | collective-permute-start | bytes 2359304 | tf_op jit(solution)/shard_map/ppermute | solution.py:616
  140.5 2.0 collective-permute-start.22
  145.1 9.6 %collective-permute-start.23 = (bf16[256,512]{1,0:T(8,128)(2,1)S(1)}, bf16[256,512]{1,0:T(8,128)(2,1)S(1)}, u32[]{:S(2)}, u32[]{:S(2)}) collective-permute-start(bf16[256,512]{1,0:T(8,128)(2,1)S(1)} %get-tuple-element.84), channel_id=1, source_target_pairs={{0,2},{1,3},{2,6},{3,7},{6,4},{7,5},{4,0},{5,1},{8,10},{9,11},{10,... | collective-permute-start | bytes 786440 | tf_op jit(solution)/shard_map/ppermute | solution.py:613
  146.7 8.1 %collective-permute-start.24 = (bf16[256,512]{1,0:T(8,128)(2,1)S(1)}, bf16[256,512]{1,0:T(8,128)(2,1)S(1)}, u32[]{:S(2)}, u32[]{:S(2)}) collective-permute-start(bf16[256,512]{1,0:T(8,128)(2,1)S(1)} %get-tuple-element.85), channel_id=1, source_target_pairs={{0,8},{8,0},{1,9},{9,1},{2,10},{10,2},{3,11},{11,3},{4,12},{12,4},... | collective-permute-start | bytes 786440 | tf_op jit(solution)/shard_map/ppermute | solution.py:619
  154.9 14.3 %collective-permute-start.25 = (bf16[512,512]{1,0:T(8,128)(2,1)S(1)}, bf16[512,512]{1,0:T(8,128)(2,1)S(1)}, u32[]{:S(2)}, u32[]{:S(2)}) collective-permute-start(bf16[512,512]{1,0:T(8,128)(2,1)S(1)} %add_convert_fusion.4), channel_id=1, source_target_pairs={{0,2},{1,3},{2,6},{3,7},{6,4},{7,5},{4,0},{5,1},{8,10},{9,11},{10,... | collective-permute-start | bytes 1572872 | tf_op jit(solution)/shard_map/ppermute | solution.py:613
  156.3 13.1 %collective-permute-start.26 = (bf16[512,512]{1,0:T(8,128)(2,1)S(1)}, bf16[512,512]{1,0:T(8,128)(2,1)S(1)}, u32[]{:S(2)}, u32[]{:S(2)}) collective-permute-start(bf16[512,512]{1,0:T(8,128)(2,1)S(1)} %add_convert_fusion.3), channel_id=1, source_target_pairs={{0,8},{8,0},{1,9},{9,1},{2,10},{10,2},{3,11},{11,3},{4,12},{12,4},... | collective-permute-start | bytes 1572872 | tf_op jit(solution)/shard_map/ppermute | solution.py:619
  169.6 13.1 %collective-permute-start.27 = (bf16[512,512]{1,0:T(8,128)(2,1)S(1)}, bf16[512,512]{1,0:T(8,128)(2,1)S(1)}, u32[]{:S(2)}, u32[]{:S(2)}) collective-permute-start(bf16[512,512]{1,0:T(8,128)(2,1)S(1)} %add_convert_fusion.2), channel_id=1, source_target_pairs={{0,2},{1,3},{2,6},{3,7},{6,4},{7,5},{4,0},{5,1},{8,10},{9,11},{10,... | collective-permute-start | bytes 1572872 | tf_op jit(solution)/shard_map/ppermute | solution.py:613
  170.6 12.1 %collective-permute-start.28 = (bf16[512,512]{1,0:T(8,128)(2,1)S(1)}, bf16[512,512]{1,0:T(8,128)(2,1)S(1)}, u32[]{:S(2)}, u32[]{:S(2)}) collective-permute-start(bf16[512,512]{1,0:T(8,128)(2,1)S(1)} %get-tuple-element.108), channel_id=1, source_target_pairs={{0,8},{8,0},{1,9},{9,1},{2,10},{10,2},{3,11},{11,3},{4,12},{12,4},... | collective-permute-start | bytes 1572872 | tf_op jit(solution)/shard_map/ppermute | solution.py:619
  183.0 12.2 %collective-permute-start.29 = (bf16[512,512]{1,0:T(8,128)(2,1)S(1)}, bf16[512,512]{1,0:T(8,128)(2,1)S(1)}, u32[]{:S(2)}, u32[]{:S(2)}) collective-permute-start(bf16[512,512]{1,0:T(8,128)(2,1)S(1)} %add_convert_fusion.1), channel_id=1, source_target_pairs={{0,2},{1,3},{2,6},{3,7},{6,4},{7,5},{4,0},{5,1},{8,10},{9,11},{10,... | collective-permute-start | bytes 1572872 | tf_op jit(solution)/shard_map/ppermute | solution.py:613
  183.9 11.3 %collective-permute-start.30 = (bf16[512,512]{1,0:T(8,128)(2,1)S(1)}, bf16[512,512]{1,0:T(8,128)(2,1)S(1)}, u32[]{:S(2)}, u32[]{:S(2)}) collective-permute-start(bf16[512,512]{1,0:T(8,128)(2,1)S(1)} %get-tuple-element.112), channel_id=1, source_target_pairs={{0,8},{8,0},{1,9},{9,1},{2,10},{10,2},{3,11},{11,3},{4,12},{12,4},... | collective-permute-start | bytes 1572872 | tf_op jit(solution)/shard_map/ppermute | solution.py:619
  (3 other events, 19.1 us)

commit v5 on v4

--- a/solution.py
+++ b/solution.py
@@ -705,14 +705,20 @@
     early, late = order[:1], order[1:]
     first = block_grad_pass(flipped, cotangents, meta, rows, slots, ((1, tuple(early)),), True)
     cotangents, first = lax.optimization_barrier((cotangents, first))
-    jobs = ((1, tuple(late)), (0, tuple(order)))
+    jobs = tuple((role, chosen) for role, chosen in ((1, tuple(late[:1])), (0, tuple(early))) if chosen)
     grads = block_grad_pass(flipped, cotangents, meta, rows, slots, jobs)
     if places > 1:
         moving = lax.optimization_barrier((ring(first[1]), partner(first[0]), grads))
     else:
         moving = lax.optimization_barrier((partner(first[1]), partner(first[0]), grads))
     lower, upper, grads = moving
-    leaving, staying = list(grads[: len(late)]), grads[len(late) :]
+    leaving, staying = list(grads[: len(late[:1])]), [grads[-1]]
+    if places > 1:
+        cotangents, lower, upper = lax.optimization_barrier((cotangents, lower, upper))
+        jobs = tuple((role, chosen) for role, chosen in ((1, tuple(late[1:])), (0, tuple(late))) if chosen)
+        grads = block_grad_pass(flipped, cotangents, meta, rows, slots, jobs)
+        leaving += grads[: len(late[1:])]
+        staying += grads[len(late[1:]) :]
     if places > 1:
         upper = jnp.concatenate([upper, jnp.zeros_like(lower)], axis=0)
         travelling = add_rounded(staying[0], upper)
@@ -721,9 +727,7 @@
         travelling = add_rounded(staying[0], jnp.concatenate([upper, lower], axis=0))
     for index in range(places - 1):
         kept, outgoing = staying[index + 1], leaving[index]
-        passed, coming, leaving = lax.optimization_barrier(
-            (ring(travelling), partner(outgoing), leaving)
-        )
+        passed, coming = lax.optimization_barrier((ring(travelling), partner(outgoing)))
         total = kept.astype(jnp.float32) + coming.astype(jnp.float32) + passed.astype(jnp.float32)
         travelling = total.astype(jnp.bfloat16)
     travelling = jnp.where(live, travelling, jnp.zeros_like(travelling))

time: 198 us -> 196 us (0.990)
  waiting for transfers between devices: 74 us -> 68.5 us
  Pallas kernels: 77.1 us -> 80.7 us
    ppermute x7, waiting for transfers between devices: 58.7 us -> 34.8 us  [ring(): return lax.ppermute(array, 'dp', hops)]
    ppermute x8, waiting for transfers between devices: 12 us -> 30.3 us  [partner(): lax.ppermute(array, 'side', [(i, sides - 1 - i) for i in range(sides)])]
    pallas_call x2 -> x3, Pallas kernels: 9.1 us -> 12.8 us  [block_grad_pass(): pl.pallas_call(functools.partial(block_grad_kernel, rows, slots, jobs, ha...]
  transfers between devices with their start and end apart: 31 -> 31, of which waited for: 15 -> 17; matrix products, arithmetic and copies ran while one was open for 2% -> 3% of each run, Pallas kernels for 32% -> 34%
where the time goes in v5:
time: 196 us
  Pallas kernels  80.7 us (41%)
  waiting for transfers between devices  68.5 us (35%)
  starting transfers between devices  33.3 us (17%)
  local copies, waits for them, and re-layouts  10 us (5%)
  other arithmetic  2.69 us (1%)
    pallas_call x4, Pallas kernels, forward_pass(): pl.pallas_call(functools.partial(forward_kernel, rows, slots, len(straigh...  53.6 us
    ppermute x7, waiting for transfers between devices, ring(): return lax.ppermute(array, 'dp', hops)  34.8 us
    ppermute x8, waiting for transfers between devices, partner(): lax.ppermute(array, 'side', [(i, sides - 1 - i) for i in range(sides)])  30.3 us
    pallas_call x3, Pallas kernels, block_grad_pass(): pl.pallas_call(functools.partial(block_grad_kernel, rows, slots, jobs, ha...  12.8 us
    ppermute x7, starting transfers between devices, ring(): return lax.ppermute(array, 'dp', hops)  12.6 us
    ppermute x8, starting transfers between devices, partner(): lax.ppermute(array, 'side', [(i, sides - 1 - i) for i in range(sides)])  11.1 us
    pallas_call x2, Pallas kernels, backward_pass(): pl.pallas_call(functools.partial(backward_kernel, rows, slots, len(across...  10.3 us
    ppermute x4, starting transfers between devices, hop(): return lax.ppermute(array, 'stage', route)  7.32 us
  transfers between devices with their start and end apart: 31, of which 17 were waited for; matrix products, arithmetic and copies ran while one was open for 3% of the time, Pallas kernels for 34%

profile of v5, /device:TPU:0, one launch (start us, length us, event | category | flops | bytes accessed | tf_op | source)
XLA Modules:
  0.0 195.6 jit_solution(14057573760771065307)
XLA Ops:
  0.9 2.1 %reshape_squeeze.4 = bf16[8,8,64,64]{3,2,1,0:T(8,128)(2,1)S(1)} reshape(bf16[1,8,8,4096]{3,2,1,0:T(8,128)(2,1)} %param.9) | data formatting | bytes 1048576 | tf_op jit(solution)/shard_map/reshape;squeeze | solution.py:570
  4.7 3.1 %collective-permute-start = (bf16[528,512]{1,0:T(8,128)(2,1)S(1)}, bf16[528,512]{1,0:T(8,128)(2,1)S(1)}, u32[]{:S(2)}, u32[]{:S(2)}) collective-permute-start(bf16[528,512]{1,0:T(8,128)(2,1)S(1)} %fusion.3.refs_0_.rest_2_.rest_3_.rest_0_), channel_id=1, source_target_pairs={{0,2},{1,3},{2,6},{3,7},{6,4},{7,5},{4,0},{5,1},{8,10},{9,11},{10,... | collective-permute-start | bytes 1622024 | tf_op jit(solution)/shard_map/ppermute | solution.py:613
  10.5 10.5 %collective-permute-done.refs_1_.rest_3_.rest_4_.rest_1_ = bf16[528,512]{1,0:T(8,128)(2,1)S(1)} collective-permute-done((bf16[528,512]{1,0:T(8,128)(2,1)S(1)}, bf16[528,512]{1,0:T(8,128)(2,1)S(1)}, u32[]{:S(2)}, u32[]{:S(2)}) %collective-permute-start) | collective-permute-done | bytes 540704 | tf_op jit(solution)/shard_map/ppermute | solution.py:613
  21.5 2.6 %collective-permute-start.3 = (bf16[528,512]{1,0:T(8,128)(2,1)S(1)}, bf16[528,512]{1,0:T(8,128)(2,1)}, u32[]{:S(2)}, u32[]{:S(2)}) collective-permute-start(bf16[528,512]{1,0:T(8,128)(2,1)S(1)} %collective-permute-done.refs_1_.rest_3_.rest_4_.rest_1_), channel_id=1, source_target_pairs={{0,2},{1,3},{2,6},{3,7},{6,4},{7,5},{4,0},{5,1},{8,10},{9,11},{10,... | collective-permute-start | bytes 1622024 | tf_op jit(solution)/shard_map/ppermute | solution.py:613
  27.5 8.1 %collective-permute-done.3.refs_2_.rest_4_.rest_5_.rest_2_ = bf16[528,512]{1,0:T(8,128)(2,1)} collective-permute-done((bf16[528,512]{1,0:T(8,128)(2,1)S(1)}, bf16[528,512]{1,0:T(8,128)(2,1)}, u32[]{:S(2)}, u32[]{:S(2)}) %collective-permute-start.3) | collective-permute-done | bytes 540704 | tf_op jit(solution)/shard_map/ppermute | solution.py:613
  36.8 1.5 collective-permute-start.7
  41.3 8.4 %collective-permute-done.7.refs_3_.rest_5_.rest_6_.rest_3_ = bf16[528,512]{1,0:T(8,128)(2,1)} collective-permute-done((bf16[528,512]{1,0:T(8,128)(2,1)}, bf16[528,512]{1,0:T(8,128)(2,1)}, u32[]{:S(2)}, u32[]{:S(2)}) %collective-permute-start.7) | collective-permute-done | bytes 540704 | tf_op jit(solution)/shard_map/ppermute | solution.py:613
  50.7 1.5 collective-permute-start.11
  52.8 8.9 %collective-permute-done.11.refs_11_.rest_13_.rest_14_.rest_11_ = bf16[528,512]{1,0:T(8,128)(2,1)S(1)} collective-permute-done((bf16[528,512]{1,0:T(8,128)(2,1)}, bf16[528,512]{1,0:T(8,128)(2,1)S(1)}, u32[]{:S(2)}, u32[]{:S(2)}) %collective-permute-start.11) | collective-permute-done | bytes 540704 | tf_op jit(solution)/shard_map/ppermute | solution.py:619
  64.7 10.0 %forward_layers.3 = bf16[48,4096]{1,0:T(8,128)(2,1)S(1)} custom-call(s32[16,128]{1,0:T(8,128)S(1)} %list_columns.1.cols, s32[8]{0:T(128)S(1)} %add_multiply_fusion.bases, s32[3]{0:T(128)S(1)} %pad_add_fusion.flags, bf16[48,4096]{1,0:T(8,128)(2,1)S(1)} %constant_dynamic-slice_fusion.3.rest_0_.rest_1_, ...), custom_call_target="tpu_custom_call" | custom-call | flops 8800000000 | bytes 1048576 | tf_op jit(solution)/shard_map/forward_layers/pallas_call | solution.py:353
  74.7 3.4 %collective-permute-start.16 = (bf16[48,4096]{1,0:T(8,128)(2,1)S(1)}, bf16[48,4096]{1,0:T(8,128)(2,1)S(1)}, u32[]{:S(2)}, u32[]{:S(2)}) collective-permute-start(bf16[48,4096]{1,0:T(8,128)(2,1)S(1)} %forward_layers.3), channel_id=1, source_target_pairs={{0,16},{1,17},{2,18},{3,19},{4,20},{5,21},{6,22},{7,23},{8,24},{9,... | collective-permute-start | bytes 1179656 | tf_op jit(solution)/shard_map/ppermute | solution.py:669
  78.2 8.7 %forward_layers.2 = bf16[32,4096]{1,0:T(8,128)(2,1)S(1)} custom-call(s32[16,128]{1,0:T(8,128)S(1)} %list_columns.1.cols, s32[8]{0:T(128)S(1)} %add_multiply_fusion.bases, s32[3]{0:T(128)S(1)} %pad_add_fusion.flags, bf16[32,4096]{1,0:T(8,128)(2,1)S(1)} %copy-done.1, bf16[32,4096]{1,0:T(8,128)(2,1)S(1)} %copy-done.1, ...), custom_call_target="tpu_custom_call" | custom-call | flops 8800000000 | bytes 1048576 | tf_op jit(solution)/shard_map/forward_layers/pallas_call | solution.py:353
  88.2 18.5 %turning_layers.3 = (bf16[2,48,4096]{2,1,0:T(8,128)(2,1)S(1)}, bf16[48,4096]{1,0:T(8,128)(2,1)S(1)}, bf16[48,4096]{1,0:T(8,128)(2,1)S(1)}) custom-call(s32[16,128]{1,0:T(8,128)S(1)} %list_columns.1.cols, s32[8]{0:T(128)S(1)} %add_multiply_fusion.bases, s32[3]{0:T(128)S(1)} %pad_add_fusion.flags, ...), custom_call_target="tpu_custom_call" | custom-call | flops 15399999488 | bytes 1048576 | tf_op jit(solution)/shard_map/turning_layers/pallas_call | solution.py:353
  108.0 16.4 %turning_layers.2 = (bf16[2,32,4096]{2,1,0:T(8,128)(2,1)S(1)}, bf16[32,4096]{1,0:T(8,128)(2,1)S(1)}, bf16[32,4096]{1,0:T(8,128)(2,1)S(1)}) custom-call(s32[16,128]{1,0:T(8,128)S(1)} %list_columns.1.cols, s32[8]{0:T(128)S(1)} %add_multiply_fusion.bases, s32[3]{0:T(128)S(1)} %pad_add_fusion.flags, bf16[32,4096]{1,0:T(8,128)(2,1)S(1)} %copy-done.1, ...), custom_call_target="tpu_custom_call" | custom-call | flops 15399999488 | bytes 1048576 | tf_op jit(solution)/shard_map/turning_layers/pallas_call | solution.py:353
  126.3 5.2 %backward_layers.2.rest_0_ = bf16[2,48,4096]{2,1,0:T(8,128)(2,1)S(1)} custom-call(s32[16,128]{1,0:T(8,128)S(1)} %list_columns.1.cols, s32[8]{0:T(128)S(1)} %add_multiply_fusion.bases, s32[3]{0:T(128)S(1)} %pad_add_fusion.flags, bf16[2,48,4096]{2,1,0:T(8,128)(2,1)S(1)} %get-tuple-element.73.refs_0_.stash, bf16[48,4096]{1,0:T(8,128)(2,1)S(1)} %get-tuple-element.75.loss_grad, ...), custom_call_target="tpu_custom_call" | custom-call | flops 4400000000 | bytes 1048576 | tf_op jit(solution)/shard_map/backward_layers/pallas_call | solution.py:400
  131.7 3.1 %flip_rows.1.turned = bf16[2,32,64,160]{3,2,1,0:T(8,128)(2,1)S(1)} custom-call(s32[8]{0:T(128)S(1)} %add_multiply_fusion.bases, bf16[2,48,4096]{2,1,0:T(8,128)(2,1)S(1)} %get-tuple-element.73.refs_0_.stash, bf16[2,32,4096]{2,1,0:T(8,128)(2,1)S(1)} %get-tuple-element.77.refs_1_.stash, bf16[2,48,4096]{2,1,0:T(8,128)(2,1)S(1)} %collective-permute-done.17.refs_2_, ...), custom_call_target="tpu_custom_call" | custom-call | flops 4400000000 | bytes 1048576 | tf_op jit(solution)/shard_map/flip_rows/pallas_call | solution.py:459
  135.4 5.1 %backward_layers.3.rest_1_ = bf16[2,32,4096]{2,1,0:T(8,128)(2,1)S(1)} custom-call(s32[16,128]{1,0:T(8,128)S(1)} %list_columns.1.cols, s32[8]{0:T(128)S(1)} %add_multiply_fusion.bases, s32[3]{0:T(128)S(1)} %pad_add_fusion.flags, bf16[2,32,4096]{2,1,0:T(8,128)(2,1)S(1)} %get-tuple-element.77.refs_1_.stash, bf16[32,4096]{1,0:T(8,128)(2,1)S(1)} %get-tuple-element.78.loss_grad, ...), custom_call_target="tpu_custom_call" | custom-call | flops 4400000000 | bytes 1048576 | tf_op jit(solution)/shard_map/backward_layers/pallas_call | solution.py:400
  140.6 1.9 collective-permute-done.22.rest_3_
  142.5 2.6 %block_grads.3 = (bf16[256,512]{1,0:T(8,128)(2,1)S(1)}, bf16[256,512]{1,0:T(8,128)(2,1)S(1)}) custom-call(s32[16,128]{1,0:T(8,128)S(1)} %list_columns.1.cols, s32[3]{0:T(128)S(1)} %pad_add_fusion.flags, bf16[2,32,64,160]{3,2,1,0:T(8,128)(2,1)S(1)} %flip_rows.1.turned, bf16[2,48,4096]{2,1,0:T(8,128)(2,1)S(1)} %backward_layers.2.rest_0_, ...), custom_call_target="tpu_custom_call" | custom-call | flops 3300000000 | bytes 1048576 | tf_op jit(solution)/shard_map/block_grads/pallas_call | solution.py:512
  145.1 1.6 collective-permute-start.23
  146.7 1.5 collective-permute-start.24
  148.2 4.5 %block_grads.4 = (bf16[512,512]{1,0:T(8,128)(2,1)S(1)}, bf16[512,512]{1,0:T(8,128)(2,1)S(1)}) custom-call(s32[16,128]{1,0:T(8,128)S(1)} %list_columns.1.cols, s32[3]{0:T(128)S(1)} %pad_add_fusion.flags, bf16[2,32,64,160]{3,2,1,0:T(8,128)(2,1)S(1)} %flip_rows.1.turned, bf16[2,48,4096]{2,1,0:T(8,128)(2,1)S(1)} %backward_layers.2.rest_0_, ...), custom_call_target="tpu_custom_call" | custom-call | flops 4400000000 | bytes 1048576 | tf_op jit(solution)/shard_map/block_grads/pallas_call | solution.py:512
  152.7 1.8 collective-permute-done.23
  156.3 1.6 collective-permute-start.26
  157.8 5.7 %block_grads.5 = (bf16[512,512]{1,0:T(8,128)(2,1)S(1)}, bf16[512,512]{1,0:T(8,128)(2,1)S(1)}, bf16[512,512]{1,0:T(8,128)(2,1)S(1)}, bf16[512,512]{1,0:T(8,128)(2,1)S(1)}, bf16[512,512]{1,0:T(8,128)(2,1)S(1)}) custom-call(s32[16,128]{1,0:T(8,128)S(1)} %list_columns.1.cols, s32[3]{0:T(128)S(1)} %pad_add_fusion.flags, ...), custom_call_target="tpu_custom_call" | custom-call | flops 5500000256 | bytes 1048576 | tf_op jit(solution)/shard_map/block_grads/pallas_call | solution.py:512
  164.1 4.5 %collective-permute-done.25 = bf16[512,512]{1,0:T(8,128)(2,1)S(1)} collective-permute-done((bf16[512,512]{1,0:T(8,128)(2,1)S(1)}, bf16[512,512]{1,0:T(8,128)(2,1)S(1)}, u32[]{:S(2)}, u32[]{:S(2)}) %collective-permute-start.25) | collective-permute-done | bytes 524320 | tf_op jit(solution)/shard_map/ppermute | solution.py:613
  168.6 2.6 %collective-permute-done.26 = bf16[512,512]{1,0:T(8,128)(2,1)S(1)} collective-permute-done((bf16[512,512]{1,0:T(8,128)(2,1)S(1)}, bf16[512,512]{1,0:T(8,128)(2,1)S(1)}, u32[]{:S(2)}, u32[]{:S(2)}) %collective-permute-start.26) | collective-permute-done | bytes 524320 | tf_op jit(solution)/shard_map/ppermute | solution.py:619
  172.6 1.5 collective-permute-start.30
  174.1 8.3 %collective-permute-done.28 = bf16[512,512]{1,0:T(8,128)(2,1)S(1)} collective-permute-done((bf16[512,512]{1,0:T(8,128)(2,1)S(1)}, bf16[512,512]{1,0:T(8,128)(2,1)S(1)}, u32[]{:S(2)}, u32[]{:S(2)}) %collective-permute-start.28) | collective-permute-done | bytes 524320 | tf_op jit(solution)/shard_map/ppermute | solution.py:619
  183.9 7.5 %collective-permute-done.30 = bf16[512,512]{1,0:T(8,128)(2,1)S(1)} collective-permute-done((bf16[512,512]{1,0:T(8,128)(2,1)S(1)}, bf16[512,512]{1,0:T(8,128)(2,1)S(1)}, u32[]{:S(2)}, u32[]{:S(2)}) %collective-permute-start.30) | collective-permute-done | bytes 524320 | tf_op jit(solution)/shard_map/ppermute | solution.py:619
  191.4 1.6 collective-permute-done.29
  194.0 1.6 broadcast_in_dim_reshape.3
  (79 shorter events, 29.7 us)
Async XLA Ops:
  0.0 26.8 %copy-start = (bf16[2,80,4096]{2,1,0:T(8,128)(2,1)S(1)}, bf16[2,80,4096]{2,1,0:T(8,128)(2,1)}, u32[]{:S(2)}) copy-start(bf16[2,80,4096]{2,1,0:T(8,128)(2,1)} %param.7) | copy-start | bytes 3932164
  4.7 16.4 %collective-permute-start = (bf16[528,512]{1,0:T(8,128)(2,1)S(1)}, bf16[528,512]{1,0:T(8,128)(2,1)S(1)}, u32[]{:S(2)}, u32[]{:S(2)}) collective-permute-start(bf16[528,512]{1,0:T(8,128)(2,1)S(1)} %fusion.3.refs_0_.rest_2_.rest_3_.rest_0_), channel_id=1, source_target_pairs={{0,2},{1,3},{2,6},{3,7},{6,4},{7,5},{4,0},{5,1},{8,10},{9,11},{10,... | collective-permute-start | bytes 1622024 | tf_op jit(solution)/shard_map/ppermute | solution.py:613
  7.8 13.7 %collective-permute-start.1 = (bf16[528,512]{1,0:T(8,128)(2,1)S(1)}, bf16[528,512]{1,0:T(8,128)(2,1)S(1)}, u32[]{:S(2)}, u32[]{:S(2)}) collective-permute-start(bf16[528,512]{1,0:T(8,128)(2,1)S(1)} %fusion.3.refs_0_.rest_2_.rest_3_.rest_0_), channel_id=1, source_target_pairs={{0,8},{8,0},{1,9},{9,1},{2,10},{10,2},{3,11},{11,3},{4,12},{12,4},... | collective-permute-start | bytes 1622024 | tf_op jit(solution)/shard_map/ppermute | solution.py:619
  9.3 12.2 %collective-permute-start.2 = (bf16[528,512]{1,0:T(8,128)(2,1)S(1)}, bf16[528,512]{1,0:T(8,128)(2,1)S(1)}, u32[]{:S(2)}, u32[]{:S(2)}) collective-permute-start(bf16[528,512]{1,0:T(8,128)(2,1)S(1)} %fusion.3.refs_0_.rest_2_.rest_3_.rest_0_), channel_id=1, source_target_pairs={{0,1},{1,0},{2,3},{3,2},{4,5},{5,4},{6,7},{7,6},{8,9},{9,8},{10,11... | collective-permute-start | bytes 1622024 | tf_op jit(solution)/shard_map/ppermute | solution.py:616
  21.5 14.0 %collective-permute-start.3 = (bf16[528,512]{1,0:T(8,128)(2,1)S(1)}, bf16[528,512]{1,0:T(8,128)(2,1)}, u32[]{:S(2)}, u32[]{:S(2)}) collective-permute-start(bf16[528,512]{1,0:T(8,128)(2,1)S(1)} %collective-permute-done.refs_1_.rest_3_.rest_4_.rest_1_), channel_id=1, source_target_pairs={{0,2},{1,3},{2,6},{3,7},{6,4},{7,5},{4,0},{5,1},{8,10},{9,11},{10,... | collective-permute-start | bytes 1622024 | tf_op jit(solution)/shard_map/ppermute | solution.py:613
  24.1 12.7 %collective-permute-start.4 = (bf16[528,512]{1,0:T(8,128)(2,1)S(1)}, bf16[528,512]{1,0:T(8,128)(2,1)}, u32[]{:S(2)}, u32[]{:S(2)}) collective-permute-start(bf16[528,512]{1,0:T(8,128)(2,1)S(1)} %collective-permute-done.refs_1_.rest_3_.rest_4_.rest_1_), channel_id=1, source_target_pairs={{0,8},{8,0},{1,9},{9,1},{2,10},{10,2},{3,11},{11,3},{4,12},{12,4},... | collective-permute-start | bytes 1622024 | tf_op jit(solution)/shard_map/ppermute | solution.py:619
  25.6 11.2 %collective-permute-start.6 = (bf16[528,512]{1,0:T(8,128)(2,1)S(1)}, bf16[528,512]{1,0:T(8,128)(2,1)}, u32[]{:S(2)}, u32[]{:S(2)}) collective-permute-start(bf16[528,512]{1,0:T(8,128)(2,1)S(1)} %collective-permute-done.refs_1_.rest_3_.rest_4_.rest_1_), channel_id=1, source_target_pairs={{0,1},{1,0},{2,3},{3,2},{4,5},{5,4},{6,7},{7,6},{8,9},{9,8},{10,11... | collective-permute-start | bytes 1622024 | tf_op jit(solution)/shard_map/ppermute | solution.py:616
  25.6 11.2 %collective-permute-start.5 = (bf16[528,512]{1,0:T(8,128)(2,1)S(1)}, bf16[528,512]{1,0:T(8,128)(2,1)}, u32[]{:S(2)}, u32[]{:S(2)}) collective-permute-start(bf16[528,512]{1,0:T(8,128)(2,1)S(1)} %collective-permute-done.1.refs_8_.rest_10_.rest_11_.rest_8_), channel_id=1, source_target_pairs={{0,1},{1,0},{2,3},{3,2},{4,5},{5,4},{6,7},{7,6},{8,9},{9,8},{10,11... | collective-permute-start | bytes 1622024 | tf_op jit(solution)/shard_map/ppermute | solution.py:616
  36.8 12.8 %collective-permute-start.7 = (bf16[528,512]{1,0:T(8,128)(2,1)}, bf16[528,512]{1,0:T(8,128)(2,1)}, u32[]{:S(2)}, u32[]{:S(2)}) collective-permute-start(bf16[528,512]{1,0:T(8,128)(2,1)} %collective-permute-done.3.refs_2_.rest_4_.rest_5_.rest_2_), channel_id=1, source_target_pairs={{0,2},{1,3},{2,6},{3,7},{6,4},{7,5},{4,0},{5,1},{8,10},{9,11},{10,... | collective-permute-start | bytes 1622024 | tf_op jit(solution)/shard_map/ppermute | solution.py:613
  38.3 12.4 %collective-permute-start.8 = (bf16[528,512]{1,0:T(8,128)(2,1)}, bf16[528,512]{1,0:T(8,128)(2,1)}, u32[]{:S(2)}, u32[]{:S(2)}) collective-permute-start(bf16[528,512]{1,0:T(8,128)(2,1)} %collective-permute-done.3.refs_2_.rest_4_.rest_5_.rest_2_), channel_id=1, source_target_pairs={{0,8},{8,0},{1,9},{9,1},{2,10},{10,2},{3,11},{11,3},{4,12},{12,4},... | collective-permute-start | bytes 1622024 | tf_op jit(solution)/shard_map/ppermute | solution.py:619
  39.8 10.9 %collective-permute-start.10 = (bf16[528,512]{1,0:T(8,128)(2,1)}, bf16[528,512]{1,0:T(8,128)(2,1)}, u32[]{:S(2)}, u32[]{:S(2)}) collective-permute-start(bf16[528,512]{1,0:T(8,128)(2,1)} %collective-permute-done.3.refs_2_.rest_4_.rest_5_.rest_2_), channel_id=1, source_target_pairs={{0,1},{1,0},{2,3},{3,2},{4,5},{5,4},{6,7},{7,6},{8,9},{9,8},{10,11... | collective-permute-start | bytes 1622024 | tf_op jit(solution)/shard_map/ppermute | solution.py:616
  39.8 10.9 %collective-permute-start.9 = (bf16[528,512]{1,0:T(8,128)(2,1)}, bf16[528,512]{1,0:T(8,128)(2,1)}, u32[]{:S(2)}, u32[]{:S(2)}) collective-permute-start(bf16[528,512]{1,0:T(8,128)(2,1)} %collective-permute-done.4.refs_9_.rest_11_.rest_12_.rest_9_), channel_id=1, source_target_pairs={{0,1},{1,0},{2,3},{3,2},{4,5},{5,4},{6,7},{7,6},{8,9},{9,8},{10,11... | collective-permute-start | bytes 1622024 | tf_op jit(solution)/shard_map/ppermute | solution.py:616
  50.7 11.0 %collective-permute-start.11 = (bf16[528,512]{1,0:T(8,128)(2,1)}, bf16[528,512]{1,0:T(8,128)(2,1)S(1)}, u32[]{:S(2)}, u32[]{:S(2)}) collective-permute-start(bf16[528,512]{1,0:T(8,128)(2,1)} %collective-permute-done.7.refs_3_.rest_5_.rest_6_.rest_3_), channel_id=1, source_target_pairs={{0,8},{8,0},{1,9},{9,1},{2,10},{10,2},{3,11},{11,3},{4,12},{12,4},... | collective-permute-start | bytes 1622024 | tf_op jit(solution)/shard_map/ppermute | solution.py:619
  52.2 9.5 %collective-permute-start.13 = (bf16[528,512]{1,0:T(8,128)(2,1)}, bf16[528,512]{1,0:T(8,128)(2,1)S(1)}, u32[]{:S(2)}, u32[]{:S(2)}) collective-permute-start(bf16[528,512]{1,0:T(8,128)(2,1)} %collective-permute-done.7.refs_3_.rest_5_.rest_6_.rest_3_), channel_id=1, source_target_pairs={{0,1},{1,0},{2,3},{3,2},{4,5},{5,4},{6,7},{7,6},{8,9},{9,8},{10,11... | collective-permute-start | bytes 1622024 | tf_op jit(solution)/shard_map/ppermute | solution.py:616
  52.2 9.5 %collective-permute-start.12 = (bf16[528,512]{1,0:T(8,128)(2,1)}, bf16[528,512]{1,0:T(8,128)(2,1)S(1)}, u32[]{:S(2)}, u32[]{:S(2)}) collective-permute-start(bf16[528,512]{1,0:T(8,128)(2,1)} %collective-permute-done.8.refs_10_.rest_12_.rest_13_.rest_10_), channel_id=1, source_target_pairs={{0,1},{1,0},{2,3},{3,2},{4,5},{5,4},{6,7},{7,6},{8,9},{9,8},{10,11... | collective-permute-start | bytes 1622024 | tf_op jit(solution)/shard_map/ppermute | solution.py:616
  61.7 1.9 collective-permute-start.14
  74.7 13.5 %collective-permute-start.16 = (bf16[48,4096]{1,0:T(8,128)(2,1)S(1)}, bf16[48,4096]{1,0:T(8,128)(2,1)S(1)}, u32[]{:S(2)}, u32[]{:S(2)}) collective-permute-start(bf16[48,4096]{1,0:T(8,128)(2,1)S(1)} %forward_layers.3), channel_id=1, source_target_pairs={{0,16},{1,17},{2,18},{3,19},{4,20},{5,21},{6,22},{7,23},{8,24},{9,... | collective-permute-start | bytes 1179656 | tf_op jit(solution)/shard_map/ppermute | solution.py:669
  86.9 21.2 %collective-permute-start.15 = (bf16[32,4096]{1,0:T(8,128)(2,1)S(1)}, bf16[32,4096]{1,0:T(8,128)(2,1)S(1)}, u32[]{:S(2)}, u32[]{:S(2)}) collective-permute-start(bf16[32,4096]{1,0:T(8,128)(2,1)S(1)} %forward_layers.2), channel_id=1, source_target_pairs={{0,16},{1,17},{2,18},{3,19},{4,20},{5,21},{6,22},{7,23},{8,24},{9,... | collective-permute-start | bytes 786440 | tf_op jit(solution)/shard_map/ppermute | solution.py:669
  106.7 19.7 %collective-permute-start.19 = (bf16[48,4096]{1,0:T(8,128)(2,1)S(1)}, bf16[48,4096]{1,0:T(8,128)(2,1)S(1)}, u32[]{:S(2)}, u32[]{:S(2)}) collective-permute-start(bf16[48,4096]{1,0:T(8,128)(2,1)S(1)} %get-tuple-element.76), channel_id=1, source_target_pairs={{16,0},{17,1},{18,2},{19,3},{20,4},{21,5},{22,6},{23,7},{24,8},{25... | collective-permute-start | bytes 1179656 | tf_op jit(solution)/shard_map/ppermute | solution.py:669
  108.0 23.7 %collective-permute-start.17 = (bf16[2,48,4096]{2,1,0:T(8,128)(2,1)S(1)}, bf16[2,48,4096]{2,1,0:T(8,128)(2,1)S(1)}, u32[]{:S(2)}, u32[]{:S(2)}) collective-permute-start(bf16[2,48,4096]{2,1,0:T(8,128)(2,1)S(1)} %get-tuple-element.73.refs_0_.stash), channel_id=1, source_target_pairs={{0,1},{1,0},{2,3},{3,2},{4,5},{5,4},{6,7},{7,6},{8,9},{9,8},{10,11... | collective-permute-start | bytes 2359304 | tf_op jit(solution)/shard_map/ppermute | solution.py:616
  124.5 7.2 %collective-permute-start.18 = (bf16[2,32,4096]{2,1,0:T(8,128)(2,1)S(1)}, bf16[2,32,4096]{2,1,0:T(8,128)(2,1)S(1)}, u32[]{:S(2)}, u32[]{:S(2)}) collective-permute-start(bf16[2,32,4096]{2,1,0:T(8,128)(2,1)S(1)} %get-tuple-element.77.refs_1_.stash), channel_id=1, source_target_pairs={{0,1},{1,0},{2,3},{3,2},{4,5},{5,4},{6,7},{7,6},{8,9},{9,8},{10,11... | collective-permute-start | bytes 1572872 | tf_op jit(solution)/shard_map/ppermute | solution.py:616
  125.0 10.4 %collective-permute-start.20 = (bf16[32,4096]{1,0:T(8,128)(2,1)S(1)}, bf16[32,4096]{1,0:T(8,128)(2,1)S(1)}, u32[]{:S(2)}, u32[]{:S(2)}) collective-permute-start(bf16[32,4096]{1,0:T(8,128)(2,1)S(1)} %get-tuple-element.79), channel_id=1, source_target_pairs={{16,0},{17,1},{18,2},{19,3},{20,4},{21,5},{22,6},{23,7},{24,8},{25... | collective-permute-start | bytes 786440 | tf_op jit(solution)/shard_map/ppermute | solution.py:669
  131.5 9.1 %collective-permute-start.21 = (bf16[2,48,4096]{2,1,0:T(8,128)(2,1)S(1)}, bf16[2,48,4096]{2,1,0:T(8,128)(2,1)S(1)}, u32[]{:S(2)}, u32[]{:S(2)}) collective-permute-start(bf16[2,48,4096]{2,1,0:T(8,128)(2,1)S(1)} %backward_layers.2.rest_0_), channel_id=1, source_target_pairs={{0,1},{1,0},{2,3},{3,2},{4,5},{5,4},{6,7},{7,6},{8,9},{9,8},{10,11... | collective-permute-start | bytes 2359304 | tf_op jit(solution)/shard_map/ppermute | solution.py:616
  140.5 2.0 %collective-permute-start.22 = (bf16[2,32,4096]{2,1,0:T(8,128)(2,1)S(1)}, bf16[2,32,4096]{2,1,0:T(8,128)(2,1)S(1)}, u32[]{:S(2)}, u32[]{:S(2)}) collective-permute-start(bf16[2,32,4096]{2,1,0:T(8,128)(2,1)S(1)} %backward_layers.3.rest_1_), channel_id=1, source_target_pairs={{0,1},{1,0},{2,3},{3,2},{4,5},{5,4},{6,7},{7,6},{8,9},{9,8},{10,11... | collective-permute-start | bytes 1572872 | tf_op jit(solution)/shard_map/ppermute | solution.py:616
  145.1 9.3 %collective-permute-start.23 = (bf16[256,512]{1,0:T(8,128)(2,1)S(1)}, bf16[256,512]{1,0:T(8,128)(2,1)S(1)}, u32[]{:S(2)}, u32[]{:S(2)}) collective-permute-start(bf16[256,512]{1,0:T(8,128)(2,1)S(1)} %get-tuple-element.86), channel_id=1, source_target_pairs={{0,2},{1,3},{2,6},{3,7},{6,4},{7,5},{4,0},{5,1},{8,10},{9,11},{10,... | collective-permute-start | bytes 786440 | tf_op jit(solution)/shard_map/ppermute | solution.py:613
  146.7 8.1 %collective-permute-start.24 = (bf16[256,512]{1,0:T(8,128)(2,1)S(1)}, bf16[256,512]{1,0:T(8,128)(2,1)S(1)}, u32[]{:S(2)}, u32[]{:S(2)}) collective-permute-start(bf16[256,512]{1,0:T(8,128)(2,1)S(1)} %get-tuple-element.87), channel_id=1, source_target_pairs={{0,8},{8,0},{1,9},{9,1},{2,10},{10,2},{3,11},{11,3},{4,12},{12,4},... | collective-permute-start | bytes 786440 | tf_op jit(solution)/shard_map/ppermute | solution.py:619
  154.8 13.8 %collective-permute-start.25 = (bf16[512,512]{1,0:T(8,128)(2,1)S(1)}, bf16[512,512]{1,0:T(8,128)(2,1)S(1)}, u32[]{:S(2)}, u32[]{:S(2)}) collective-permute-start(bf16[512,512]{1,0:T(8,128)(2,1)S(1)} %add_convert_fusion.4), channel_id=1, source_target_pairs={{0,2},{1,3},{2,6},{3,7},{6,4},{7,5},{4,0},{5,1},{8,10},{9,11},{10,... | collective-permute-start | bytes 1572872 | tf_op jit(solution)/shard_map/ppermute | solution.py:613
  156.3 14.9 %collective-permute-start.26 = (bf16[512,512]{1,0:T(8,128)(2,1)S(1)}, bf16[512,512]{1,0:T(8,128)(2,1)S(1)}, u32[]{:S(2)}, u32[]{:S(2)}) collective-permute-start(bf16[512,512]{1,0:T(8,128)(2,1)S(1)} %add_convert_fusion.3), channel_id=1, source_target_pairs={{0,8},{8,0},{1,9},{9,1},{2,10},{10,2},{3,11},{11,3},{4,12},{12,4},... | collective-permute-start | bytes 1572872 | tf_op jit(solution)/shard_map/ppermute | solution.py:619
  163.5 18.9 %collective-permute-start.28 = (bf16[512,512]{1,0:T(8,128)(2,1)S(1)}, bf16[512,512]{1,0:T(8,128)(2,1)S(1)}, u32[]{:S(2)}, u32[]{:S(2)}) collective-permute-start(bf16[512,512]{1,0:T(8,128)(2,1)S(1)} %get-tuple-element.105), channel_id=1, source_target_pairs={{0,8},{8,0},{1,9},{9,1},{2,10},{10,2},{3,11},{11,3},{4,12},{12,4},... | collective-permute-start | bytes 1572872 | tf_op jit(solution)/shard_map/ppermute | solution.py:619
  171.4 11.0 %collective-permute-start.27 = (bf16[512,512]{1,0:T(8,128)(2,1)S(1)}, bf16[512,512]{1,0:T(8,128)(2,1)S(1)}, u32[]{:S(2)}, u32[]{:S(2)}) collective-permute-start(bf16[512,512]{1,0:T(8,128)(2,1)S(1)} %add_convert_fusion.2), channel_id=1, source_target_pairs={{0,2},{1,3},{2,6},{3,7},{6,4},{7,5},{4,0},{5,1},{8,10},{9,11},{10,... | collective-permute-start | bytes 1572872 | tf_op jit(solution)/shard_map/ppermute | solution.py:613
  172.6 18.7 %collective-permute-start.30 = (bf16[512,512]{1,0:T(8,128)(2,1)S(1)}, bf16[512,512]{1,0:T(8,128)(2,1)S(1)}, u32[]{:S(2)}, u32[]{:S(2)}) collective-permute-start(bf16[512,512]{1,0:T(8,128)(2,1)S(1)} %get-tuple-element.108), channel_id=1, source_target_pairs={{0,8},{8,0},{1,9},{9,1},{2,10},{10,2},{3,11},{11,3},{4,12},{12,4},... | collective-permute-start | bytes 1572872 | tf_op jit(solution)/shard_map/ppermute | solution.py:619
  182.7 10.3 %collective-permute-start.29 = (bf16[512,512]{1,0:T(8,128)(2,1)S(1)}, bf16[512,512]{1,0:T(8,128)(2,1)S(1)}, u32[]{:S(2)}, u32[]{:S(2)}) collective-permute-start(bf16[512,512]{1,0:T(8,128)(2,1)S(1)} %add_convert_fusion.1), channel_id=1, source_target_pairs={{0,2},{1,3},{2,6},{3,7},{6,4},{7,5},{4,0},{5,1},{8,10},{9,11},{10,... | collective-permute-start | bytes 1572872 | tf_op jit(solution)/shard_map/ppermute | solution.py:613
  (3 other events, 19.1 us)

commit v6 on v5

--- a/solution.py
+++ b/solution.py
@@ -11,7 +11,7 @@
 LANES = 128
 EPSILON = 1e-05
 MIB = 1024 * 1024
-STEP_ROWS = 8
+STEP_ROWS = 16
 
 TAIL = 16
 

time: 196 us -> 190 us (0.969)
  Pallas kernels: 80.7 us -> 73.3 us
    pallas_call x4, Pallas kernels: 53.6 us -> 47 us  [forward_pass(): pl.pallas_call(functools.partial(forward_kernel, rows, slots, len(straigh...]
  transfers between devices with their start and end apart: 31 -> 31, of which waited for: 17 -> 17; matrix products, arithmetic and copies ran while one was open for 3% -> 3% of each run, Pallas kernels for 34% -> 32%
where the time goes in v6:
time: 190 us
  Pallas kernels  73.3 us (39%)
  waiting for transfers between devices  69.3 us (36%)
  starting transfers between devices  33.9 us (18%)
  local copies, waits for them, and re-layouts  10 us (5%)
  other arithmetic  2.69 us (1%)
    pallas_call x4, Pallas kernels, forward_pass(): pl.pallas_call(functools.partial(forward_kernel, rows, slots, len(straigh...  47 us
    ppermute x7, waiting for transfers between devices, ring(): return lax.ppermute(array, 'dp', hops)  34.8 us
    ppermute x8, waiting for transfers between devices, partner(): lax.ppermute(array, 'side', [(i, sides - 1 - i) for i in range(sides)])  30.7 us
    pallas_call x3, Pallas kernels, block_grad_pass(): pl.pallas_call(functools.partial(block_grad_kernel, rows, slots, jobs, ha...  12.8 us
    ppermute x8, starting transfers between devices, partner(): lax.ppermute(array, 'side', [(i, sides - 1 - i) for i in range(sides)])  12.2 us
    ppermute x7, starting transfers between devices, ring(): return lax.ppermute(array, 'dp', hops)  12 us
    pallas_call x2, Pallas kernels, backward_pass(): pl.pallas_call(functools.partial(backward_kernel, rows, slots, len(across...  9.38 us
    ppermute x4, starting transfers between devices, hop(): return lax.ppermute(array, 'stage', route)  7.35 us
  transfers between devices with their start and end apart: 31, of which 17 were waited for; matrix products, arithmetic and copies ran while one was open for 3% of the time, Pallas kernels for 32%

profile of v6, /device:TPU:0, one launch (start us, length us, event | category | flops | bytes accessed | tf_op | source)
XLA Modules:
  0.0 189.6 jit_solution(16913079610680943707)
XLA Ops:
  0.9 2.1 %reshape_squeeze.4 = bf16[8,8,64,64]{3,2,1,0:T(8,128)(2,1)S(1)} reshape(bf16[1,8,8,4096]{3,2,1,0:T(8,128)(2,1)} %param.9) | data formatting | bytes 1048576 | tf_op jit(solution)/shard_map/reshape;squeeze | solution.py:570
  4.7 3.1 %collective-permute-start = (bf16[528,512]{1,0:T(8,128)(2,1)S(1)}, bf16[528,512]{1,0:T(8,128)(2,1)S(1)}, u32[]{:S(2)}, u32[]{:S(2)}) collective-permute-start(bf16[528,512]{1,0:T(8,128)(2,1)S(1)} %fusion.3.refs_0_.rest_2_.rest_3_.rest_0_), channel_id=1, source_target_pairs={{0,2},{1,3},{2,6},{3,7},{6,4},{7,5},{4,0},{5,1},{8,10},{9,11},{10,... | collective-permute-start | bytes 1622024 | tf_op jit(solution)/shard_map/ppermute | solution.py:613
  10.5 10.5 %collective-permute-done.refs_1_.rest_3_.rest_4_.rest_1_ = bf16[528,512]{1,0:T(8,128)(2,1)S(1)} collective-permute-done((bf16[528,512]{1,0:T(8,128)(2,1)S(1)}, bf16[528,512]{1,0:T(8,128)(2,1)S(1)}, u32[]{:S(2)}, u32[]{:S(2)}) %collective-permute-start) | collective-permute-done | bytes 540704 | tf_op jit(solution)/shard_map/ppermute | solution.py:613
  21.5 2.6 %collective-permute-start.3 = (bf16[528,512]{1,0:T(8,128)(2,1)S(1)}, bf16[528,512]{1,0:T(8,128)(2,1)}, u32[]{:S(2)}, u32[]{:S(2)}) collective-permute-start(bf16[528,512]{1,0:T(8,128)(2,1)S(1)} %collective-permute-done.refs_1_.rest_3_.rest_4_.rest_1_), channel_id=1, source_target_pairs={{0,2},{1,3},{2,6},{3,7},{6,4},{7,5},{4,0},{5,1},{8,10},{9,11},{10,... | collective-permute-start | bytes 1622024 | tf_op jit(solution)/shard_map/ppermute | solution.py:613
  24.1 1.5 collective-permute-start.4
  27.5 8.1 %collective-permute-done.3.refs_2_.rest_4_.rest_5_.rest_2_ = bf16[528,512]{1,0:T(8,128)(2,1)} collective-permute-done((bf16[528,512]{1,0:T(8,128)(2,1)S(1)}, bf16[528,512]{1,0:T(8,128)(2,1)}, u32[]{:S(2)}, u32[]{:S(2)}) %collective-permute-start.3) | collective-permute-done | bytes 540704 | tf_op jit(solution)/shard_map/ppermute | solution.py:613
  36.8 1.5 collective-permute-start.7
  41.3 8.4 %collective-permute-done.7.refs_3_.rest_5_.rest_6_.rest_3_ = bf16[528,512]{1,0:T(8,128)(2,1)} collective-permute-done((bf16[528,512]{1,0:T(8,128)(2,1)}, bf16[528,512]{1,0:T(8,128)(2,1)}, u32[]{:S(2)}, u32[]{:S(2)}) %collective-permute-start.7) | collective-permute-done | bytes 540704 | tf_op jit(solution)/shard_map/ppermute | solution.py:613
  50.7 1.5 collective-permute-start.11
  52.8 8.9 %collective-permute-done.11.refs_11_.rest_13_.rest_14_.rest_11_ = bf16[528,512]{1,0:T(8,128)(2,1)S(1)} collective-permute-done((bf16[528,512]{1,0:T(8,128)(2,1)}, bf16[528,512]{1,0:T(8,128)(2,1)S(1)}, u32[]{:S(2)}, u32[]{:S(2)}) %collective-permute-start.11) | collective-permute-done | bytes 540704 | tf_op jit(solution)/shard_map/ppermute | solution.py:619
  64.7 8.9 %forward_layers.3 = bf16[48,4096]{1,0:T(8,128)(2,1)S(1)} custom-call(s32[16,128]{1,0:T(8,128)S(1)} %list_columns.1.cols, s32[8]{0:T(128)S(1)} %add_multiply_fusion.bases, s32[3]{0:T(128)S(1)} %pad_add_fusion.flags, bf16[48,4096]{1,0:T(8,128)(2,1)S(1)} %constant_dynamic-slice_fusion.3.rest_0_.rest_1_, ...), custom_call_target="tpu_custom_call" | custom-call | flops 8800000000 | bytes 1048576 | tf_op jit(solution)/shard_map/forward_layers/pallas_call | solution.py:353
  73.7 3.5 %collective-permute-start.16 = (bf16[48,4096]{1,0:T(8,128)(2,1)S(1)}, bf16[48,4096]{1,0:T(8,128)(2,1)S(1)}, u32[]{:S(2)}, u32[]{:S(2)}) collective-permute-start(bf16[48,4096]{1,0:T(8,128)(2,1)S(1)} %forward_layers.3), channel_id=1, source_target_pairs={{0,16},{1,17},{2,18},{3,19},{4,20},{5,21},{6,22},{7,23},{8,24},{9,... | collective-permute-start | bytes 1179656 | tf_op jit(solution)/shard_map/ppermute | solution.py:669
  77.1 7.6 %forward_layers.2 = bf16[32,4096]{1,0:T(8,128)(2,1)S(1)} custom-call(s32[16,128]{1,0:T(8,128)S(1)} %list_columns.1.cols, s32[8]{0:T(128)S(1)} %add_multiply_fusion.bases, s32[3]{0:T(128)S(1)} %pad_add_fusion.flags, bf16[32,4096]{1,0:T(8,128)(2,1)S(1)} %copy-done.1, bf16[32,4096]{1,0:T(8,128)(2,1)S(1)} %copy-done.1, ...), custom_call_target="tpu_custom_call" | custom-call | flops 8800000000 | bytes 1048576 | tf_op jit(solution)/shard_map/forward_layers/pallas_call | solution.py:353
  86.1 16.2 %turning_layers.3 = (bf16[2,48,4096]{2,1,0:T(8,128)(2,1)S(1)}, bf16[48,4096]{1,0:T(8,128)(2,1)S(1)}, bf16[48,4096]{1,0:T(8,128)(2,1)S(1)}) custom-call(s32[16,128]{1,0:T(8,128)S(1)} %list_columns.1.cols, s32[8]{0:T(128)S(1)} %add_multiply_fusion.bases, s32[3]{0:T(128)S(1)} %pad_add_fusion.flags, ...), custom_call_target="tpu_custom_call" | custom-call | flops 15399999488 | bytes 1048576 | tf_op jit(solution)/shard_map/turning_layers/pallas_call | solution.py:353
  103.7 14.3 %turning_layers.2 = (bf16[2,32,4096]{2,1,0:T(8,128)(2,1)S(1)}, bf16[32,4096]{1,0:T(8,128)(2,1)S(1)}, bf16[32,4096]{1,0:T(8,128)(2,1)S(1)}) custom-call(s32[16,128]{1,0:T(8,128)S(1)} %list_columns.1.cols, s32[8]{0:T(128)S(1)} %add_multiply_fusion.bases, s32[3]{0:T(128)S(1)} %pad_add_fusion.flags, bf16[32,4096]{1,0:T(8,128)(2,1)S(1)} %copy-done.1, ...), custom_call_target="tpu_custom_call" | custom-call | flops 15399999488 | bytes 1048576 | tf_op jit(solution)/shard_map/turning_layers/pallas_call | solution.py:353
  119.8 4.8 %backward_layers.2.rest_0_ = bf16[2,48,4096]{2,1,0:T(8,128)(2,1)S(1)} custom-call(s32[16,128]{1,0:T(8,128)S(1)} %list_columns.1.cols, s32[8]{0:T(128)S(1)} %add_multiply_fusion.bases, s32[3]{0:T(128)S(1)} %pad_add_fusion.flags, bf16[2,48,4096]{2,1,0:T(8,128)(2,1)S(1)} %get-tuple-element.73.refs_0_.stash, bf16[48,4096]{1,0:T(8,128)(2,1)S(1)} %get-tuple-element.75.loss_grad, ...), custom_call_target="tpu_custom_call" | custom-call | flops 4400000000 | bytes 1048576 | tf_op jit(solution)/shard_map/backward_layers/pallas_call | solution.py:400
  124.8 3.1 %flip_rows.1.turned = bf16[2,32,64,160]{3,2,1,0:T(8,128)(2,1)S(1)} custom-call(s32[8]{0:T(128)S(1)} %add_multiply_fusion.bases, bf16[2,48,4096]{2,1,0:T(8,128)(2,1)S(1)} %get-tuple-element.73.refs_0_.stash, bf16[2,32,4096]{2,1,0:T(8,128)(2,1)S(1)} %get-tuple-element.77.refs_1_.stash, bf16[2,48,4096]{2,1,0:T(8,128)(2,1)S(1)} %collective-permute-done.17.refs_2_, ...), custom_call_target="tpu_custom_call" | custom-call | flops 4400000000 | bytes 1048576 | tf_op jit(solution)/shard_map/flip_rows/pallas_call | solution.py:459
  129.0 4.6 %backward_layers.3.rest_1_ = bf16[2,32,4096]{2,1,0:T(8,128)(2,1)S(1)} custom-call(s32[16,128]{1,0:T(8,128)S(1)} %list_columns.1.cols, s32[8]{0:T(128)S(1)} %add_multiply_fusion.bases, s32[3]{0:T(128)S(1)} %pad_add_fusion.flags, bf16[2,32,4096]{2,1,0:T(8,128)(2,1)S(1)} %get-tuple-element.77.refs_1_.stash, bf16[32,4096]{1,0:T(8,128)(2,1)S(1)} %get-tuple-element.78.loss_grad, ...), custom_call_target="tpu_custom_call" | custom-call | flops 4400000000 | bytes 1048576 | tf_op jit(solution)/shard_map/backward_layers/pallas_call | solution.py:400
  133.6 1.9 collective-permute-done.22.rest_3_
  135.5 2.6 %block_grads.3 = (bf16[256,512]{1,0:T(8,128)(2,1)S(1)}, bf16[256,512]{1,0:T(8,128)(2,1)S(1)}) custom-call(s32[16,128]{1,0:T(8,128)S(1)} %list_columns.1.cols, s32[3]{0:T(128)S(1)} %pad_add_fusion.flags, bf16[2,32,64,160]{3,2,1,0:T(8,128)(2,1)S(1)} %flip_rows.1.turned, bf16[2,48,4096]{2,1,0:T(8,128)(2,1)S(1)} %backward_layers.2.rest_0_, ...), custom_call_target="tpu_custom_call" | custom-call | flops 3300000000 | bytes 1048576 | tf_op jit(solution)/shard_map/block_grads/pallas_call | solution.py:512
  138.1 1.6 collective-permute-start.23
  139.7 2.1 %collective-permute-start.24 = (bf16[256,512]{1,0:T(8,128)(2,1)S(1)}, bf16[256,512]{1,0:T(8,128)(2,1)S(1)}, u32[]{:S(2)}, u32[]{:S(2)}) collective-permute-start(bf16[256,512]{1,0:T(8,128)(2,1)S(1)} %get-tuple-element.87), channel_id=1, source_target_pairs={{0,8},{8,0},{1,9},{9,1},{2,10},{10,2},{3,11},{11,3},{4,12},{12,4},... | collective-permute-start | bytes 786440 | tf_op jit(solution)/shard_map/ppermute | solution.py:619
  141.8 4.5 %block_grads.4 = (bf16[512,512]{1,0:T(8,128)(2,1)S(1)}, bf16[512,512]{1,0:T(8,128)(2,1)S(1)}) custom-call(s32[16,128]{1,0:T(8,128)S(1)} %list_columns.1.cols, s32[3]{0:T(128)S(1)} %pad_add_fusion.flags, bf16[2,32,64,160]{3,2,1,0:T(8,128)(2,1)S(1)} %flip_rows.1.turned, bf16[2,48,4096]{2,1,0:T(8,128)(2,1)S(1)} %backward_layers.2.rest_0_, ...), custom_call_target="tpu_custom_call" | custom-call | flops 4400000000 | bytes 1048576 | tf_op jit(solution)/shard_map/block_grads/pallas_call | solution.py:512
  149.6 1.8 collective-permute-start.26
  151.4 5.7 %block_grads.5 = (bf16[512,512]{1,0:T(8,128)(2,1)S(1)}, bf16[512,512]{1,0:T(8,128)(2,1)S(1)}, bf16[512,512]{1,0:T(8,128)(2,1)S(1)}, bf16[512,512]{1,0:T(8,128)(2,1)S(1)}, bf16[512,512]{1,0:T(8,128)(2,1)S(1)}) custom-call(s32[16,128]{1,0:T(8,128)S(1)} %list_columns.1.cols, s32[3]{0:T(128)S(1)} %pad_add_fusion.flags, ...), custom_call_target="tpu_custom_call" | custom-call | flops 5500000256 | bytes 1048576 | tf_op jit(solution)/shard_map/block_grads/pallas_call | solution.py:512
  157.5 4.8 %collective-permute-done.25 = bf16[512,512]{1,0:T(8,128)(2,1)S(1)} collective-permute-done((bf16[512,512]{1,0:T(8,128)(2,1)S(1)}, bf16[512,512]{1,0:T(8,128)(2,1)S(1)}, u32[]{:S(2)}, u32[]{:S(2)}) %collective-permute-start.25) | collective-permute-done | bytes 524320 | tf_op jit(solution)/shard_map/ppermute | solution.py:613
  162.3 2.3 %collective-permute-done.26 = bf16[512,512]{1,0:T(8,128)(2,1)S(1)} collective-permute-done((bf16[512,512]{1,0:T(8,128)(2,1)S(1)}, bf16[512,512]{1,0:T(8,128)(2,1)S(1)}, u32[]{:S(2)}, u32[]{:S(2)}) %collective-permute-start.26) | collective-permute-done | bytes 524320 | tf_op jit(solution)/shard_map/ppermute | solution.py:619
  165.7 2.0 %collective-permute-start.30 = (bf16[512,512]{1,0:T(8,128)(2,1)S(1)}, bf16[512,512]{1,0:T(8,128)(2,1)S(1)}, u32[]{:S(2)}, u32[]{:S(2)}) collective-permute-start(bf16[512,512]{1,0:T(8,128)(2,1)S(1)} %get-tuple-element.108), channel_id=1, source_target_pairs={{0,8},{8,0},{1,9},{9,1},{2,10},{10,2},{3,11},{11,3},{4,12},{12,4},... | collective-permute-start | bytes 1572872 | tf_op jit(solution)/shard_map/ppermute | solution.py:619
  167.7 8.0 %collective-permute-done.28 = bf16[512,512]{1,0:T(8,128)(2,1)S(1)} collective-permute-done((bf16[512,512]{1,0:T(8,128)(2,1)S(1)}, bf16[512,512]{1,0:T(8,128)(2,1)S(1)}, u32[]{:S(2)}, u32[]{:S(2)}) %collective-permute-start.28) | collective-permute-done | bytes 524320 | tf_op jit(solution)/shard_map/ppermute | solution.py:619
  177.0 8.1 %collective-permute-done.30 = bf16[512,512]{1,0:T(8,128)(2,1)S(1)} collective-permute-done((bf16[512,512]{1,0:T(8,128)(2,1)S(1)}, bf16[512,512]{1,0:T(8,128)(2,1)S(1)}, u32[]{:S(2)}, u32[]{:S(2)}) %collective-permute-start.30) | collective-permute-done | bytes 524320 | tf_op jit(solution)/shard_map/ppermute | solution.py:619
  185.0 1.9 collective-permute-done.29
  188.0 1.6 broadcast_in_dim_reshape.3
  (79 shorter events, 29.4 us)
Async XLA Ops:
  0.0 26.8 %copy-start = (bf16[2,80,4096]{2,1,0:T(8,128)(2,1)S(1)}, bf16[2,80,4096]{2,1,0:T(8,128)(2,1)}, u32[]{:S(2)}) copy-start(bf16[2,80,4096]{2,1,0:T(8,128)(2,1)} %param.7) | copy-start | bytes 3932164
  4.7 16.4 %collective-permute-start = (bf16[528,512]{1,0:T(8,128)(2,1)S(1)}, bf16[528,512]{1,0:T(8,128)(2,1)S(1)}, u32[]{:S(2)}, u32[]{:S(2)}) collective-permute-start(bf16[528,512]{1,0:T(8,128)(2,1)S(1)} %fusion.3.refs_0_.rest_2_.rest_3_.rest_0_), channel_id=1, source_target_pairs={{0,2},{1,3},{2,6},{3,7},{6,4},{7,5},{4,0},{5,1},{8,10},{9,11},{10,... | collective-permute-start | bytes 1622024 | tf_op jit(solution)/shard_map/ppermute | solution.py:613
  7.8 13.7 %collective-permute-start.1 = (bf16[528,512]{1,0:T(8,128)(2,1)S(1)}, bf16[528,512]{1,0:T(8,128)(2,1)S(1)}, u32[]{:S(2)}, u32[]{:S(2)}) collective-permute-start(bf16[528,512]{1,0:T(8,128)(2,1)S(1)} %fusion.3.refs_0_.rest_2_.rest_3_.rest_0_), channel_id=1, source_target_pairs={{0,8},{8,0},{1,9},{9,1},{2,10},{10,2},{3,11},{11,3},{4,12},{12,4},... | collective-permute-start | bytes 1622024 | tf_op jit(solution)/shard_map/ppermute | solution.py:619
  9.3 12.2 %collective-permute-start.2 = (bf16[528,512]{1,0:T(8,128)(2,1)S(1)}, bf16[528,512]{1,0:T(8,128)(2,1)S(1)}, u32[]{:S(2)}, u32[]{:S(2)}) collective-permute-start(bf16[528,512]{1,0:T(8,128)(2,1)S(1)} %fusion.3.refs_0_.rest_2_.rest_3_.rest_0_), channel_id=1, source_target_pairs={{0,1},{1,0},{2,3},{3,2},{4,5},{5,4},{6,7},{7,6},{8,9},{9,8},{10,11... | collective-permute-start | bytes 1622024 | tf_op jit(solution)/shard_map/ppermute | solution.py:616
  21.5 14.0 %collective-permute-start.3 = (bf16[528,512]{1,0:T(8,128)(2,1)S(1)}, bf16[528,512]{1,0:T(8,128)(2,1)}, u32[]{:S(2)}, u32[]{:S(2)}) collective-permute-start(bf16[528,512]{1,0:T(8,128)(2,1)S(1)} %collective-permute-done.refs_1_.rest_3_.rest_4_.rest_1_), channel_id=1, source_target_pairs={{0,2},{1,3},{2,6},{3,7},{6,4},{7,5},{4,0},{5,1},{8,10},{9,11},{10,... | collective-permute-start | bytes 1622024 | tf_op jit(solution)/shard_map/ppermute | solution.py:613
  24.1 12.7 %collective-permute-start.4 = (bf16[528,512]{1,0:T(8,128)(2,1)S(1)}, bf16[528,512]{1,0:T(8,128)(2,1)}, u32[]{:S(2)}, u32[]{:S(2)}) collective-permute-start(bf16[528,512]{1,0:T(8,128)(2,1)S(1)} %collective-permute-done.refs_1_.rest_3_.rest_4_.rest_1_), channel_id=1, source_target_pairs={{0,8},{8,0},{1,9},{9,1},{2,10},{10,2},{3,11},{11,3},{4,12},{12,4},... | collective-permute-start | bytes 1622024 | tf_op jit(solution)/shard_map/ppermute | solution.py:619
  25.6 11.2 %collective-permute-start.6 = (bf16[528,512]{1,0:T(8,128)(2,1)S(1)}, bf16[528,512]{1,0:T(8,128)(2,1)}, u32[]{:S(2)}, u32[]{:S(2)}) collective-permute-start(bf16[528,512]{1,0:T(8,128)(2,1)S(1)} %collective-permute-done.refs_1_.rest_3_.rest_4_.rest_1_), channel_id=1, source_target_pairs={{0,1},{1,0},{2,3},{3,2},{4,5},{5,4},{6,7},{7,6},{8,9},{9,8},{10,11... | collective-permute-start | bytes 1622024 | tf_op jit(solution)/shard_map/ppermute | solution.py:616
  25.6 11.2 %collective-permute-start.5 = (bf16[528,512]{1,0:T(8,128)(2,1)S(1)}, bf16[528,512]{1,0:T(8,128)(2,1)}, u32[]{:S(2)}, u32[]{:S(2)}) collective-permute-start(bf16[528,512]{1,0:T(8,128)(2,1)S(1)} %collective-permute-done.1.refs_8_.rest_10_.rest_11_.rest_8_), channel_id=1, source_target_pairs={{0,1},{1,0},{2,3},{3,2},{4,5},{5,4},{6,7},{7,6},{8,9},{9,8},{10,11... | collective-permute-start | bytes 1622024 | tf_op jit(solution)/shard_map/ppermute | solution.py:616
  36.8 12.8 %collective-permute-start.7 = (bf16[528,512]{1,0:T(8,128)(2,1)}, bf16[528,512]{1,0:T(8,128)(2,1)}, u32[]{:S(2)}, u32[]{:S(2)}) collective-permute-start(bf16[528,512]{1,0:T(8,128)(2,1)} %collective-permute-done.3.refs_2_.rest_4_.rest_5_.rest_2_), channel_id=1, source_target_pairs={{0,2},{1,3},{2,6},{3,7},{6,4},{7,5},{4,0},{5,1},{8,10},{9,11},{10,... | collective-permute-start | bytes 1622024 | tf_op jit(solution)/shard_map/ppermute | solution.py:613
  38.3 12.4 %collective-permute-start.8 = (bf16[528,512]{1,0:T(8,128)(2,1)}, bf16[528,512]{1,0:T(8,128)(2,1)}, u32[]{:S(2)}, u32[]{:S(2)}) collective-permute-start(bf16[528,512]{1,0:T(8,128)(2,1)} %collective-permute-done.3.refs_2_.rest_4_.rest_5_.rest_2_), channel_id=1, source_target_pairs={{0,8},{8,0},{1,9},{9,1},{2,10},{10,2},{3,11},{11,3},{4,12},{12,4},... | collective-permute-start | bytes 1622024 | tf_op jit(solution)/shard_map/ppermute | solution.py:619
  39.8 10.9 %collective-permute-start.10 = (bf16[528,512]{1,0:T(8,128)(2,1)}, bf16[528,512]{1,0:T(8,128)(2,1)}, u32[]{:S(2)}, u32[]{:S(2)}) collective-permute-start(bf16[528,512]{1,0:T(8,128)(2,1)} %collective-permute-done.3.refs_2_.rest_4_.rest_5_.rest_2_), channel_id=1, source_target_pairs={{0,1},{1,0},{2,3},{3,2},{4,5},{5,4},{6,7},{7,6},{8,9},{9,8},{10,11... | collective-permute-start | bytes 1622024 | tf_op jit(solution)/shard_map/ppermute | solution.py:616
  39.8 10.9 %collective-permute-start.9 = (bf16[528,512]{1,0:T(8,128)(2,1)}, bf16[528,512]{1,0:T(8,128)(2,1)}, u32[]{:S(2)}, u32[]{:S(2)}) collective-permute-start(bf16[528,512]{1,0:T(8,128)(2,1)} %collective-permute-done.4.refs_9_.rest_11_.rest_12_.rest_9_), channel_id=1, source_target_pairs={{0,1},{1,0},{2,3},{3,2},{4,5},{5,4},{6,7},{7,6},{8,9},{9,8},{10,11... | collective-permute-start | bytes 1622024 | tf_op jit(solution)/shard_map/ppermute | solution.py:616
  50.7 11.0 %collective-permute-start.11 = (bf16[528,512]{1,0:T(8,128)(2,1)}, bf16[528,512]{1,0:T(8,128)(2,1)S(1)}, u32[]{:S(2)}, u32[]{:S(2)}) collective-permute-start(bf16[528,512]{1,0:T(8,128)(2,1)} %collective-permute-done.7.refs_3_.rest_5_.rest_6_.rest_3_), channel_id=1, source_target_pairs={{0,8},{8,0},{1,9},{9,1},{2,10},{10,2},{3,11},{11,3},{4,12},{12,4},... | collective-permute-start | bytes 1622024 | tf_op jit(solution)/shard_map/ppermute | solution.py:619
  52.2 9.5 %collective-permute-start.13 = (bf16[528,512]{1,0:T(8,128)(2,1)}, bf16[528,512]{1,0:T(8,128)(2,1)S(1)}, u32[]{:S(2)}, u32[]{:S(2)}) collective-permute-start(bf16[528,512]{1,0:T(8,128)(2,1)} %collective-permute-done.7.refs_3_.rest_5_.rest_6_.rest_3_), channel_id=1, source_target_pairs={{0,1},{1,0},{2,3},{3,2},{4,5},{5,4},{6,7},{7,6},{8,9},{9,8},{10,11... | collective-permute-start | bytes 1622024 | tf_op jit(solution)/shard_map/ppermute | solution.py:616
  52.2 9.5 %collective-permute-start.12 = (bf16[528,512]{1,0:T(8,128)(2,1)}, bf16[528,512]{1,0:T(8,128)(2,1)S(1)}, u32[]{:S(2)}, u32[]{:S(2)}) collective-permute-start(bf16[528,512]{1,0:T(8,128)(2,1)} %collective-permute-done.8.refs_10_.rest_12_.rest_13_.rest_10_), channel_id=1, source_target_pairs={{0,1},{1,0},{2,3},{3,2},{4,5},{5,4},{6,7},{7,6},{8,9},{9,8},{10,11... | collective-permute-start | bytes 1622024 | tf_op jit(solution)/shard_map/ppermute | solution.py:616
  61.7 1.9 %collective-permute-start.14 = (bf16[528,512]{1,0:T(8,128)(2,1)S(1)}, bf16[528,512]{1,0:T(8,128)(2,1)S(1)}, u32[]{:S(2)}, u32[]{:S(2)}) collective-permute-start(bf16[528,512]{1,0:T(8,128)(2,1)S(1)} %collective-permute-done.11.refs_11_.rest_13_.rest_14_.rest_11_), channel_id=1, source_target_pairs={{0,1},{1,0},{2,3},{3,2},{4,5},{5,4},{6,7},{7,6},{8,9},{9,8},{10,11... | collective-permute-start | bytes 1622024 | tf_op jit(solution)/shard_map/ppermute | solution.py:616
  73.7 12.4 %collective-permute-start.16 = (bf16[48,4096]{1,0:T(8,128)(2,1)S(1)}, bf16[48,4096]{1,0:T(8,128)(2,1)S(1)}, u32[]{:S(2)}, u32[]{:S(2)}) collective-permute-start(bf16[48,4096]{1,0:T(8,128)(2,1)S(1)} %forward_layers.3), channel_id=1, source_target_pairs={{0,16},{1,17},{2,18},{3,19},{4,20},{5,21},{6,22},{7,23},{8,24},{9,... | collective-permute-start | bytes 1179656 | tf_op jit(solution)/shard_map/ppermute | solution.py:669
  84.7 18.9 %collective-permute-start.15 = (bf16[32,4096]{1,0:T(8,128)(2,1)S(1)}, bf16[32,4096]{1,0:T(8,128)(2,1)S(1)}, u32[]{:S(2)}, u32[]{:S(2)}) collective-permute-start(bf16[32,4096]{1,0:T(8,128)(2,1)S(1)} %forward_layers.2), channel_id=1, source_target_pairs={{0,16},{1,17},{2,18},{3,19},{4,20},{5,21},{6,22},{7,23},{8,24},{9,... | collective-permute-start | bytes 786440 | tf_op jit(solution)/shard_map/ppermute | solution.py:669
  102.3 17.5 %collective-permute-start.19 = (bf16[48,4096]{1,0:T(8,128)(2,1)S(1)}, bf16[48,4096]{1,0:T(8,128)(2,1)S(1)}, u32[]{:S(2)}, u32[]{:S(2)}) collective-permute-start(bf16[48,4096]{1,0:T(8,128)(2,1)S(1)} %get-tuple-element.76), channel_id=1, source_target_pairs={{16,0},{17,1},{18,2},{19,3},{20,4},{21,5},{22,6},{23,7},{24,8},{25... | collective-permute-start | bytes 1179656 | tf_op jit(solution)/shard_map/ppermute | solution.py:669
  103.6 21.2 %collective-permute-start.17 = (bf16[2,48,4096]{2,1,0:T(8,128)(2,1)S(1)}, bf16[2,48,4096]{2,1,0:T(8,128)(2,1)S(1)}, u32[]{:S(2)}, u32[]{:S(2)}) collective-permute-start(bf16[2,48,4096]{2,1,0:T(8,128)(2,1)S(1)} %get-tuple-element.73.refs_0_.stash), channel_id=1, source_target_pairs={{0,1},{1,0},{2,3},{3,2},{4,5},{5,4},{6,7},{7,6},{8,9},{9,8},{10,11... | collective-permute-start | bytes 2359304 | tf_op jit(solution)/shard_map/ppermute | solution.py:616
  118.0 6.8 %collective-permute-start.18 = (bf16[2,32,4096]{2,1,0:T(8,128)(2,1)S(1)}, bf16[2,32,4096]{2,1,0:T(8,128)(2,1)S(1)}, u32[]{:S(2)}, u32[]{:S(2)}) collective-permute-start(bf16[2,32,4096]{2,1,0:T(8,128)(2,1)S(1)} %get-tuple-element.77.refs_1_.stash), channel_id=1, source_target_pairs={{0,1},{1,0},{2,3},{3,2},{4,5},{5,4},{6,7},{7,6},{8,9},{9,8},{10,11... | collective-permute-start | bytes 1572872 | tf_op jit(solution)/shard_map/ppermute | solution.py:616
  118.5 10.4 %collective-permute-start.20 = (bf16[32,4096]{1,0:T(8,128)(2,1)S(1)}, bf16[32,4096]{1,0:T(8,128)(2,1)S(1)}, u32[]{:S(2)}, u32[]{:S(2)}) collective-permute-start(bf16[32,4096]{1,0:T(8,128)(2,1)S(1)} %get-tuple-element.79), channel_id=1, source_target_pairs={{16,0},{17,1},{18,2},{19,3},{20,4},{21,5},{22,6},{23,7},{24,8},{25... | collective-permute-start | bytes 786440 | tf_op jit(solution)/shard_map/ppermute | solution.py:669
  124.6 9.0 %collective-permute-start.21 = (bf16[2,48,4096]{2,1,0:T(8,128)(2,1)S(1)}, bf16[2,48,4096]{2,1,0:T(8,128)(2,1)S(1)}, u32[]{:S(2)}, u32[]{:S(2)}) collective-permute-start(bf16[2,48,4096]{2,1,0:T(8,128)(2,1)S(1)} %backward_layers.2.rest_0_), channel_id=1, source_target_pairs={{0,1},{1,0},{2,3},{3,2},{4,5},{5,4},{6,7},{7,6},{8,9},{9,8},{10,11... | collective-permute-start | bytes 2359304 | tf_op jit(solution)/shard_map/ppermute | solution.py:616
  133.5 2.0 %collective-permute-start.22 = (bf16[2,32,4096]{2,1,0:T(8,128)(2,1)S(1)}, bf16[2,32,4096]{2,1,0:T(8,128)(2,1)S(1)}, u32[]{:S(2)}, u32[]{:S(2)}) collective-permute-start(bf16[2,32,4096]{2,1,0:T(8,128)(2,1)S(1)} %backward_layers.3.rest_1_), channel_id=1, source_target_pairs={{0,1},{1,0},{2,3},{3,2},{4,5},{5,4},{6,7},{7,6},{8,9},{9,8},{10,11... | collective-permute-start | bytes 1572872 | tf_op jit(solution)/shard_map/ppermute | solution.py:616
  138.1 9.3 %collective-permute-start.23 = (bf16[256,512]{1,0:T(8,128)(2,1)S(1)}, bf16[256,512]{1,0:T(8,128)(2,1)S(1)}, u32[]{:S(2)}, u32[]{:S(2)}) collective-permute-start(bf16[256,512]{1,0:T(8,128)(2,1)S(1)} %get-tuple-element.86), channel_id=1, source_target_pairs={{0,2},{1,3},{2,6},{3,7},{6,4},{7,5},{4,0},{5,1},{8,10},{9,11},{10,... | collective-permute-start | bytes 786440 | tf_op jit(solution)/shard_map/ppermute | solution.py:613
  139.7 8.4 %collective-permute-start.24 = (bf16[256,512]{1,0:T(8,128)(2,1)S(1)}, bf16[256,512]{1,0:T(8,128)(2,1)S(1)}, u32[]{:S(2)}, u32[]{:S(2)}) collective-permute-start(bf16[256,512]{1,0:T(8,128)(2,1)S(1)} %get-tuple-element.87), channel_id=1, source_target_pairs={{0,8},{8,0},{1,9},{9,1},{2,10},{10,2},{3,11},{11,3},{4,12},{12,4},... | collective-permute-start | bytes 786440 | tf_op jit(solution)/shard_map/ppermute | solution.py:619
  148.2 14.1 %collective-permute-start.25 = (bf16[512,512]{1,0:T(8,128)(2,1)S(1)}, bf16[512,512]{1,0:T(8,128)(2,1)S(1)}, u32[]{:S(2)}, u32[]{:S(2)}) collective-permute-start(bf16[512,512]{1,0:T(8,128)(2,1)S(1)} %add_convert_fusion.4), channel_id=1, source_target_pairs={{0,2},{1,3},{2,6},{3,7},{6,4},{7,5},{4,0},{5,1},{8,10},{9,11},{10,... | collective-permute-start | bytes 1572872 | tf_op jit(solution)/shard_map/ppermute | solution.py:613
  149.6 14.9 %collective-permute-start.26 = (bf16[512,512]{1,0:T(8,128)(2,1)S(1)}, bf16[512,512]{1,0:T(8,128)(2,1)S(1)}, u32[]{:S(2)}, u32[]{:S(2)}) collective-permute-start(bf16[512,512]{1,0:T(8,128)(2,1)S(1)} %add_convert_fusion.3), channel_id=1, source_target_pairs={{0,8},{8,0},{1,9},{9,1},{2,10},{10,2},{3,11},{11,3},{4,12},{12,4},... | collective-permute-start | bytes 1572872 | tf_op jit(solution)/shard_map/ppermute | solution.py:619
  157.1 18.7 %collective-permute-start.28 = (bf16[512,512]{1,0:T(8,128)(2,1)S(1)}, bf16[512,512]{1,0:T(8,128)(2,1)S(1)}, u32[]{:S(2)}, u32[]{:S(2)}) collective-permute-start(bf16[512,512]{1,0:T(8,128)(2,1)S(1)} %get-tuple-element.105), channel_id=1, source_target_pairs={{0,8},{8,0},{1,9},{9,1},{2,10},{10,2},{3,11},{11,3},{4,12},{12,4},... | collective-permute-start | bytes 1572872 | tf_op jit(solution)/shard_map/ppermute | solution.py:619
  164.8 11.0 %collective-permute-start.27 = (bf16[512,512]{1,0:T(8,128)(2,1)S(1)}, bf16[512,512]{1,0:T(8,128)(2,1)S(1)}, u32[]{:S(2)}, u32[]{:S(2)}) collective-permute-start(bf16[512,512]{1,0:T(8,128)(2,1)S(1)} %add_convert_fusion.2), channel_id=1, source_target_pairs={{0,2},{1,3},{2,6},{3,7},{6,4},{7,5},{4,0},{5,1},{8,10},{9,11},{10,... | collective-permute-start | bytes 1572872 | tf_op jit(solution)/shard_map/ppermute | solution.py:613
  165.7 19.3 %collective-permute-start.30 = (bf16[512,512]{1,0:T(8,128)(2,1)S(1)}, bf16[512,512]{1,0:T(8,128)(2,1)S(1)}, u32[]{:S(2)}, u32[]{:S(2)}) collective-permute-start(bf16[512,512]{1,0:T(8,128)(2,1)S(1)} %get-tuple-element.108), channel_id=1, source_target_pairs={{0,8},{8,0},{1,9},{9,1},{2,10},{10,2},{3,11},{11,3},{4,12},{12,4},... | collective-permute-start | bytes 1572872 | tf_op jit(solution)/shard_map/ppermute | solution.py:619
  176.0 10.9 %collective-permute-start.29 = (bf16[512,512]{1,0:T(8,128)(2,1)S(1)}, bf16[512,512]{1,0:T(8,128)(2,1)S(1)}, u32[]{:S(2)}, u32[]{:S(2)}) collective-permute-start(bf16[512,512]{1,0:T(8,128)(2,1)S(1)} %add_convert_fusion.1), channel_id=1, source_target_pairs={{0,2},{1,3},{2,6},{3,7},{6,4},{7,5},{4,0},{5,1},{8,10},{9,11},{10,... | collective-permute-start | bytes 1572872 | tf_op jit(solution)/shard_map/ppermute | solution.py:613
  (3 other events, 18.1 us)
